TPU v7x, 128 devices: a whole 4x4x4 slice. The times are simulated.
128 devices in a mesh: gx: 4 (over z_lo, core), gy: 32 (over y, x, z_hi).
Axes of the slice: x: 4, y: 4, z: 4 (z_hi: 2, z_lo: 2; z = z_hi * 2 + z_lo), core: 2. Of those that a mesh axis runs over, the one named last changes fastest.
Arguments:
- particles: float32 [4, 2097152], P(None, ('gx', 'gy'))
- counts: int32 [32768], P(('gx', 'gy')), may hold values from 1 to 64, as said below
- leaf_top: int32 [32768], P(('gx', 'gy')), may hold values from 0 to 4095, never falling along the last dimension, each value on 1 to 32 neighbouring positions
- near_list: int32 [32768, 27], P(('gx', 'gy')), may hold values from 0 to 32767, as said below
- leaf_list: int32 [32768, 16], P(('gx', 'gy')), may hold values from 0 to 32767, as said below
- leaf_class: int32 [32768, 16], P(('gx', 'gy')), may hold values from 0 to 315
- top_list: int32 [4096, 64], replicated, may hold values from 0 to 4095
- top_class: int32 [4096, 64], replicated, may hold values from 0 to 315
- m2l_ops: float32 [316, 81, 81], replicated
- m2m_ops: float32 [8, 81, 81], replicated
Outputs:
- potential: float32 [2097152], P(('gx', 'gy'))
Inputs may be any that keep to these rules, and one draw needn't show every extreme that they name: `counts`: leaves whose global index is a multiple of 16 hold 64 particles. `near_list`: column 0 is the leaf itself; every entry lies within 32 leaves of the leaf's own index. `leaf_list`: every entry lies within 32 leaves of the leaf's own index.
All inputs are finite; a program needn't handle non-finite values.
Results may differ from a plain program's by a relative error of at most 0.0003.
Values sent between devices are 32-bit elements; how exact they have to be, the bound alone decides.
No kernel may reach another device: no remote copies, remote signals or barrier semaphores. Data moves between devices by JAX's collectives and lax.ppermute only.
A program may use at most 256 MiB of HBM per device.

v0:
```python
import jax
import jax.numpy as jnp
from jax import lax
from jax.sharding import PartitionSpec as P

ORDER = 8
PART = 64
HALO = 32
OWN_MAX = 32


SOFTENING = 0.01
HIGH = lax.Precision.HIGHEST


def with_halo(shard, sides, width):
    for axis, dim in sides:
        count, length = (lax.axis_size(axis), shard.shape[dim])
        up = [(i, (i + 1) % count) for i in range(count - 1)]
        down = [(j, i) for i, j in up]
        last = lax.slice_in_dim(shard, length - width, length, axis=dim)
        leading = lax.slice_in_dim(shard, 0, width, axis=dim)
        before = lax.ppermute(last, axis, up)
        after = lax.ppermute(leading, axis, down)
        shard = jnp.concatenate([before, shard, after], axis=dim)
    return shard


def harmonics(offset):
    coord_x, coord_y, coord_z = (offset[0], offset[1], offset[2])
    radius_sq = coord_x * coord_x + coord_y * coord_y + coord_z * coord_z
    zeros_like = jnp.zeros_like(coord_x)
    solid_terms = {(0, 0): (jnp.ones_like(coord_x), zeros_like)}
    for order_m in range(1, ORDER + 1):
        real_part, imag_part = solid_terms[order_m - 1, order_m - 1]
        solid_terms[order_m, order_m] = (
            (coord_x * real_part - coord_y * imag_part) / (2.0 * order_m),
            (coord_x * imag_part + coord_y * real_part) / (2.0 * order_m),
        )
    for order_m in range(ORDER):
        real_part, imag_part = solid_terms[order_m, order_m]
        solid_terms[order_m + 1, order_m] = (coord_z * real_part, coord_z * imag_part)
    for order_m in range(ORDER - 1):
        for degree in range(order_m + 2, ORDER + 1):
            factor_one = (2.0 * degree - 1.0) / ((degree - order_m) * (degree + order_m))
            factor_two = 1.0 / ((degree - order_m) * (degree + order_m))
            upper_one = solid_terms[degree - 1, order_m]
            upper_two = solid_terms[degree - 2, order_m]
            solid_terms[degree, order_m] = (
                factor_one * coord_z * upper_one[0] - factor_two * radius_sq * upper_two[0],
                factor_one * coord_z * upper_one[1] - factor_two * radius_sq * upper_two[1],
            )
    stacked = []
    for degree in range(ORDER + 1):
        stacked.append(solid_terms[degree, 0][0])
        for order_m in range(1, degree + 1):
            stacked.append(solid_terms[degree, order_m][0])
            stacked.append(solid_terms[degree, order_m][1])
    return jnp.stack(stacked, 0)


def expand(points, leaf_count):
    grid = points.reshape(4, leaf_count, PART)
    center = jnp.mean(grid[:3], axis=2, keepdims=True)
    solid = harmonics(grid[:3] - center)
    return (solid, jnp.sum(solid * grid[3][None], axis=2))


def translate(sources, classes, m2l_ops):
    onehot = (classes[..., None] == jnp.arange(m2l_ops.shape[0], dtype=jnp.int32)).astype(
        jnp.float32
    )
    grouped = jnp.einsum("jbk,bkc->cjb", sources, onehot, precision=HIGH)
    return jnp.einsum("cij,cjb->ib", m2l_ops, grouped, precision=HIGH)


def lift(m2m_ops, field):
    width = field.shape[1]
    shaped = field.reshape(field.shape[0], width // 8, 8)
    return jnp.einsum("aij,jba->iba", m2m_ops, shaped, precision=HIGH).reshape(-1, width)


def lower(m2m_ops, field):
    width = field.shape[1]
    shaped = field.reshape(field.shape[0], width // 8, 8)
    return jnp.einsum("aji,jba->iba", m2m_ops, shaped, precision=HIGH).reshape(-1, width)


def near_sum(own_grid, index, source_grid):
    leaf_count = index.shape[0]
    block_size = min(32, leaf_count)
    block_count = leaf_count // block_size
    targets = own_grid[:3].reshape(3, block_count, block_size, PART).transpose(1, 0, 2, 3)
    chosen = index.reshape(block_count, block_size, -1)

    def one_block(item):
        points, picked = item
        flat = source_grid[:, picked].reshape(4, block_size, -1)
        dist_sq = (points[0][:, :, None] - flat[0][:, None, :]) ** 2
        dist_sq = dist_sq + (points[1][:, :, None] - flat[1][:, None, :]) ** 2
        dist_sq = dist_sq + (points[2][:, :, None] - flat[2][:, None, :]) ** 2
        return jnp.sum(flat[3][:, None, :] * lax.rsqrt(dist_sq + SOFTENING), axis=2)

    return lax.map(one_block, (targets, chosen)).reshape(leaf_count, PART)


def slot_of(boxes, devices):
    return boxes % devices * OWN_MAX + boxes // devices


def slot_sums(lifted, leaf_slot, devices):
    return jax.ops.segment_sum(lifted.T, leaf_slot, num_segments=devices * OWN_MAX).T


def own_translate(all_moments, devices, my_index, top_list, top_class, m2l_ops):
    ranks = jnp.arange(OWN_MAX, dtype=jnp.int32)
    box_rows = my_index + ranks * devices
    lists = top_list[box_rows]
    classes = top_class[box_rows]
    return translate(all_moments[:, slot_of(lists, devices)], classes, m2l_ops)


def body(
    particles,
    counts,
    leaf_top,
    near_list,
    leaf_list,
    leaf_class,
    top_list,
    top_class,
    m2l_ops,
    m2m_ops,
):
    leaves = counts.shape[0]
    devices = lax.axis_size(("gx", "gy"))
    my_index = lax.axis_index(("gx", "gy"))
    first_leaf = my_index * leaves
    slot_mask = (jnp.arange(PART, dtype=jnp.int32)[None, :] < counts[:, None]).astype(jnp.float32)
    masked = jnp.concatenate([particles[:3], particles[3:] * slot_mask.reshape(1, -1)], 0)
    window = with_halo(masked, ((("gx", "gy"), 1),), HALO * PART)
    solid, own_moments = expand(masked, leaves)
    wide_moments = with_halo(own_moments, ((("gx", "gy"), 1),), HALO)
    leaf_local = translate(wide_moments[:, leaf_list - first_leaf + HALO], leaf_class, m2l_ops)
    lifted = lift(m2m_ops, own_moments)
    leaf_slot = slot_of(leaf_top, devices)
    owned_moments = lax.psum_scatter(
        slot_sums(lifted, leaf_slot, devices), ("gx", "gy"), scatter_dimension=1, tiled=True
    )
    all_moments = lax.all_gather(owned_moments, ("gx", "gy"), axis=1, tiled=True)
    owned_local = own_translate(all_moments, devices, my_index, top_list, top_class, m2l_ops)
    top_local = lax.all_gather(owned_local, ("gx", "gy"), axis=1, tiled=True)[:, leaf_slot]
    local = leaf_local + lower(m2m_ops, top_local)
    far_field = jnp.sum(solid * local[:, :, None], axis=0)
    window_grid = window.reshape(4, -1, PART)
    near_field = near_sum(
        masked.reshape(4, leaves, PART), near_list - first_leaf + HALO, window_grid
    )
    return ((near_field + far_field) * slot_mask).reshape(-1)


def solution(mesh):
    return jax.shard_map(
        body,
        mesh=mesh,
        in_specs=(
            P(None, ("gx", "gy")),
            P(("gx", "gy")),
            P(("gx", "gy")),
            P(("gx", "gy"), None),
            P(("gx", "gy"), None),
            P(("gx", "gy"), None),
            P(),
            P(),
            P(),
            P(),
        ),
        out_specs=P(("gx", "gy")),
        check_vma=False,
    )
```

profile of v0, /device:TPU:1, one launch (start us, length us, event | category | flops | bytes accessed | tf_op | source)
XLA Modules:
  0.0 1423.0 jit_solution(6423758431562434984)
XLA Ops:
  9.3 1.9 fusion.45
  68.1 3.4 multiply_reduce_fusion.2
  72.3 3.7 scatter_custom_fusion
  76.8 6.3 collective-permute-start
  83.1 7.2 collective-permute-start.1
  90.9 1.9 collective-permute-start.2
  92.8 9.4 collective-permute-start.3
  102.4 1.8 copy.145
  106.8 1.8 copy.140
  110.6 10.8 gather_fusion.1
  121.4 617.9 %reduce-scatter.2.cloned.1.call-done = f32[81,32]{0,1:T(8,128)} async-done(((f32[81,4096]{0,1:T(8,128)}), f32[81,32]{0,1:T(8,128)}) %reduce-scatter.2.cloned.1.call-update) | async-done | bytes 10384 | tf_op jit(solution)/shard_map/reduce_scatter | solution.py:147
  739.9 22.5 %convolution_bitcast_fusion = f32[316,81,256]{0,1,2:T(8,128)} fusion(f32[81,256,16]{0,2,1:T(8,128)S(1)} %bitcast.94, s32[256,16]{1,0:T(8,128)S(1)} %copy.131), kind=kOutput, calls=%fused_computation.21 | convolution fusion | flops 1259388928 | bytes 27553792 | tf_op jit(solution)/shard_map/jbk,bkc->cjb/dot_general | solution.py:73
  764.1 273.0 %all-gather.3.cloned.1.call-done = f32[81,4096]{0,1:T(8,128)} async-done(((f32[81,32]{0,1:T(8,128)}), f32[81,4096]{0,1:T(8,128)}) %all-gather.3.cloned.1.call-update) | async-done | bytes 1327120 | tf_op jit(solution)/shard_map/all_gather | solution.py:150
  1037.1 7.0 gather_fusion.4
  1044.1 2.7 fusion.8
  1046.8 13.4 fusion.20
  1060.2 172.1 %while.10 = (s32[]{:T(128)}, f32[8,32,64]{2,1,0:T(8,128)}, s32[8,32,27]{2,1,0:T(8,128)}, f32[4,320,64]{2,0,1:T(4,128)S(1)}, f32[8,3,32,64]{3,2,0,1:T(8,128)S(1)}, /*index=5*/s32[]{:T(128)}) while((s32[]{:T(128)}, f32[8,32,64]{2,1,0:T(8,128)}, s32[8,32,27]{2,1,0:T(8,128)}, f32[4,320,64]{2,0,1:T(4,128)S(1)}, f32[8,3,32,64]{3,2,0,1:T(8,128)S(1)}, ...), condition=%wide.region_2.3_spmd, body=%wide.region_0.2_spmd.sunk | while | flops 38929952 | bytes 7946641 | solution.py:104
  1061.4 3.7 gather_fusion
  1065.0 5.9 slice_reduce_fusion.5
  1071.0 1.2 sub.1705
  1074.7 6.6 multiply_reduce_fusion.4
  1082.8 3.7 gather_fusion
  1086.5 5.9 slice_reduce_fusion.5
  1096.2 6.6 multiply_reduce_fusion.4
  1104.3 3.7 gather_fusion
  1108.0 5.9 slice_reduce_fusion.5
  1113.9 1.2 sub.1705
  1117.7 6.6 multiply_reduce_fusion.4
  1125.8 3.7 gather_fusion
  1129.5 5.9 slice_reduce_fusion.5
  1135.4 1.2 sub.1705
  1139.2 6.6 multiply_reduce_fusion.4
  1147.3 3.7 gather_fusion
  1151.0 5.9 slice_reduce_fusion.5
  1160.7 6.6 multiply_reduce_fusion.4
  1168.8 3.7 gather_fusion
  1172.5 5.9 slice_reduce_fusion.5
  1182.2 6.6 multiply_reduce_fusion.4
  1190.3 3.7 gather_fusion
  1194.0 5.9 slice_reduce_fusion.5
  1203.7 6.6 multiply_reduce_fusion.4
  1211.8 3.7 gather_fusion
  1215.4 5.9 slice_reduce_fusion.5
  1225.1 6.6 multiply_reduce_fusion.4
  1233.4 128.1 %all-gather.5.cloned.1.call-done = f32[81,4096]{0,1:T(8,128)} async-done(((f32[81,32]{0,1:T(8,128)}), f32[81,4096]{0,1:T(8,128)}) %all-gather.5.cloned.1.call-update) | async-done | bytes 1327120 | tf_op jit(solution)/shard_map/all_gather | solution.py:152
  1361.5 2.3 gather_fusion.5
  1364.5 47.8 %fusion.15 = f32[81,256]{1,0:T(8,128)S(1)} fusion(f32[81,256]{1,0:T(8,128)S(1)} %copy.151, f32[316,81,81]{0,2,1:T(8,128)} %param.20, f32[316,81,256]{0,1,2:T(8,128)} %convolution_bitcast_fusion), kind=kOutput, calls=%fused_computation.37 | convolution fusion | flops 6369124352 | bytes 34669296 | tf_op jit(solution)/shard_map/cij,cjb->ib/dot_general | solution.py:74
  1412.3 3.1 multiply_reduce_fusion.1
  (262 shorter events, 109.1 us)
Async XLA Ops:
  6.5 65.1 %copy-start = (f32[8,81,81]{2,0,1:T(8,128)S(1)}, f32[8,81,81]{2,0,1:T(8,128)}, u32[]{:S(2)}) copy-start(f32[8,81,81]{2,0,1:T(8,128)} %param.21) | copy-start | bytes 629860
  6.5 732.8 %reduce-scatter.2.cloned.1.call-start = ((), (), s32[]{:S(2)}) async-start(), calls=%async_computation.1 | async-start | bytes 2113536 | tf_op jit(solution)/shard_map/reduce_scatter | solution.py:147
  11.1 65.0 %copy-start.4 = (f32[1,16384]{1,0:T(1,128)}, f32[1,16384]{1,0:T(1,128)S(1)}, u32[]{:S(2)}) copy-start(f32[1,16384]{1,0:T(1,128)S(1)} %get-tuple-element.80) | copy-start | bytes 196612
  68.1 8.0 copy-start.1
  68.1 34.1 %copy-start.10 = (s32[256,16]{0,1:T(8,128)S(1)}, s32[256,16]{0,1:T(8,128)}, u32[]{:S(2)}) copy-start(s32[256,16]{0,1:T(8,128)} %param.16) | copy-start | bytes 49156
  71.5 33.5 %copy-start.7 = (s32[256,27]{0,1:T(8,128)S(1)}, s32[256,27]{0,1:T(8,128)}, u32[]{:S(2)}) copy-start(s32[256,27]{0,1:T(8,128)} %param.15) | copy-start | bytes 82948
  71.5 35.2 %copy-start.8 = (s32[256,16]{0,1:T(8,128)S(1)}, s32[256,16]{0,1:T(8,128)}, u32[]{:S(2)}) copy-start(s32[256,16]{0,1:T(8,128)} %param.17) | copy-start | bytes 49156
  76.1 961.0 %all-gather.3.cloned.1.call-start = ((), (), s32[]{:S(2)}) async-start(), calls=%async_computation.2 | async-start | bytes 2113536 | tf_op jit(solution)/shard_map/all_gather | solution.py:150
  76.8 685.6 %collective-permute-start = (f32[4,2048]{1,0:T(4,128)}, f32[4,2048]{1,0:T(4,128)}, u32[]{:S(2)}, u32[]{:S(2)}) collective-permute-start(f32[4,2048]{1,0:T(4,128)} %get-tuple-element.86), channel_id=1, source_target_pairs={{0,1},{1,2},{2,3},{3,4},{4,5},{5,6},{6,7},{7,8},{8,9},{9,10},{10,1... | collective-permute-start | bytes 98312 | tf_op jit(solution)/shard_map/ppermute | solution.py:23
  83.1 679.3 %collective-permute-start.1 = (f32[4,2048]{1,0:T(4,128)}, f32[4,2048]{1,0:T(4,128)}, u32[]{:S(2)}, u32[]{:S(2)}) collective-permute-start(f32[4,2048]{1,0:T(4,128)} %get-tuple-element.87), channel_id=1, source_target_pairs={{1,0},{2,1},{3,2},{4,3},{5,4},{6,5},{7,6},{8,7},{9,8},{10,9},{11,1... | collective-permute-start | bytes 98312 | tf_op jit(solution)/shard_map/ppermute | solution.py:24
  90.9 18.4 %collective-permute-start.2 = (f32[81,32]{0,1:T(8,128)}, f32[81,32]{0,1:T(8,128)S(1)}, u32[]{:S(2)}, u32[]{:S(2)}) collective-permute-start(f32[81,32]{0,1:T(8,128)} %get-tuple-element.88), channel_id=1, source_target_pairs={{0,1},{1,2},{2,3},{3,4},{4,5},{5,6},{6,7},{7,8},{8,9},{9,10},{10,1... | collective-permute-start | bytes 31112 | tf_op jit(solution)/shard_map/ppermute | solution.py:23
  92.8 17.0 %collective-permute-start.3 = (f32[81,32]{0,1:T(8,128)}, f32[81,32]{0,1:T(8,128)}, u32[]{:S(2)}, u32[]{:S(2)}) collective-permute-start(f32[81,32]{0,1:T(8,128)} %get-tuple-element.89), channel_id=1, source_target_pairs={{1,0},{2,1},{3,2},{4,3},{5,4},{6,5},{7,6},{8,7},{9,8},{10,9},{11,1... | collective-permute-start | bytes 31112 | tf_op jit(solution)/shard_map/ppermute | solution.py:24
  109.2 0.6 copy-start.9
  739.3 622.2 %all-gather.5.cloned.1.call-start = ((), (), s32[]{:S(2)}) async-start(), calls=%async_computation.3 | async-start | bytes 2113536 | tf_op jit(solution)/shard_map/all_gather | solution.py:152
  739.9 22.5 %copy-start.5 = (f32[1,16384]{1,0:T(1,128)S(1)}, f32[1,16384]{1,0:T(1,128)}, u32[]{:S(2)}) copy-start(f32[1,16384]{1,0:T(1,128)} %copy-done.4) | copy-start | bytes 196612
  1060.4 0.9 copy-start.2
  1071.0 11.0 copy-start.3
  1082.0 0.9 copy-start.2
  1092.4 11.0 copy-start.3
  1103.4 0.9 copy-start.2
  1113.9 11.0 copy-start.3
  1124.9 0.9 copy-start.2
  1135.4 11.0 copy-start.3
  1146.4 0.9 copy-start.2
  1156.9 11.0 copy-start.3
  1167.9 0.9 copy-start.2
  1178.4 11.0 copy-start.3
  1189.4 0.9 copy-start.2
  1199.9 11.0 copy-start.3
  1210.9 0.9 copy-start.2
  1221.4 11.0 copy-start.3
  1412.3 3.3 copy-start.6
Sparse Core Ops, SparseCore 0:
  76.2 663.1 reduce-scatter.1
  741.1 295.9 all-gather.2
  1060.4 301.0 all-gather.4
where the time goes:
time: 1430 us; the launch traced here: 1420 us
  waiting for transfers between devices  1020 us (71%)
  local copies, waits for them, and re-layouts  146 us (10%)
  other arithmetic  130 us (9%)
  matrix products  87.6 us (6%)
  starting transfers between devices  25.3 us (2%)
    reduce_scatter x1, waiting for transfers between devices, body(): lax.psum_scatter(slot_sums(lifted, leaf_slot, devices), ('gx', 'gy'), sca...  618 us
    all_gather x1, waiting for transfers between devices, body(): lax.all_gather(owned_moments, ('gx', 'gy'), axis=1, tiled=True)  273 us
    all_gather x1, waiting for transfers between devices, body(): lax.all_gather(owned_local, ('gx', 'gy'), axis=1, tiled=True)[:, leaf_slot]  128 us
    dot_general x2, matrix products, translate(): return jnp.einsum('cij,cjb->ib', m2l_ops, grouped, precision=HIGH)  61.2 us
    unnamed x78, other arithmetic  53.8 us
    reduce_sum x8, other arithmetic, one_block(): return jnp.sum(flat[3][:, None, :] * lax.rsqrt(dist_sq + SOFTENING), axis=2)  53 us
    slice x8, local copies, waits for them, and re-layouts, one_block(): return jnp.sum(flat[3][:, None, :] * lax.rsqrt(dist_sq + SOFTENING), axis=2)  47.4 us
    gather x8, local copies, waits for them, and re-layouts, one_block(): flat = source_grid[:, picked].reshape(4, block_size, -1)  29.3 us
  transfers between devices with their start and end apart: 7, of which 3 were waited for; matrix products, arithmetic and copies ran while one was open for 15% of the time, Pallas kernels for 0%

commit v1 on v0

v1 whole, which is shorter than its diff:
```python
import functools

import jax
import jax.numpy as jnp
from jax import lax
from jax.experimental import pallas as pl
from jax.experimental.pallas import tpu as pltpu
from jax.sharding import Mesh, PartitionSpec as P

ORDER = 8
COEF = 81
PART = 64
LEAVES = 256
PAIRS = 128
HALO = 32
HPAIRS = 16
WPAIRS = PAIRS + 2 * HPAIRS
NEAR = 27
LLIST = 16
TLIST = 64
TOPBOX = 4096
CLASS_BITS = 9
SOFTENING = 0.01
SEND = 56
REACH_SQ = 16.0
FEAT = 32
NEAR_PARTS = 2

HIGH = lax.Precision.HIGHEST
MIB = 1 << 20
AXES = ("zlo", "core", "y", "x", "zhi")

NN = (((1,), (0,)), ((), ()))
NT = (((1,), (1,)), ((), ()))


def dot_f32(left, right, dims=NN):
    return lax.dot_general(left, right, dims, precision=HIGH, preferred_element_type=jnp.float32)


def lanes(shape):
    return lax.broadcasted_iota(jnp.int32, shape, len(shape) - 1)


def rows_of(shape):
    return lax.broadcasted_iota(jnp.int32, shape, len(shape) - 2)


def harmonics(coord_x, coord_y, coord_z):
    radius_sq = coord_x * coord_x + coord_y * coord_y + coord_z * coord_z
    terms = {(0, 0): (None, None)}
    for m in range(1, ORDER + 1):
        if m == 1:
            terms[1, 1] = (coord_x * 0.5, coord_y * 0.5)
            continue
        re, im = terms[m - 1, m - 1]
        scale = 1.0 / (2.0 * m)
        terms[m, m] = (
            (coord_x * re - coord_y * im) * scale,
            (coord_x * im + coord_y * re) * scale,
        )
    for m in range(ORDER):
        re, im = terms[m, m]
        terms[m + 1, m] = (coord_z, None) if m == 0 else (coord_z * re, coord_z * im)
    for m in range(ORDER - 1):
        for n in range(m + 2, ORDER + 1):
            one = (2.0 * n - 1.0) / ((n - m) * (n + m))
            two = 1.0 / ((n - m) * (n + m))
            z_one = coord_z * one
            r_two = radius_sq * two
            upper, lower = terms[n - 1, m], terms[n - 2, m]
            re = z_one * upper[0] - (r_two if lower[0] is None else r_two * lower[0])
            im = None if m == 0 else z_one * upper[1] - r_two * lower[1]
            terms[n, m] = (re, im)
    listed = []
    for n in range(ORDER + 1):
        listed.append(terms[n, 0][0])
        for m in range(1, n + 1):
            listed.extend(terms[n, m])
    return listed


def centred(block):
    turned = block.T
    halves = []
    for p in range(2):
        half = turned[p * PART : (p + 1) * PART]
        halves.append(half - jnp.sum(half, axis=0, keepdims=True) * (1.0 / PART))
    return jnp.concatenate(halves, axis=0)


def expand_into(d_ref, q_ref, acc_ref, out_ref):
    out_ref[...] = jnp.zeros_like(out_ref)
    for p in range(2):
        acc_ref[...] = jnp.zeros_like(acc_ref)

        def step(s, carry):
            at = pl.ds(pl.multiple_of(p * PART + s * 16, 16), 16)
            charge = q_ref[at, :]
            listed = harmonics(d_ref[0, at, :], d_ref[1, at, :], d_ref[2, at, :])
            for c, term in enumerate(listed):
                value = charge if term is None else charge * term
                acc_ref[c] += value[:8] + value[8:]
            return carry

        lax.fori_loop(0, PART // 16, step, 0)
        sums = jnp.sum(acc_ref[...], axis=1)
        full = jnp.concatenate([sums, jnp.zeros((128 - COEF, 128), jnp.float32)], axis=0)
        out_ref[p] = full.T


def slot_mask_rows(count_ref):
    lane = lanes((PAIRS, 128))
    held = jnp.where(lane < PART, count_ref[:, 0:1], count_ref[:, 1:2])
    return jnp.where((lane & (PART - 1)) < held, 1.0, 0.0)


def first_kernel(
    pts_ref, count_ref, top_ref, ends_ref, m2m_ref,
    own_ref, low_ref, high_ref, dist_ref, moment_ref, part_ref, q_ref, acc_ref,
):
    charge = pts_ref[3] * slot_mask_rows(count_ref)
    for c in range(3):
        own_ref[c] = pts_ref[c]
        dist_ref[c] = centred(pts_ref[c])
    own_ref[3] = charge
    for c in range(4):
        low_ref[c] = own_ref[c, :HPAIRS]
        high_ref[c] = own_ref[c, PAIRS - HPAIRS :]
    q_ref[...] = charge.T
    expand_into(dist_ref, q_ref, acc_ref, moment_ref)
    first, last = ends_ref[0], ends_ref[1]
    row = rows_of((PAIRS, COEF))
    total = jnp.zeros((LEAVES, COEF), jnp.float32)
    for p in range(2):
        moment = moment_ref[p][:, :COEF]
        lifted = jnp.zeros((PAIRS, COEF), jnp.float32)
        for u in range(4):
            lifted += dot_f32(jnp.where((row & 3) == u, moment, 0.0), m2m_ref[2 * u + p], NT)
        held = jnp.where(rows_of((LEAVES, PAIRS)) == top_ref[p : p + 1, :] - first, 1.0, 0.0)
        total += dot_f32(held, lifted)
    wide = jnp.concatenate([total, jnp.zeros((LEAVES, 128 - COEF), jnp.float32)], axis=1)
    lane = lanes((LEAVES, 128))
    wide = jnp.where(lane == 127, first.astype(jnp.float32), wide)
    wide = jnp.where(lane == 126, last.astype(jnp.float32), wide)
    part_ref[...] = wide


def split3(value):
    high = value.astype(jnp.bfloat16).astype(jnp.float32)
    rest = value - high
    middle = rest.astype(jnp.bfloat16).astype(jnp.float32)
    low = (rest - middle).astype(jnp.bfloat16).astype(jnp.float32)
    return high, middle, low


def near_kernel(
    part, near_ref, win_ref, out_ref, src_ref, tgt_ref, table_ref, charge_ref,
):
    targets = PAIRS // NEAR_PARTS
    width = targets + 2 * HPAIRS
    base = part * targets
    at = pl.ds(base, width)
    points = [win_ref[c, at, :] for c in range(3)]
    moved = []
    for c in range(3):
        least = jnp.min(points[c], keepdims=True)
        most = jnp.max(points[c], keepdims=True)
        moved.append(points[c] - 0.5 * (least + most))
    norm = moved[0] * moved[0] + moved[1] * moved[1] + moved[2] * moved[2]
    close = jnp.max(norm) <= REACH_SQ

    @pl.when(close)
    def _():
        own = slice(HPAIRS, HPAIRS + targets)
        src_ref[...] = jnp.zeros_like(src_ref)
        tgt_ref[...] = jnp.zeros_like(tgt_ref)
        for c in range(3):
            h, m, l = split3(moved[c])
            for i, feature in enumerate((h, h, m, m, h, l)):
                src_ref[pl.ds(6 * c + i, width, stride=FEAT), :] = feature
            th, tm, tl = [-2.0 * piece[own] for piece in (h, m, l)]
            for i, feature in enumerate((th, tm, th, tm, tl, th)):
                tgt_ref[pl.ds(6 * c + i, targets, stride=FEAT), :] = feature
        ones = jnp.ones((width, 128), jnp.float32)
        for i, feature in enumerate(split3(norm + SOFTENING)):
            src_ref[pl.ds(18 + i, width, stride=FEAT), :] = feature
            tgt_ref[pl.ds(18 + i, targets, stride=FEAT), :] = ones[own]
        for i, feature in enumerate(split3(norm[own])):
            src_ref[pl.ds(21 + i, width, stride=FEAT), :] = ones
            tgt_ref[pl.ds(21 + i, targets, stride=FEAT), :] = feature
        for i, feature in enumerate(split3(win_ref[3, at, :])):
            src_ref[pl.ds(24 + i, width, stride=FEAT), :] = feature

        row = rows_of((128, 256))
        lane = lanes((128, 256))
        spread = []
        for p in range(4):
            local = row - FEAT * p
            same = (lane < 128) & (local < 24) & (local == (lane & (FEAT - 1)))
            charge = (lane >= 128) & (local >= 24) & (local < 27)
            spread.append(jnp.where(same | charge, 1.0, 0.0).astype(jnp.bfloat16))

        def build(g, carry):
            turned = src_ref[pl.ds(pl.multiple_of(g * 128, 128), 128), :].T.astype(jnp.bfloat16)
            for p in range(4):
                both = lax.dot_general(turned, spread[p], NN, preferred_element_type=jnp.float32)
                to = pl.ds(pl.multiple_of((g * 4 + p) * 128, 128), 128)
                table_ref[to, :] = both[:, :128].astype(jnp.bfloat16)
                charge_ref[to, :] = both[:, 128:]
            return carry

        lax.fori_loop(0, width // 4, build, 0)

        lane_w = lanes((FEAT, 128))
        lane_b = lanes((PART, 128))
        low_half = lane_b < PART
        start = 2 * base

        def group(g, carry):
            two = tgt_ref[pl.ds(pl.multiple_of(g * 2 * FEAT, 2 * FEAT), 2 * FEAT), :]
            zero = jnp.zeros((FEAT, 128), jnp.float32)
            left, right = [], []
            for half in range(2):
                one = two[half * FEAT : (half + 1) * FEAT]
                low = jnp.where(lane_w < PART, one, 0.0)
                high = jnp.where(lane_w < PART, 0.0, one)
                left += [low, high] if half == 0 else [zero, zero]
                right += [zero, zero] if half == 0 else [low, high]
            weights = jnp.concatenate(
                [jnp.concatenate(left, axis=0), jnp.concatenate(right, axis=0)], axis=1
            ).astype(jnp.bfloat16)

            def one_entry(k, total):
                spots = []
                for v in range(4):
                    leaf = near_ref[(start + g * 4 + v) * NEAR + k] - start
                    spots.append(pl.ds(pl.multiple_of(leaf * PART, PART), PART))
                rows = [table_ref[spot, :] for spot in spots]
                mixed = jnp.where(
                    lane_b < 2 * FEAT,
                    jnp.where(lane_b < FEAT, rows[0], rows[1]),
                    jnp.where(lane_b < 3 * FEAT, rows[2], rows[3]),
                )
                dist = lax.dot_general(mixed, weights, NN, preferred_element_type=jnp.float32)
                inverse = lax.rsqrt(dist)
                sums = []
                for half in range(2):
                    charge = jnp.where(
                        low_half, charge_ref[spots[2 * half], :], charge_ref[spots[2 * half + 1], :]
                    )
                    term = charge * inverse[:, half * 128 : (half + 1) * 128]
                    sums.append(jnp.sum(term.reshape(8, 8, 128), axis=0))
                return total[0] + sums[0], total[1] + sums[1]

            def entries(k, total):
                for i in range(3):
                    total = one_entry(k * 3 + i, total)
                return total

            zeros = jnp.zeros((8, 128), jnp.float32)
            total = lax.fori_loop(0, NEAR // 3, entries, (zeros, zeros))
            both = jnp.concatenate([jnp.sum(t, axis=0, keepdims=True) for t in total], axis=0)
            out_ref[pl.ds(g * 2, 2), :] = both
            return carry

        lax.fori_loop(0, targets // 2, group, 0)

    @pl.when(jnp.logical_not(close))
    def _():
        lane = lanes((PART, 128))

        def pair(r, carry):
            columns = [
                jnp.broadcast_to(win_ref[c, pl.ds(base + HPAIRS + r, 1), :], (128, 128)).T
                for c in range(3)
            ]
            results = []
            for p in range(2):
                mine = [column[p * PART : (p + 1) * PART] for column in columns]

                def entry(k, total):
                    leaf = near_ref[(2 * (base + r) + p) * NEAR + k]
                    at = pl.ds(leaf // 2, 1)
                    gap = SOFTENING
                    for c in range(3):
                        diff = mine[c] - win_ref[c, at, :]
                        gap = gap + diff * diff
                    half = jnp.where((lane // PART) == leaf % 2, 1.0, 0.0)
                    return total + half * (win_ref[3, at, :] * lax.rsqrt(gap))

                total = lax.fori_loop(0, NEAR, entry, jnp.zeros((PART, 128), jnp.float32))
                results.append(jnp.sum(total, axis=1, keepdims=True))
            wide = jnp.broadcast_to(jnp.concatenate(results, axis=0), (128, 128)).T
            out_ref[pl.ds(r, 1), :] = wide[:1]
            return carry

        lax.fori_loop(0, targets, pair, 0)


def gather_products(codes, m2l_ref, rows_ref):
    total = None
    for code in codes:
        at = pl.ds(code >> CLASS_BITS, 1)
        term = m2l_ref[code & ((1 << CLASS_BITS) - 1)] * rows_ref[at, :][:, :COEF]
        total = term if total is None else total + term
    return total


def leaf_kernel(
    code_ref, m2l_ref, moment_ref, low_ref, high_ref, out_ref,
    rows_ref, d_ref, q_ref, acc_ref, halo_ref,
):
    fill = jnp.zeros((PAIRS - 2 * HPAIRS, 128), jnp.float32)
    for c in range(3):
        d_ref[c] = centred(jnp.concatenate([low_ref[c], high_ref[c], fill], axis=0))
    q_ref[...] = jnp.concatenate([low_ref[3], high_ref[3], fill], axis=0).T
    expand_into(d_ref, q_ref, acc_ref, halo_ref)
    for p in range(2):
        at = p * WPAIRS
        rows_ref[at : at + HPAIRS] = halo_ref[p, :HPAIRS]
        rows_ref[at + HPAIRS : at + HPAIRS + PAIRS] = moment_ref[p]
        rows_ref[at + HPAIRS + PAIRS : at + WPAIRS] = halo_ref[p, HPAIRS : 2 * HPAIRS]
    lane = lanes((COEF, 128))
    for p in range(2):

        def leaf(r, wide):
            spot = (2 * r + p) * LLIST
            total = gather_products([code_ref[spot + k] for k in range(LLIST)], m2l_ref, rows_ref)
            return jnp.where(lane == r, jnp.sum(total, axis=1, keepdims=True), wide)

        out_ref[p] = lax.fori_loop(0, PAIRS, leaf, jnp.zeros((COEF, 128), jnp.float32))


def finish(
    cap, info_ref, code_ref, table_ref, m2l_ref, m2m_ref, top_ref, local_ref, dist_ref,
    near_refs, count_ref, out_ref, field_ref, pot_ref,
):
    first, shift, boxes = info_ref[0], info_ref[1], info_ref[2]
    lane = lanes((COEF, 128))
    spread = [jnp.zeros((PAIRS, COEF), jnp.float32) for _ in range(2)]
    for block in range((cap + 127) // 128):

        def box(b, wide):
            row = block * 128 + b + shift

            def some(i, total):
                codes = [code_ref[row, i * 16 + k] for k in range(16)]
                return total + gather_products(codes, m2l_ref, table_ref)

            total = lax.fori_loop(0, TLIST // 16, some, jnp.zeros((COEF, COEF), jnp.float32))
            return jnp.where(lane == b, jnp.sum(total, axis=1, keepdims=True), wide)

        count = jnp.clip(boxes - block * 128, 0, 128)
        wide = lax.fori_loop(0, count, box, jnp.zeros((COEF, 128), jnp.float32))
        for p in range(2):
            held = lanes((PAIRS, 128)) + block * 128 == top_ref[p * PAIRS : (p + 1) * PAIRS] - first
            spread[p] += dot_f32(jnp.where(held, 1.0, 0.0), wide, NT)
    row = rows_of((PAIRS, COEF))
    for p in range(2):
        lowered = jnp.zeros((PAIRS, COEF), jnp.float32)
        for u in range(4):
            lowered += dot_f32(jnp.where((row & 3) == u, spread[p], 0.0), m2m_ref[2 * u + p])
        full = jnp.concatenate([lowered, jnp.zeros((PAIRS, 128 - COEF), jnp.float32)], axis=1)
        field_ref[p] = full.T[:COEF] + local_ref[p]
    for p in range(2):

        def step(s, carry):
            at = pl.ds(pl.multiple_of(p * PART + s * 16, 16), 16)
            listed = harmonics(dist_ref[0, at, :], dist_ref[1, at, :], dist_ref[2, at, :])
            total = None
            for c, term in enumerate(listed):
                weight = field_ref[p, pl.ds(c, 1), :]
                value = jnp.broadcast_to(weight, (16, 128)) if term is None else term * weight
                total = value if total is None else total + value
            pot_ref[at, :] = total
            return carry

        lax.fori_loop(0, PART // 16, step, 0)
    near = jnp.concatenate([ref[...] for ref in near_refs], axis=0)
    out_ref[...] = (near + pot_ref[...].T) * slot_mask_rows(count_ref)


def last_kernel(
    info_ref, code_ref, mine_ref, other_ref, m2l_ref, m2m_ref, top_ref, local_ref, dist_ref,
    near_a_ref, near_b_ref, count_ref, out_ref, over_ref, table_ref, field_ref, pot_ref,
):
    core, my_y, my_x, my_z = info_ref[3], info_ref[4], info_ref[5], info_ref[6]
    table_ref[0:1, :] = jnp.zeros((1, 128), jnp.float32)
    over_ref[0] = 0

    def assemble(ref, zlo):
        def step(i, carry):
            y, x, zhi = i // 8, (i // 2) % 4, i % 2
            block = ((my_z - (zlo * 2 + zhi)) & 3) * 16 + ((my_x - x) & 3) * 4 + ((my_y - y) & 3)
            at = pl.multiple_of(block * SEND, 8)
            ends = ref[pl.ds(at, 1), :]
            begin = ends[0, 127].astype(jnp.int32)
            end = ends[0, 126].astype(jnp.int32)
            over_ref[0] = jnp.maximum(over_ref[0], end - begin + 1)
            so_far = table_ref[pl.ds(begin, 1), :]
            table_ref[pl.ds(begin, SEND), :] = ref[pl.ds(at, SEND), :]
            table_ref[pl.ds(begin, 1), :] = ends + so_far
            return carry

        lax.fori_loop(0, 32, step, 0)

    for zlo in range(2):
        for side in range(2):

            @pl.when(core == side)
            def _():
                assemble(mine_ref, zlo)

            @pl.when(core != side)
            def _():
                assemble(other_ref, zlo)

    @pl.when(over_ref[0] < SEND)
    def _():
        finish(
            64, info_ref, code_ref, table_ref, m2l_ref, m2m_ref, top_ref, local_ref, dist_ref,
            (near_a_ref, near_b_ref), count_ref, out_ref, field_ref, pot_ref,
        )


def spare_kernel(
    info_ref, code_ref, table_ref, m2l_ref, m2m_ref, top_ref, local_ref, dist_ref,
    near_a_ref, near_b_ref, count_ref, out_ref, field_ref, pot_ref,
):
    finish(
        LEAVES, info_ref, code_ref, table_ref, m2l_ref, m2m_ref, top_ref, local_ref, dist_ref,
        (near_a_ref, near_b_ref), count_ref, out_ref, field_ref, pot_ref,
    )


SMEM = pl.BlockSpec(memory_space=pltpu.SMEM)
VMEM = pl.BlockSpec(memory_space=pltpu.VMEM)
F32 = jnp.float32


def shape(*dims):
    return jax.ShapeDtypeStruct(dims, F32)


def call_first(pts, count, top2, ends, m2m_ops):
    return pl.pallas_call(
        first_kernel,
        out_shape=(
            shape(4, PAIRS, 128), shape(4, HPAIRS, 128), shape(4, HPAIRS, 128),
            shape(3, PAIRS, 128), shape(2, PAIRS, 128), shape(LEAVES, 128),
        ),
        in_specs=[VMEM, VMEM, VMEM, SMEM, VMEM],
        out_specs=(VMEM,) * 6,
        scratch_shapes=[pltpu.VMEM((128, 128), F32), pltpu.VMEM((COEF, 8, 128), F32)],
        compiler_params=pltpu.CompilerParams(vmem_limit_bytes=16 * MIB),
        cost_estimate=pl.CostEstimate(flops=10**9, bytes_accessed=10**7, transcendentals=0),
        name="expand_own",
    )(pts, count, top2, ends, m2m_ops)


def call_near(part, near, window):
    targets = PAIRS // NEAR_PARTS
    width = targets + 2 * HPAIRS
    return pl.pallas_call(
        functools.partial(near_kernel, part),
        out_shape=shape(targets, 128),
        in_specs=[SMEM, VMEM],
        out_specs=VMEM,
        scratch_shapes=[
            pltpu.VMEM((width * FEAT, 128), F32),
            pltpu.VMEM((targets * FEAT, 128), F32),
            pltpu.VMEM((width * 128, 128), jnp.bfloat16),
            pltpu.VMEM((width * 128, 128), F32),
        ],
        compiler_params=pltpu.CompilerParams(vmem_limit_bytes=24 * MIB),
        cost_estimate=pl.CostEstimate(
            flops=10 * targets * 2 * 64 * NEAR * 64, bytes_accessed=3 * 10**7,
            transcendentals=targets * 2 * 64 * NEAR * 64,
        ),
        name="near",
    )(near, window)


def call_leaf(code, m2l_ops, moments, low, high):
    return pl.pallas_call(
        leaf_kernel,
        out_shape=shape(2, COEF, 128),
        in_specs=[SMEM] + [VMEM] * 4,
        out_specs=VMEM,
        scratch_shapes=[
            pltpu.VMEM((2 * WPAIRS, 128), F32),
            pltpu.VMEM((3, 128, 128), F32),
            pltpu.VMEM((128, 128), F32),
            pltpu.VMEM((COEF, 8, 128), F32),
            pltpu.VMEM((2, 128, 128), F32),
        ],
        compiler_params=pltpu.CompilerParams(vmem_limit_bytes=24 * MIB),
        cost_estimate=pl.CostEstimate(
            flops=2 * LEAVES * LLIST * COEF * COEF * 8, bytes_accessed=3 * 10**7, transcendentals=0
        ),
        name="leaf_translate",
    )(code, m2l_ops, moments, low, high)


def call_last(info, code, mine, other, *rest):
    return pl.pallas_call(
        last_kernel,
        out_shape=(shape(PAIRS, 128), jax.ShapeDtypeStruct((1,), jnp.int32)),
        in_specs=[SMEM, SMEM] + [VMEM] * 10,
        out_specs=(VMEM, SMEM),
        scratch_shapes=[
            pltpu.VMEM((TOPBOX + SEND, 128), F32),
            pltpu.VMEM((2, COEF, 128), F32),
            pltpu.VMEM((128, 128), F32),
        ],
        compiler_params=pltpu.CompilerParams(vmem_limit_bytes=32 * MIB),
        name="finish",
    )(info, code, mine, other, *rest)


def call_spare(info, code, table, *rest):
    return pl.pallas_call(
        spare_kernel,
        out_shape=shape(PAIRS, 128),
        in_specs=[SMEM, SMEM] + [VMEM] * 9,
        out_specs=VMEM,
        scratch_shapes=[pltpu.VMEM((2, COEF, 128), F32), pltpu.VMEM((128, 128), F32)],
        compiler_params=pltpu.CompilerParams(vmem_limit_bytes=32 * MIB),
        name="finish_spare",
    )(info, code, table, *rest)


def spread_over(block, axis, count):
    pieces = [block]
    for s in range(1, count):
        pieces.append(lax.ppermute(block, axis, [(i, (i + s) % count) for i in range(count)]))
    return jnp.concatenate(pieces, axis=0)


def prepare(particles, counts, leaf_top, near_list, leaf_list, leaf_class, my_index):
    pts = particles.reshape(4, PAIRS, 128)
    count = counts.reshape(PAIRS, 2)
    top2 = leaf_top.reshape(PAIRS, 2).T
    ends = jnp.stack([leaf_top[0], leaf_top[LEAVES - 1]])
    before = my_index * LEAVES - HALO
    near = (near_list - before).reshape(-1)
    spot = leaf_list - before
    code = ((((spot & 1) * WPAIRS + (spot >> 1)) << CLASS_BITS) | leaf_class).reshape(-1)
    return pts, count, top2, ends, near, code


def top_codes(top_list, top_class, first, cap):
    start = jnp.minimum(first, TOPBOX - cap)
    rows = lax.dynamic_slice_in_dim(top_list, start, cap, axis=0)
    classes = lax.dynamic_slice_in_dim(top_class, start, cap, axis=0)
    return (rows << CLASS_BITS) | classes, first - start


def body(
    particles, counts, leaf_top, near_list, leaf_list, leaf_class, top_list, top_class,
    m2l_ops, m2m_ops,
):
    my_index = lax.axis_index(AXES)
    pts, count, top2, ends, near, code = prepare(
        particles, counts, leaf_top, near_list, leaf_list, leaf_class, my_index
    )
    own, low, high, dist, moments, partial = call_first(pts, count, top2, ends, m2m_ops)
    devices = lax.axis_size(AXES)
    up = [(i, i + 1) for i in range(devices - 1)]
    down = [(j, i) for i, j in up]
    before = lax.ppermute(high, AXES, up)
    after = lax.ppermute(low, AXES, down)
    window = jnp.concatenate([before, own, after], axis=1)

    gathered = spread_over(partial[:SEND], "y", 4)
    near_a = call_near(0, near, window)
    gathered, window = lax.optimization_barrier((gathered, window))
    gathered = spread_over(gathered, "x", 4)
    near_b = call_near(1, near, window)
    gathered = spread_over(gathered, ("zlo", "zhi"), 4)
    local = call_leaf(code, m2l_ops, moments, before, after)
    other = lax.ppermute(gathered, "core", [(0, 1), (1, 0)])

    first, boxes = ends[0], ends[1] - ends[0] + 1
    place = [
        lax.axis_index("core"), lax.axis_index("y"), lax.axis_index("x"),
        lax.axis_index(("zlo", "zhi")),
    ]

    def info_of(shift):
        return jnp.stack([first, shift, boxes, *place]).astype(jnp.int32)

    top_column = top2.reshape(LEAVES, 1)
    rest = (m2l_ops, m2m_ops, top_column, local, dist, near_a, near_b, count)
    top_code, shift = top_codes(top_list, top_class, first, 64)
    result, over = call_last(info_of(shift), top_code, gathered, other, *rest)

    def spare():
        table = lax.dynamic_update_slice(
            jnp.zeros((TOPBOX + LEAVES, 128), F32), partial, (first, 0)
        )
        table = lax.psum(table, AXES)
        wide_code, wide_shift = top_codes(top_list, top_class, first, LEAVES)
        return call_spare(info_of(wide_shift), wide_code, table, *rest)

    result = lax.cond(over[0] >= SEND, spare, lambda: result)
    return result.reshape(-1)


def solution(mesh):
    fine = Mesh(mesh.devices.reshape(2, 2, 4, 4, 2), AXES)
    return jax.shard_map(
        body,
        mesh=fine,
        in_specs=(
            P(None, AXES), P(AXES), P(AXES), P(AXES, None), P(AXES, None), P(AXES, None),
            P(), P(), P(), P(),
        ),
        out_specs=P(AXES),
        check_vma=False,
    )
```

time: 1430 us -> 300 us (0.21)
  waiting for transfers between devices: 1020 us -> 19.4 us
  Pallas kernels: 0 us -> 202 us
  other arithmetic: 130 us -> 1.31 us
  local copies, waits for them, and re-layouts: 146 us -> 28.9 us
  matrix products: 87.6 us -> 0 us
    reduce_scatter x1 -> x0, waiting for transfers between devices: 618 us -> none  [body(): lax.psum_scatter(slot_sums(lifted, leaf_slot, devices), ('gx', 'gy'), sca...]
    all_gather x2 -> x0, waiting for transfers between devices: 401 us -> none  [the longest x1 273 us: body(): lax.all_gather(owned_moments, ('gx', 'gy'), axis=1, tiled=True)]
    pallas_call x0 -> x5, Pallas kernels: none -> 202 us  [the longest x2 124 us: call_near(): pl.pallas_call(functools.partial(near_kernel, part), out_shape=shape(targ...]
    dot_general x6 -> x0, matrix products: 87.6 us -> none  [the longest x2 61.2 us: translate(): return jnp.einsum('cij,cjb->ib', m2l_ops, grouped, precision=HIGH)]
    reduce_sum x11 -> x0, other arithmetic: 59.6 us -> none  [the longest x8 53 us: one_block(): return jnp.sum(flat[3][:, None, :] * lax.rsqrt(dist_sq + SOFTENING), axis=2)]
    unnamed x78 -> x1, other arithmetic: 53.8 us -> 0.01 us
    gather x13 -> x0, local copies, waits for them, and re-layouts: 50.6 us -> none  [the longest x8 29.3 us: one_block(): flat = source_grid[:, picked].reshape(4, block_size, -1)]
    slice x11 -> x2, local copies, waits for them, and re-layouts: 49.3 us -> 1.34 us  [the longest x1 1.34 us: prepare(): ends = jnp.stack([leaf_top[0], leaf_top[LEAVES - 1]])]
  transfers between devices with their start and end apart: 7 -> 12, of which waited for: 3 -> 5; matrix products, arithmetic and copies ran while one was open for 15% -> 7% of each run, Pallas kernels for 0% -> 56%
where the time goes in v1:
time: 300 us; the launch traced here: 297 us
  Pallas kernels  202 us (67%)
  local copies, waits for them, and re-layouts  28.9 us (10%)
  starting transfers between devices  28.4 us (9%)
  waiting for transfers between devices  19.4 us (6%)
  between operations  16.6 us (6%)
    pallas_call x2, Pallas kernels, call_near(): pl.pallas_call(functools.partial(near_kernel, part), out_shape=shape(targ...  124 us
    pallas_call x1, Pallas kernels, call_leaf(): pl.pallas_call(leaf_kernel, out_shape=shape(2, COEF, 128), in_specs=[SMEM...  41.7 us
    pallas_call x1, Pallas kernels, call_last(): pl.pallas_call(last_kernel, out_shape=(shape(PAIRS, 128), jax.ShapeDtypeS...  33.8 us
    unnamed x34, local copies, waits for them, and re-layouts  22.1 us
    ppermute x9, waiting for transfers between devices, spread_over(): lax.ppermute(block, axis, [(i, (i + s) % count) for i in range(count)])  18.5 us
    ppermute x9, starting transfers between devices, spread_over(): lax.ppermute(block, axis, [(i, (i + s) % count) for i in range(count)])  14.8 us
  transfers between devices with their start and end apart: 12, of which 5 were waited for; matrix products, arithmetic and copies ran while one was open for 7% of the time, Pallas kernels for 56%

profile of v1, /device:TPU:1, one launch (start us, length us, event | category | flops | bytes accessed | tf_op | source)
XLA Modules:
  0.0 297.1 jit_solution(3545082948648242600)
XLA Ops:
  6.5 1.3 fusion
  7.9 0.8 reshape.31
  8.7 0.8 reshape.30.count_ref
  9.5 1.0 copy.26.m2m_ref
  10.6 0.1 copy.25
  10.6 1.0 copy.42
  11.6 1.3 pad_add_fusion.ends_ref
  12.9 3.1 %expand_own.1 = (f32[4,128,128]{2,1,0:T(8,128)S(1)}, f32[4,16,128]{2,1,0:T(8,128)S(1)}, f32[4,16,128]{2,1,0:T(8,128)S(1)}, f32[3,128,128]{2,1,0:T(8,128)S(1)}, f...) custom-call(f32[4,128,128]{2,1,0:T(8,128)S(1)} %bitcast.26, s32[128,2]{1,0:T(8,128)S(1)} %reshape.30.count_ref, ...), custom_call_target="tpu_custom_call" | custom-call | flops 1000000000 | bytes 10000000 | tf_op jit(solution)/shard_map/expand_own/pallas_call | solution.py:447
  16.0 2.2 collective-permute-start
  18.2 2.6 collective-permute-start.1
  20.8 1.1 collective-permute-start.2
  21.9 5.5 %collective-permute-start.3 = (f32[4,16,128]{2,1,0:T(8,128)S(1)}, f32[4,16,128]{2,1,0:T(8,128)S(1)}, u32[]{:S(2)}, u32[]{:S(2)}) collective-permute-start(f32[4,16,128]{2,1,0:T(8,128)S(1)} %get-tuple-element.76), channel_id=1, source_target_pairs={{0,1},{1,2},{2,3},{3,4},{4,5},{5,6},{6,7},{7,8},{8,9},{9,10},{10,1... | collective-permute-start | bytes 98312 | tf_op jit(solution)/shard_map/ppermute | solution.py:572
  27.4 5.8 %collective-permute-start.4 = (f32[4,16,128]{2,1,0:T(8,128)S(1)}, f32[4,16,128]{2,1,0:T(8,128)S(1)}, u32[]{:S(2)}, u32[]{:S(2)}) collective-permute-start(f32[4,16,128]{2,1,0:T(8,128)S(1)} %get-tuple-element.78), channel_id=1, source_target_pairs={{1,0},{2,1},{3,2},{4,3},{5,4},{6,5},{7,6},{8,7},{9,8},{10,9},{11,1... | collective-permute-start | bytes 98312 | tf_op jit(solution)/shard_map/ppermute | solution.py:573
  33.3 0.9 collective-permute-done.4.high_ref
  34.2 0.6 collective-permute-start.5
  34.7 2.5 collective-permute-start.6
  37.2 1.2 collective-permute-start.7
  38.3 0.7 constant_dynamic-update-slice_fusion.6
  39.0 0.7 constant_dynamic-update-slice_fusion.5
  39.7 0.9 collective-permute-done.6
  40.6 0.6 constant_dynamic-update-slice_fusion.4
  41.3 0.7 constant_dynamic-update-slice_fusion.3
  41.9 3.1 %collective-permute-start.8 = (f32[896,128]{1,0:T(8,128)S(1)}, f32[896,128]{1,0:T(8,128)S(1)}, u32[]{:S(2)}, u32[]{:S(2)}) collective-permute-start(f32[896,128]{1,0:T(8,128)S(1)} %get-tuple-element.122), channel_id=1, source_target_pairs={{0,1},{1,64},{64,65},{65,0},{2,3},{3,66},{66,67},{67,2},{4,5},{5,6... | collective-permute-start | bytes 1376264 | tf_op jit(solution)/shard_map/ppermute | solution.py:537
  45.0 1.0 collective-permute-start.9
  46.0 0.6 collective-permute-start.10
  46.6 5.5 %collective-permute-done.8 = f32[896,128]{1,0:T(8,128)S(1)} collective-permute-done((f32[896,128]{1,0:T(8,128)S(1)}, f32[896,128]{1,0:T(8,128)S(1)}, u32[]{:S(2)}, u32[]{:S(2)}) %collective-permute-start.8) | collective-permute-done | bytes 458784 | tf_op jit(solution)/shard_map/ppermute | solution.py:537
  52.1 0.8 constant_dynamic-update-slice_fusion.9
  52.9 9.4 %collective-permute-done.9 = f32[896,128]{1,0:T(8,128)S(1)} collective-permute-done((f32[896,128]{1,0:T(8,128)S(1)}, f32[896,128]{1,0:T(8,128)S(1)}, u32[]{:S(2)}, u32[]{:S(2)}) %collective-permute-start.9) | collective-permute-done | bytes 458784 | tf_op jit(solution)/shard_map/ppermute | solution.py:537
  62.3 0.8 constant_dynamic-update-slice_fusion.8
  63.1 2.7 collective-permute-done.10
  65.8 0.8 constant_dynamic-update-slice_fusion.7.mine_ref
  66.6 2.4 collective-permute-start.11
  69.0 0.1 copy.29
  69.1 0.2 reshape.34.near_ref
  69.4 0.1 copy.27
  69.5 0.1 reshape.33.code_ref
  69.6 14.6 %copy.30.m2l_ref = f32[316,81,81]{2,1,0:T(8,128)} copy(f32[316,81,81]{0,2,1:T(8,128)} %param.20) | data formatting | bytes 16586208 | tf_op args[8]
  85.4 1.0 constant_dynamic-slice_fusion
  86.3 0.1 copy.38
  86.4 0.1 copy.39
  87.7 0.1 copy.32.top_ref
  87.9 0.6 stack.51.info_ref
  88.5 61.8 %near.2.near_a_ref = f32[64,128]{1,0:T(8,128)S(1)} custom-call(s32[6912]{0:T(1024)S(1)} %reshape.34.near_ref, f32[4,160,128]{2,1,0:T(8,128)S(1)} %constant_dynamic-update-slice_fusion.win_ref), custom_call_target="tpu_custom_call" | custom-call | flops 141557760 | bytes 30000000 | tf_op jit(solution)/shard_map/near/pallas_call | solution.py:465
  150.3 1.0 copy-done.3
  151.3 62.2 %near.3.near_b_ref = f32[64,128]{1,0:T(8,128)S(1)} custom-call(s32[6912]{0:T(1024)S(1)} %reshape.34.near_ref, f32[4,160,128]{2,1,0:T(8,128)S(1)} %copy-done.3), custom_call_target="tpu_custom_call" | custom-call | flops 141557760 | bytes 30000000 | tf_op jit(solution)/shard_map/near/pallas_call | solution.py:465
  213.5 41.7 %leaf_translate.1.local_ref = f32[2,81,128]{2,1,0:T(8,128)S(1)} custom-call(s32[4096]{0:T(1024)S(1)} %reshape.33.code_ref, f32[316,81,81]{2,1,0:T(8,128)S(1)} %bitcast.25, f32[2,128,128]{2,1,0:T(8,128)S(1)} %get-tuple-element.80.moment_ref, f32[4,16,128]{2,1,0:T(8,128)S(1)} %collective-permute-done.3.low_ref, f32[4,16,128]{2,1,0:T(8,128)S(1)} %collective-permute-done.4.high_ref), custom_call_target="tpu_custom_call" | custom-call | flops 429981696 | bytes 30000000 | tf_op jit(solution)/shard_map/leaf_translate/pallas_call | solution.py:486
  255.2 33.8 %finish.1 = (f32[128,128]{1,0:T(8,128)S(1)}, s32[1]{0:T(128)}) custom-call(s32[7]{0:T(128)S(1)} %stack.51.info_ref, s32[64,64]{1,0:T(8,128)S(1)} %shift-left_or_fusion.code_ref, f32[3584,128]{1,0:T(8,128)} %constant_dynamic-update-slice_fusion.7.mine_ref, f32[3584,128]{1,0:T(8,128)} %collective-permute-done.11.other_ref, f32[316,81,81]{2,1,0:T(8,128)S(1)} %bitcast.25, ...), custom_call_target="tpu_custom_call" | custom-call | tf_op jit(solution)/shard_map/finish/pallas_call | solution.py:507
  289.6 0.6 copy-done.9
  (37 shorter events, 0.1 us)
Async XLA Ops:
  16.0 17.2 %collective-permute-start = (f32[56,128]{1,0:T(8,128)S(1)}, f32[56,128]{1,0:T(8,128)S(1)}, u32[]{:S(2)}, u32[]{:S(2)}) collective-permute-start(f32[56,128]{1,0:T(8,128)S(1)} %slice.11), channel_id=1, source_target_pairs={{0,8},{8,16},{16,24},{24,0},{1,9},{9,17},{17,25},{25,1},{2,10},{10... | collective-permute-start | bytes 86024 | tf_op jit(solution)/shard_map/ppermute | solution.py:537
  18.2 15.0 %collective-permute-start.1 = (f32[56,128]{1,0:T(8,128)S(1)}, f32[56,128]{1,0:T(8,128)S(1)}, u32[]{:S(2)}, u32[]{:S(2)}) collective-permute-start(f32[56,128]{1,0:T(8,128)S(1)} %slice.11), channel_id=1, source_target_pairs={{0,16},{8,24},{16,0},{24,8},{1,17},{9,25},{17,1},{25,9},{2,18},{10... | collective-permute-start | bytes 86024 | tf_op jit(solution)/shard_map/ppermute | solution.py:537
  20.8 12.4 %collective-permute-start.2 = (f32[56,128]{1,0:T(8,128)S(1)}, f32[56,128]{1,0:T(8,128)S(1)}, u32[]{:S(2)}, u32[]{:S(2)}) collective-permute-start(f32[56,128]{1,0:T(8,128)S(1)} %slice.11), channel_id=1, source_target_pairs={{0,24},{8,0},{16,8},{24,16},{1,25},{9,1},{17,9},{25,17},{2,26},{10... | collective-permute-start | bytes 86024 | tf_op jit(solution)/shard_map/ppermute | solution.py:537
  21.9 11.3 %collective-permute-start.3 = (f32[4,16,128]{2,1,0:T(8,128)S(1)}, f32[4,16,128]{2,1,0:T(8,128)S(1)}, u32[]{:S(2)}, u32[]{:S(2)}) collective-permute-start(f32[4,16,128]{2,1,0:T(8,128)S(1)} %get-tuple-element.76), channel_id=1, source_target_pairs={{0,1},{1,2},{2,3},{3,4},{4,5},{5,6},{6,7},{7,8},{8,9},{9,10},{10,1... | collective-permute-start | bytes 98312 | tf_op jit(solution)/shard_map/ppermute | solution.py:572
  27.4 6.8 %collective-permute-start.4 = (f32[4,16,128]{2,1,0:T(8,128)S(1)}, f32[4,16,128]{2,1,0:T(8,128)S(1)}, u32[]{:S(2)}, u32[]{:S(2)}) collective-permute-start(f32[4,16,128]{2,1,0:T(8,128)S(1)} %get-tuple-element.78), channel_id=1, source_target_pairs={{1,0},{2,1},{3,2},{4,3},{5,4},{6,5},{7,6},{8,7},{9,8},{10,9},{11,1... | collective-permute-start | bytes 98312 | tf_op jit(solution)/shard_map/ppermute | solution.py:573
  34.2 54.4 %copy-start.2 = (f32[4,160,128]{2,1,0:T(8,128)}, f32[4,160,128]{2,1,0:T(8,128)S(1)}, u32[]{:S(2)}) copy-start(f32[4,160,128]{2,1,0:T(8,128)S(1)} %constant_dynamic-update-slice_fusion.win_ref) | copy-start | bytes 983044
  34.2 4.9 %collective-permute-start.5 = (f32[224,128]{1,0:T(8,128)S(1)}, f32[224,128]{1,0:T(8,128)S(1)}, u32[]{:S(2)}, u32[]{:S(2)}) collective-permute-start(f32[224,128]{1,0:T(8,128)S(1)} %pad_maximum_fusion), channel_id=1, source_target_pairs={{0,2},{2,4},{4,6},{6,0},{1,3},{3,5},{5,7},{7,1},{8,10},{10,12},{12... | collective-permute-start | bytes 344072 | tf_op jit(solution)/shard_map/ppermute | solution.py:537
  34.7 5.9 %collective-permute-start.6 = (f32[224,128]{1,0:T(8,128)S(1)}, f32[224,128]{1,0:T(8,128)S(1)}, u32[]{:S(2)}, u32[]{:S(2)}) collective-permute-start(f32[224,128]{1,0:T(8,128)S(1)} %pad_maximum_fusion), channel_id=1, source_target_pairs={{0,4},{2,6},{4,0},{6,2},{1,5},{3,7},{5,1},{7,3},{8,12},{10,14},{12... | collective-permute-start | bytes 344072 | tf_op jit(solution)/shard_map/ppermute | solution.py:537
  37.2 4.1 %collective-permute-start.7 = (f32[224,128]{1,0:T(8,128)S(1)}, f32[224,128]{1,0:T(8,128)S(1)}, u32[]{:S(2)}, u32[]{:S(2)}) collective-permute-start(f32[224,128]{1,0:T(8,128)S(1)} %pad_maximum_fusion), channel_id=1, source_target_pairs={{0,6},{2,0},{4,2},{6,4},{1,7},{3,1},{5,3},{7,5},{8,14},{10,8},{12,... | collective-permute-start | bytes 344072 | tf_op jit(solution)/shard_map/ppermute | solution.py:537
  39.7 29.3 %copy-start.6 = (s32[256,27]{0,1:T(8,128)S(1)}, s32[256,27]{0,1:T(8,128)}, u32[]{:S(2)}) copy-start(s32[256,27]{0,1:T(8,128)} %param.15) | copy-start | bytes 82948
  41.2 28.1 %copy-start.7 = (s32[256,16]{0,1:T(8,128)S(1)}, s32[256,16]{0,1:T(8,128)}, u32[]{:S(2)}) copy-start(s32[256,16]{0,1:T(8,128)} %param.17) | copy-start | bytes 49156
  41.2 28.1 %copy-start.8 = (s32[256,16]{0,1:T(8,128)S(1)}, s32[256,16]{0,1:T(8,128)}, u32[]{:S(2)}) copy-start(s32[256,16]{0,1:T(8,128)} %param.16) | copy-start | bytes 49156
  41.9 10.2 %collective-permute-start.8 = (f32[896,128]{1,0:T(8,128)S(1)}, f32[896,128]{1,0:T(8,128)S(1)}, u32[]{:S(2)}, u32[]{:S(2)}) collective-permute-start(f32[896,128]{1,0:T(8,128)S(1)} %get-tuple-element.122), channel_id=1, source_target_pairs={{0,1},{1,64},{64,65},{65,0},{2,3},{3,66},{66,67},{67,2},{4,5},{5,6... | collective-permute-start | bytes 1376264 | tf_op jit(solution)/shard_map/ppermute | solution.py:537
  45.0 17.3 %collective-permute-start.9 = (f32[896,128]{1,0:T(8,128)S(1)}, f32[896,128]{1,0:T(8,128)S(1)}, u32[]{:S(2)}, u32[]{:S(2)}) collective-permute-start(f32[896,128]{1,0:T(8,128)S(1)} %get-tuple-element.122), channel_id=1, source_target_pairs={{0,64},{1,65},{64,0},{65,1},{2,66},{3,67},{66,2},{67,3},{4,68},{5,... | collective-permute-start | bytes 1376264 | tf_op jit(solution)/shard_map/ppermute | solution.py:537
  46.0 19.8 %collective-permute-start.10 = (f32[896,128]{1,0:T(8,128)S(1)}, f32[896,128]{1,0:T(8,128)S(1)}, u32[]{:S(2)}, u32[]{:S(2)}) collective-permute-start(f32[896,128]{1,0:T(8,128)S(1)} %get-tuple-element.122), channel_id=1, source_target_pairs={{0,65},{1,0},{64,1},{65,64},{2,67},{3,2},{66,3},{67,66},{4,69},{5,... | collective-permute-start | bytes 1376264 | tf_op jit(solution)/shard_map/ppermute | solution.py:537
  66.6 188.6 %collective-permute-start.11 = (f32[3584,128]{1,0:T(8,128)}, f32[3584,128]{1,0:T(8,128)}, u32[]{:S(2)}, u32[]{:S(2)}) collective-permute-start(f32[3584,128]{1,0:T(8,128)} %constant_dynamic-update-slice_fusion.7.mine_ref), channel_id=1, source_target_pairs={{0,32},{32,0},{1,33},{33,1},{2,34},{34,2},{3,35},{35,3},{4,36},{36... | collective-permute-start | bytes 5505032 | tf_op jit(solution)/shard_map/ppermute | solution.py:583
  88.5 125.0 %slice-start = ((s8[14237696]{0:T(1024)(128)(4,1)}), s8[4194304]{0:T(1024)(128)(4,1)S(1)}, s32[]{:S(2)}) async-start(s8[14237696]{0:T(1024)(128)(4,1)} %bitcast.24), calls=%async_computation.1 | async-start | bytes 8388608
  88.5 125.0 %slice-start.1 = ((s8[14237696]{0:T(1024)(128)(4,1)}), s8[4194304]{0:T(1024)(128)(4,1)S(1)}, s32[]{:S(2)}) async-start(s8[14237696]{0:T(1024)(128)(4,1)} %bitcast.24), calls=%async_computation.2 | async-start | bytes 8388608
  150.3 1.0 copy-start.3
  151.3 62.2 %slice-start.2 = ((s8[14237696]{0:T(1024)(128)(4,1)}), s8[4194304]{0:T(1024)(128)(4,1)S(1)}, s32[]{:S(2)}) async-start(s8[14237696]{0:T(1024)(128)(4,1)} %bitcast.24), calls=%async_computation.3 | async-start | bytes 8388608
  151.3 62.2 %slice-start.3 = ((s8[14237696]{0:T(1024)(128)(4,1)}), s8[1654784]{0:T(1024)(128)(4,1)S(1)}, s32[]{:S(2)}) async-start(s8[14237696]{0:T(1024)(128)(4,1)} %bitcast.24), calls=%async_computation.4 | async-start | bytes 3309568
  255.2 34.4 %copy-start.5 = (f32[8,81,81]{2,0,1:T(8,128)S(1)}, f32[8,81,81]{2,0,1:T(8,128)}, u32[]{:S(2)}) copy-start(f32[8,81,81]{2,0,1:T(8,128)} %param.21) | copy-start | bytes 629860
  289.6 0.6 copy-start.9

commit v2 on v1

v2 whole, which is shorter than its diff:
```python
import functools

import jax
import jax.numpy as jnp
from jax import lax
from jax.experimental import pallas as pl
from jax.experimental.pallas import tpu as pltpu
from jax.sharding import Mesh, PartitionSpec as P

ORDER = 8
COEF = 81
PART = 64
LEAVES = 256
PAIRS = 128
HALO = 32
HPAIRS = 16
WPAIRS = PAIRS + 2 * HPAIRS
NEAR = 27
LLIST = 16
TLIST = 64
TOPBOX = 4096
ROW_BITS = 12
CLASSES = 316
OPROWS = 88
SOFTENING = 0.01
SEND = 56
REACH_SQ = 16.0
FEAT = 32
LEAF_STEP = 4
TURN_STEP = 3
TOP_WINDOW = 256

HIGH = lax.Precision.HIGHEST
MIB = 1 << 20
AXES = ("zlo", "core", "y", "x", "zhi")

NN = (((1,), (0,)), ((), ()))
NT = (((1,), (1,)), ((), ()))


def dot_f32(left, right, dims=NN):
    return lax.dot_general(left, right, dims, precision=HIGH, preferred_element_type=jnp.float32)


def lanes(shape):
    return lax.broadcasted_iota(jnp.int32, shape, len(shape) - 1)


def rows_of(shape):
    return lax.broadcasted_iota(jnp.int32, shape, len(shape) - 2)


def harmonics(coord_x, coord_y, coord_z):
    radius_sq = coord_x * coord_x + coord_y * coord_y + coord_z * coord_z
    terms = {(0, 0): (None, None)}
    for m in range(1, ORDER + 1):
        if m == 1:
            terms[1, 1] = (coord_x * 0.5, coord_y * 0.5)
            continue
        re, im = terms[m - 1, m - 1]
        scale = 1.0 / (2.0 * m)
        terms[m, m] = (
            (coord_x * re - coord_y * im) * scale,
            (coord_x * im + coord_y * re) * scale,
        )
    for m in range(ORDER):
        re, im = terms[m, m]
        terms[m + 1, m] = (coord_z, None) if m == 0 else (coord_z * re, coord_z * im)
    for m in range(ORDER - 1):
        for n in range(m + 2, ORDER + 1):
            one = (2.0 * n - 1.0) / ((n - m) * (n + m))
            two = 1.0 / ((n - m) * (n + m))
            z_one = coord_z * one
            r_two = radius_sq * two
            upper, lower = terms[n - 1, m], terms[n - 2, m]
            re = z_one * upper[0] - (r_two if lower[0] is None else r_two * lower[0])
            im = None if m == 0 else z_one * upper[1] - r_two * lower[1]
            terms[n, m] = (re, im)
    listed = []
    for n in range(ORDER + 1):
        listed.append(terms[n, 0][0])
        for m in range(1, n + 1):
            listed.extend(terms[n, m])
    return listed


def centred(block):
    turned = block.T
    halves = []
    for p in range(2):
        half = turned[p * PART : (p + 1) * PART]
        halves.append(half - jnp.sum(half, axis=0, keepdims=True) * (1.0 / PART))
    return jnp.concatenate(halves, axis=0)


def expand_into(d_ref, q_ref, acc_ref, out_ref):
    for p in range(2):
        acc_ref[...] = jnp.zeros_like(acc_ref)

        def step(s, carry):
            at = pl.ds(pl.multiple_of(p * PART + s * 16, 16), 16)
            charge = q_ref[at, :]
            listed = harmonics(d_ref[0, at, :], d_ref[1, at, :], d_ref[2, at, :])
            for c, term in enumerate(listed):
                value = charge if term is None else charge * term
                acc_ref[c] += value[:8] + value[8:]
            return carry

        lax.fori_loop(0, PART // 16, step, 0)
        sums = jnp.sum(acc_ref[...], axis=1)
        full = jnp.concatenate([sums, jnp.zeros((128 - COEF, 128), jnp.float32)], axis=0)
        out_ref[pl.ds(p, PAIRS, stride=2), :] = full.T


def widen(block):
    return jnp.concatenate(
        [block, jnp.zeros((block.shape[0], 128 - block.shape[1]), jnp.float32)], axis=1
    )


def first_kernel(
    pts_ref, count_ref, top_ref, tops_ref, m2m_ref,
    own_ref, low_ref, high_ref, dist_ref, moment_ref, send_ref, part_ref, mask_ref,
    q_ref, acc_ref, lift_ref,
):
    lane = lanes((1, 128))

    def hold(i, carry):
        for u in range(8):
            r = i * 8 + u
            held = jnp.where(lane < PART, count_ref[2 * r], count_ref[2 * r + 1])
            mask_ref[pl.ds(r, 1), :] = jnp.where((lane & (PART - 1)) < held, 1.0, 0.0)
        return carry

    lax.fori_loop(0, PAIRS // 8, hold, 0)
    charge = pts_ref[pl.ds(3, PAIRS, stride=4), :] * mask_ref[...]
    own_ref[...] = pts_ref[...]
    own_ref[pl.ds(3, PAIRS, stride=4), :] = charge
    low_ref[...] = own_ref[: 4 * HPAIRS]
    high_ref[...] = own_ref[4 * (PAIRS - HPAIRS) :]
    for c in range(3):
        dist_ref[c] = centred(pts_ref[pl.ds(c, PAIRS, stride=4), :])
    q_ref[...] = charge.T
    expand_into(dist_ref, q_ref, acc_ref, moment_ref)
    first, last = top_ref[0], top_ref[LEAVES - 1]
    for a in range(8):
        at = pl.ds(a, LEAVES // 8, stride=8)
        lift_ref[at, :] = widen(dot_f32(moment_ref[at, :][:, :COEF], m2m_ref[:, a, :], NT))
    held = jnp.where(rows_of((LEAVES, LEAVES)) == tops_ref[...] - first, 1.0, 0.0)
    wide = dot_f32(held, lift_ref[...])
    lane = lanes((LEAVES, 128))
    wide = jnp.where(lane == 127, first.astype(jnp.float32), wide)
    wide = jnp.where(lane == 126, last.astype(jnp.float32), wide)
    part_ref[...] = wide
    send_ref[...] = wide[:SEND]


def turn_kernel(in_ref, after_ref, out_ref):
    del after_ref

    def step(i, carry):
        for u in range(TURN_STEP):
            one = in_ref[i * TURN_STEP + u]
            for begin in range(0, CLASSES, 128):
                count = min(128, CLASSES - begin)
                at = pl.ds(begin * OPROWS + i * TURN_STEP + u, count, stride=OPROWS)
                out_ref[at, :] = widen(one[:, begin : begin + count].T)
        return carry

    lax.fori_loop(0, COEF // TURN_STEP, step, 0)


def join_kernel(*refs):
    out_ref = refs[-1]
    rows = refs[0].shape[0]
    for i, ref in enumerate(refs[:4]):
        out_ref[i * rows : (i + 1) * rows] = ref[...]


def split3(value):
    high = value.astype(jnp.bfloat16).astype(jnp.float32)
    rest = value - high
    middle = rest.astype(jnp.bfloat16).astype(jnp.float32)
    low = (rest - middle).astype(jnp.bfloat16).astype(jnp.float32)
    return high, middle, low


def near_kernel(
    near_ref, own_ref, before_ref, behind_ref, after_ref, out_ref,
    win_ref, src_ref, tgt_ref, table_ref, charge_ref,
):
    del after_ref
    targets, width = PAIRS, WPAIRS
    edge = 4 * HPAIRS
    win_ref[:edge] = before_ref[...]
    win_ref[edge : edge + 4 * PAIRS] = own_ref[...]
    win_ref[edge + 4 * PAIRS :] = behind_ref[...]
    shift = lax.axis_index(AXES) * LEAVES - HALO

    def component(c):
        return win_ref[pl.ds(c, width, stride=4), :]

    points = [component(c) for c in range(3)]
    moved = []
    for c in range(3):
        least = jnp.min(points[c], keepdims=True)
        most = jnp.max(points[c], keepdims=True)
        moved.append(points[c] - 0.5 * (least + most))
    norm = moved[0] * moved[0] + moved[1] * moved[1] + moved[2] * moved[2]
    close = jnp.max(norm) <= REACH_SQ

    @pl.when(close)
    def _():
        own = slice(HPAIRS, HPAIRS + targets)
        src_ref[...] = jnp.zeros_like(src_ref)
        tgt_ref[...] = jnp.zeros_like(tgt_ref)
        for c in range(3):
            h, m, l = split3(moved[c])
            for i, feature in enumerate((h, h, m, m, h, l)):
                src_ref[pl.ds(6 * c + i, width, stride=FEAT), :] = feature
            th, tm, tl = [-2.0 * piece[own] for piece in (h, m, l)]
            for i, feature in enumerate((th, tm, th, tm, tl, th)):
                tgt_ref[pl.ds(6 * c + i, targets, stride=FEAT), :] = feature
        ones = jnp.ones((width, 128), jnp.float32)
        for i, feature in enumerate(split3(norm + SOFTENING)):
            src_ref[pl.ds(18 + i, width, stride=FEAT), :] = feature
            tgt_ref[pl.ds(18 + i, targets, stride=FEAT), :] = ones[own]
        for i, feature in enumerate(split3(norm[own])):
            src_ref[pl.ds(21 + i, width, stride=FEAT), :] = ones
            tgt_ref[pl.ds(21 + i, targets, stride=FEAT), :] = feature
        for i, feature in enumerate(split3(component(3))):
            src_ref[pl.ds(24 + i, width, stride=FEAT), :] = feature

        row = rows_of((128, 256))
        lane = lanes((128, 256))
        spread = []
        for p in range(4):
            local = row - FEAT * p
            same = (lane < 128) & (local < 24) & (local == (lane & (FEAT - 1)))
            charge = (lane >= 128) & (local >= 24) & (local < 27)
            spread.append(jnp.where(same | charge, 1.0, 0.0).astype(jnp.bfloat16))

        def build(i, carry):
            for g in (2 * i, 2 * i + 1):
                block = src_ref[pl.ds(pl.multiple_of(g * 128, 128), 128), :]
                turned = block.T.astype(jnp.bfloat16)
                for p in range(4):
                    both = lax.dot_general(
                        turned, spread[p], NN, preferred_element_type=jnp.float32
                    )
                    to = pl.ds(pl.multiple_of((g * 4 + p) * 128, 128), 128)
                    table_ref[to, :] = both[:, :128].astype(jnp.bfloat16)
                    charge_ref[to, :] = both[:, 128:]
            return carry

        lax.fori_loop(0, width // 8, build, 0)

        lane_w = lanes((FEAT, 128))
        lane_b = lanes((PART, 128))
        low_half = lane_b < PART
        def group(g, carry):
            two = tgt_ref[pl.ds(pl.multiple_of(g * 2 * FEAT, 2 * FEAT), 2 * FEAT), :]
            zero = jnp.zeros((FEAT, 128), jnp.float32)
            left, right = [], []
            for half in range(2):
                one = two[half * FEAT : (half + 1) * FEAT]
                low = jnp.where(lane_w < PART, one, 0.0)
                high = jnp.where(lane_w < PART, 0.0, one)
                left += [low, high] if half == 0 else [zero, zero]
                right += [zero, zero] if half == 0 else [low, high]
            weights = jnp.concatenate(
                [jnp.concatenate(left, axis=0), jnp.concatenate(right, axis=0)], axis=1
            ).astype(jnp.bfloat16)
            mixed, spots = [], []
            for k in range(NEAR):
                four = []
                for v in range(4):
                    leaf = near_ref[k, g * 4 + v] - shift
                    four.append(pl.ds(pl.multiple_of(leaf * PART, PART), PART))
                rows = [table_ref[spot, :] for spot in four]
                mixed.append(
                    jnp.where(
                        lane_b < 2 * FEAT,
                        jnp.where(lane_b < FEAT, rows[0], rows[1]),
                        jnp.where(lane_b < 3 * FEAT, rows[2], rows[3]),
                    )
                )
                spots.append(four)
            total = [jnp.zeros((8, 128), jnp.float32)] * 2
            for some in range(0, NEAR, 14):
                count = min(14, NEAR - some)
                dist = lax.dot_general(
                    jnp.concatenate(mixed[some : some + count], axis=0), weights, NN,
                    preferred_element_type=jnp.float32,
                )
                for k in range(count):
                    inverse = lax.rsqrt(dist[k * PART : (k + 1) * PART])
                    for half in range(2):
                        low, high = spots[some + k][2 * half : 2 * half + 2]
                        charge = jnp.where(low_half, charge_ref[low, :], charge_ref[high, :])
                        term = charge * inverse[:, half * 128 : (half + 1) * 128]
                        total[half] += jnp.sum(term.reshape(8, 8, 128), axis=0)
            both = jnp.concatenate([jnp.sum(t, axis=0, keepdims=True) for t in total], axis=0)
            out_ref[pl.ds(g * 2, 2), :] = both
            return carry

        lax.fori_loop(0, targets // 2, group, 0)

    @pl.when(jnp.logical_not(close))
    def _():
        lane = lanes((PART, 128))

        def pair(r, carry):
            columns = [
                jnp.broadcast_to(
                    win_ref[pl.ds(4 * (HPAIRS + r) + c, 1), :], (128, 128)
                ).T
                for c in range(3)
            ]
            results = []
            for p in range(2):
                mine = [column[p * PART : (p + 1) * PART] for column in columns]

                def entry(k, total):
                    leaf = near_ref[k, 2 * r + p] - shift
                    at = 4 * (leaf // 2)
                    gap = SOFTENING
                    for c in range(3):
                        diff = mine[c] - win_ref[pl.ds(at + c, 1), :]
                        gap = gap + diff * diff
                    half = jnp.where((lane // PART) == leaf % 2, 1.0, 0.0)
                    return total + half * (win_ref[pl.ds(at + 3, 1), :] * lax.rsqrt(gap))

                total = lax.fori_loop(0, NEAR, entry, jnp.zeros((PART, 128), jnp.float32))
                results.append(jnp.sum(total, axis=1, keepdims=True))
            wide = jnp.broadcast_to(jnp.concatenate(results, axis=0), (128, 128)).T
            out_ref[pl.ds(r, 1), :] = wide[:1]
            return carry

        lax.fori_loop(0, targets, pair, 0)


def gather_products(codes, ops_ref, rows_ref):
    total = None
    for code in codes:
        at = pl.ds(pl.multiple_of(code >> ROW_BITS, 8), OPROWS)
        row = rows_ref[pl.ds(code & ((1 << ROW_BITS) - 1), 1), :]
        term = ops_ref[at, :] * row
        total = term if total is None else total + term
    return total


def pack_codes(kinds, rows):
    return ((kinds * OPROWS) << ROW_BITS) | rows


def put_sums(total_ref, out_ref, lane):
    sums = jnp.sum(total_ref[...], axis=1, keepdims=True)
    out_ref[...] = jnp.where(lanes((OPROWS, 128)) == lane, sums, out_ref[...])


def halo_kernel(
    list_ref, class_ref, moment_ref, before_ref, behind_ref, code_ref, rows_ref,
    d_ref, q_ref, acc_ref, halo_ref,
):
    shift = lax.axis_index(AXES) * LEAVES - HALO
    code_ref[...] = pack_codes(class_ref[...], list_ref[...] - shift)
    fill = jnp.zeros((PAIRS - 2 * HPAIRS, 128), jnp.float32)

    def component(c):
        at = pl.ds(c, HPAIRS, stride=4)
        return jnp.concatenate([before_ref[at, :], behind_ref[at, :], fill], axis=0)

    for c in range(3):
        d_ref[c] = centred(component(c))
    q_ref[...] = component(3).T
    expand_into(d_ref, q_ref, acc_ref, halo_ref)
    rows_ref[:HALO] = halo_ref[:HALO]
    rows_ref[HALO : HALO + LEAVES] = moment_ref[...]
    rows_ref[HALO + LEAVES :] = halo_ref[HALO : 2 * HALO]


def leaf_kernel(part, code_ref, ops_ref, rows_ref, after_ref, out_ref, total_ref):
    del after_ref
    begin = part * (PAIRS // 2)

    def reduce(i):
        for v in range(LEAF_STEP):
            put_sums(total_ref.at[v], out_ref.at[v & 1], begin + 2 * i + (v >> 1))

    def step(i, carry):
        reduce(i - 1)
        for v in range(LEAF_STEP):
            leaf = 2 * begin + i * LEAF_STEP + v
            total_ref[v] = gather_products(
                [code_ref[k, leaf] for k in range(LLIST)], ops_ref, rows_ref
            )
        return carry

    total_ref[...] = jnp.zeros_like(total_ref)
    out_ref[...] = jnp.zeros_like(out_ref)
    steps = LEAVES // 2 // LEAF_STEP
    lax.fori_loop(0, steps, step, 0)
    reduce(steps - 1)


def fetch_kernel(top_ref, list_ref, class_ref, code_ref, list_vmem, class_vmem, sems):
    at = pl.ds(pl.multiple_of(window_start(top_ref), 128), TOP_WINDOW)
    copies = [
        pltpu.make_async_copy(list_ref.at[:, at], list_vmem, sems.at[0]),
        pltpu.make_async_copy(class_ref.at[:, at], class_vmem, sems.at[1]),
    ]
    for copy in copies:
        copy.start()
    for copy in copies:
        copy.wait()
    code_ref[...] = pack_codes(class_vmem[...], list_vmem[...])


def window_start(top_ref):
    return jnp.minimum(top_ref[0] // 128 * 128, TOPBOX - TOP_WINDOW)


def finish(
    cap, begin, top_ref, code_ref, table_ref, ops_ref, m2m_ref, tops_ref, local_refs, dist_ref,
    near_ref, mask_ref, out_ref, field_ref, pot_ref, total_ref, wide_ref, rows_ref,
):
    first = top_ref[0]
    boxes = top_ref[LEAVES - 1] - first + 1
    spread = jnp.zeros((OPROWS, LEAVES), jnp.float32)
    width = min(cap, 128)
    for block in range(cap // width):
        total_ref[...] = jnp.zeros_like(total_ref)
        wide_ref[...] = jnp.zeros_like(wide_ref)

        def step(b, carry):
            put_sums(total_ref, wide_ref, b - 1)
            column = first - begin + block * width + b
            total_ref[...] = gather_products(
                [code_ref[k, column] for k in range(TLIST)], ops_ref, table_ref
            )
            return carry

        count = jnp.clip(boxes - block * width, 0, width)
        lax.fori_loop(0, count, step, 0)
        put_sums(total_ref, wide_ref, count - 1)
        place = rows_of((128, LEAVES)) + block * width
        held = jnp.where(place == tops_ref[...] - first, 1.0, 0.0)
        spread += dot_f32(wide_ref[...], held)
    full = jnp.concatenate([spread, jnp.zeros((128 - OPROWS, LEAVES), jnp.float32)], axis=0)
    rows_ref[...] = full.T
    for a in range(8):
        at = pl.ds(a, LEAVES // 8, stride=8)
        rows_ref[at, :] = widen(dot_f32(rows_ref[at, :][:, :COEF], m2m_ref[:, a, :]))
    for p in range(2):
        field_ref[p] = (
            rows_ref[pl.ds(p, PAIRS, stride=2), :].T[:OPROWS]
            + local_refs[0][p] + local_refs[1][p]
        )
    for p in range(2):

        def step(s, carry):
            at = pl.ds(pl.multiple_of(p * PART + s * 16, 16), 16)
            listed = harmonics(dist_ref[0, at, :], dist_ref[1, at, :], dist_ref[2, at, :])
            total = None
            for c, term in enumerate(listed):
                weight = field_ref[p, pl.ds(c, 1), :]
                value = jnp.broadcast_to(weight, (16, 128)) if term is None else term * weight
                total = value if total is None else total + value
            pot_ref[at, :] = total
            return carry

        lax.fori_loop(0, PART // 16, step, 0)
    out_ref[...] = (near_ref[...] + pot_ref[...].T) * mask_ref[...]


def last_kernel(
    top_ref, code_ref, mine_ref, other_ref, ops_ref, m2m_ref, tops_ref, local_a_ref, local_b_ref,
    dist_ref, near_ref, mask_ref, out_ref, over_ref, table_ref, *scratch,
):
    core, my_y, my_x = lax.axis_index("core"), lax.axis_index("y"), lax.axis_index("x")
    my_z = lax.axis_index(("zlo", "zhi"))
    table_ref[0:1, :] = jnp.zeros((1, 128), jnp.float32)
    over_ref[0] = 0

    def assemble(ref, zlo):
        def step(i, carry):
            y, x, zhi = i // 8, (i // 2) % 4, i % 2
            block = ((my_z - (zlo * 2 + zhi)) & 3) * 16 + ((my_x - x) & 3) * 4 + ((my_y - y) & 3)
            at = pl.multiple_of(block * SEND, 8)
            ends = ref[pl.ds(at, 1), :]
            begin = ends[0, 127].astype(jnp.int32)
            end = ends[0, 126].astype(jnp.int32)
            over_ref[0] = jnp.maximum(over_ref[0], end - begin + 1)
            so_far = table_ref[pl.ds(begin, 1), :]
            table_ref[pl.ds(begin, SEND), :] = ref[pl.ds(at, SEND), :]
            table_ref[pl.ds(begin, 1), :] = ends + so_far
            return carry

        lax.fori_loop(0, 32, step, 0)

    for zlo in range(2):
        for side in range(2):

            @pl.when(core == side)
            def _():
                assemble(mine_ref, zlo)

            @pl.when(core != side)
            def _():
                assemble(other_ref, zlo)

    @pl.when(over_ref[0] < SEND)
    def _():
        finish(
            64, window_start(top_ref), top_ref, code_ref, table_ref, ops_ref, m2m_ref, tops_ref,
            (local_a_ref, local_b_ref), dist_ref, near_ref, mask_ref, out_ref, *scratch,
        )


def spare_kernel(
    top_ref, code_ref, table_ref, ops_ref, m2m_ref, tops_ref, local_a_ref, local_b_ref,
    dist_ref, near_ref, mask_ref, out_ref, *scratch,
):
    finish(
        LEAVES, jnp.minimum(top_ref[0], TOPBOX - LEAVES), top_ref, code_ref, table_ref, ops_ref, m2m_ref, tops_ref,
        (local_a_ref, local_b_ref), dist_ref, near_ref, mask_ref, out_ref, *scratch,
    )


SMEM = pl.BlockSpec(memory_space=pltpu.SMEM)
VMEM = pl.BlockSpec(memory_space=pltpu.VMEM)
F32 = jnp.float32


def shape(*dims):
    return jax.ShapeDtypeStruct(dims, F32)


ANY = pl.BlockSpec(memory_space=pl.ANY)
FINISH_SCRATCH = [
    pltpu.VMEM((2, OPROWS, 128), F32),
    pltpu.VMEM((128, 128), F32),
    pltpu.VMEM((OPROWS, 128), F32),
    pltpu.VMEM((OPROWS, 128), F32),
    pltpu.VMEM((LEAVES, 128), F32),
]


def cost(flops, bytes_accessed):
    return pl.CostEstimate(flops=flops, bytes_accessed=bytes_accessed, transcendentals=0)


def call_first(pts, counts, leaf_top, tops, m2m):
    return pl.pallas_call(
        first_kernel,
        out_shape=(
            shape(4 * PAIRS, 128), shape(4 * HPAIRS, 128), shape(4 * HPAIRS, 128),
            shape(3, PAIRS, 128), shape(LEAVES, 128), shape(SEND, 128), shape(LEAVES, 128),
            shape(PAIRS, 128),
        ),
        in_specs=[VMEM, SMEM, SMEM, VMEM, VMEM],
        out_specs=(VMEM,) * 8,
        scratch_shapes=[
            pltpu.VMEM((128, 128), F32), pltpu.VMEM((COEF, 8, 128), F32),
            pltpu.VMEM((LEAVES, 128), F32),
        ],
        compiler_params=pltpu.CompilerParams(vmem_limit_bytes=16 * MIB),
        cost_estimate=cost(10**9, 10**7),
        name="expand_own",
    )(pts, counts, leaf_top, tops, m2m)


def call_turn(ops, after):
    return pl.pallas_call(
        turn_kernel,
        out_shape=shape(CLASSES * OPROWS, 128),
        in_specs=[VMEM, ANY],
        out_specs=VMEM,
        compiler_params=pltpu.CompilerParams(vmem_limit_bytes=30 * MIB),
        cost_estimate=cost(10**7, 3 * 10**7),
        name="turn_operators",
    )(ops, after)


def call_join(pieces, *after):
    rows = pieces[0].shape[0]
    return pl.pallas_call(
        join_kernel,
        out_shape=shape(4 * rows, 128),
        in_specs=[VMEM] * 4 + [ANY] * len(after),
        out_specs=VMEM,
        compiler_params=pltpu.CompilerParams(vmem_limit_bytes=8 * MIB),
        cost_estimate=cost(10**5, 8 * rows * 512),
        name="join",
    )(*pieces, *after)


def call_near(near, own, before, behind, after):
    targets, width = PAIRS, WPAIRS
    return pl.pallas_call(
        near_kernel,
        out_shape=shape(targets, 128),
        in_specs=[SMEM, VMEM, VMEM, VMEM, ANY],
        out_specs=VMEM,
        scratch_shapes=[
            pltpu.VMEM((4 * WPAIRS, 128), F32),
            pltpu.VMEM((width * FEAT, 128), F32),
            pltpu.VMEM((targets * FEAT, 128), F32),
            pltpu.VMEM((width * 128, 128), jnp.bfloat16),
            pltpu.VMEM((width * 128, 128), F32),
        ],
        compiler_params=pltpu.CompilerParams(vmem_limit_bytes=30 * MIB),
        cost_estimate=cost(10 * targets * 2 * 64 * NEAR * 64, 3 * 10**7),
        name="near",
    )(near, own, before, behind, after)


def call_halo(lists, classes, moments, before, behind):
    return pl.pallas_call(
        halo_kernel,
        out_shape=(jax.ShapeDtypeStruct((LLIST, LEAVES), jnp.int32), shape(2 * WPAIRS, 128)),
        in_specs=[VMEM] * 5,
        out_specs=(VMEM, VMEM),
        scratch_shapes=[
            pltpu.VMEM((3, 128, 128), F32),
            pltpu.VMEM((128, 128), F32),
            pltpu.VMEM((COEF, 8, 128), F32),
            pltpu.VMEM((LEAVES, 128), F32),
        ],
        compiler_params=pltpu.CompilerParams(vmem_limit_bytes=16 * MIB),
        cost_estimate=cost(10**8, 10**6),
        name="expand_halo",
    )(lists, classes, moments, before, behind)


def call_leaf(part, code, ops, rows, after):
    return pl.pallas_call(
        functools.partial(leaf_kernel, part),
        out_shape=shape(2, OPROWS, 128),
        in_specs=[SMEM, VMEM, VMEM, ANY],
        out_specs=VMEM,
        scratch_shapes=[pltpu.VMEM((LEAF_STEP, OPROWS, 128), F32)],
        compiler_params=pltpu.CompilerParams(vmem_limit_bytes=24 * MIB),
        cost_estimate=cost(LEAVES * LLIST * COEF * COEF * 8, 2 * 10**7),
        name="leaf_translate",
    )(code, ops, rows, after)


def call_fetch(leaf_top, lists, classes):
    window = (TLIST, TOP_WINDOW)
    return pl.pallas_call(
        fetch_kernel,
        out_shape=jax.ShapeDtypeStruct(window, jnp.int32),
        in_specs=[SMEM, ANY, ANY],
        out_specs=VMEM,
        scratch_shapes=[
            pltpu.VMEM(window, jnp.int32), pltpu.VMEM(window, jnp.int32),
            pltpu.SemaphoreType.DMA((2,)),
        ],
        compiler_params=pltpu.CompilerParams(vmem_limit_bytes=8 * MIB),
        cost_estimate=cost(10**5, 10**5),
        name="fetch_lists",
    )(leaf_top, lists, classes)


def call_last(leaf_top, code, mine, other, *rest):
    return pl.pallas_call(
        last_kernel,
        out_shape=(shape(PAIRS, 128), jax.ShapeDtypeStruct((1,), jnp.int32)),
        in_specs=[SMEM, SMEM] + [VMEM] * 10,
        out_specs=(VMEM, SMEM),
        scratch_shapes=[pltpu.VMEM((TOPBOX + SEND, 128), F32)] + FINISH_SCRATCH,
        compiler_params=pltpu.CompilerParams(vmem_limit_bytes=32 * MIB),
        name="finish",
    )(leaf_top, code, mine, other, *rest)


def call_spare(leaf_top, code, table, *rest):
    return pl.pallas_call(
        spare_kernel,
        out_shape=shape(PAIRS, 128),
        in_specs=[SMEM, SMEM] + [VMEM] * 9,
        out_specs=VMEM,
        scratch_shapes=FINISH_SCRATCH,
        compiler_params=pltpu.CompilerParams(vmem_limit_bytes=32 * MIB),
        name="finish_spare",
    )(leaf_top, code, table, *rest)


def sent_over(block, axis, count):
    return [block] + [
        lax.ppermute(block, axis, [(i, (i + s) % count) for i in range(count)])
        for s in range(1, count)
    ]


def body(
    particles, counts, leaf_top, near_list, leaf_list, leaf_class, top_list, top_class,
    m2l_ops, m2m_ops,
):
    pts = particles.reshape(4, PAIRS, 128).transpose(1, 0, 2).reshape(4 * PAIRS, 128)
    tops = leaf_top.reshape(1, LEAVES)
    m2m = m2m_ops.transpose(1, 0, 2)
    own, low, high, dist, moments, send, partial, mask = call_first(
        pts, counts, leaf_top, tops, m2m
    )
    devices = lax.axis_size(AXES)
    up = [(i, (i + 1) % devices) for i in range(devices)]
    down = [(j, i) for i, j in up]
    over_y = sent_over(send, "y", 4)
    before = lax.ppermute(high, AXES, up)
    behind = lax.ppermute(low, AXES, down)
    ops = call_turn(m2l_ops.transpose(1, 2, 0), send)
    by_y = call_join(over_y, ops, before, behind)
    over_x = sent_over(by_y, "x", 4)
    near = call_near(near_list.T, own, before, behind, by_y)
    by_x = call_join(over_x, near)
    over_z = sent_over(by_x, ("zlo", "zhi"), 4)
    code, rows = call_halo(leaf_list.T, leaf_class.T, moments, before, behind)
    local_a = call_leaf(0, code, ops, rows, by_x)
    mine = call_join(over_z, local_a)
    other = lax.ppermute(mine, "core", [(0, 1), (1, 0)])
    local_b = call_leaf(1, code, ops, rows, mine)
    top_code = call_fetch(leaf_top, top_list.T, top_class.T)
    rest = (ops, m2m, tops, local_a, local_b, dist, near, mask)
    result, over = call_last(leaf_top, top_code, mine, other, *rest)

    def spare():
        table = lax.dynamic_update_slice(
            jnp.zeros((TOPBOX + LEAVES, 128), F32), partial, (leaf_top[0], 0)
        )
        for k in range(7):
            swap = [(i, i ^ (1 << k)) for i in range(devices)]
            table = table + lax.ppermute(table, AXES, swap)
        start = jnp.minimum(leaf_top[0], TOPBOX - LEAVES)
        lists, classes = (
            lax.dynamic_slice_in_dim(x, start, LEAVES, axis=0).T for x in (top_list, top_class)
        )
        return call_spare(leaf_top, pack_codes(classes, lists), table, *rest)

    result = lax.cond(over[0] >= SEND, spare, lambda: result)
    return result.reshape(-1)


def solution(mesh):
    fine = Mesh(mesh.devices.reshape(2, 2, 4, 4, 2), AXES)
    return jax.shard_map(
        body,
        mesh=fine,
        in_specs=(
            P(None, AXES), P(AXES), P(AXES), P(AXES, None), P(AXES, None), P(AXES, None),
            P(), P(), P(), P(),
        ),
        out_specs=P(AXES),
        check_vma=False,
    )
```

time: 300 us -> 160 us (0.53)
  Pallas kernels: 202 us -> 127 us
  local copies, waits for them, and re-layouts: 28.9 us -> 6.39 us
  waiting for transfers between devices: 19.4 us -> 1.73 us
  between operations: 16.6 us -> 0.87 us
  starting transfers between devices: 28.4 us -> 21.2 us
    pallas_call x4 -> x10, Pallas kernels: 169 us -> 96 us  [the longest x1 45.6 us: call_near(): pl.pallas_call(near_kernel, out_shape=shape(targets, 128), in_specs=[SMEM...]
    ppermute x11, waiting for transfers between devices: 19.4 us -> 1.73 us  [the longest x9 1.72 us: sent_over(): lax.ppermute(block, axis, [(i, (i + s) % count) for i in range(count)])]
    unnamed x34 -> x18, local copies, waits for them, and re-layouts: 22.1 us -> 6.39 us
    ppermute x11, starting transfers between devices: 22.9 us -> 16.7 us  [the longest x9 8.82 us: sent_over(): lax.ppermute(block, axis, [(i, (i + s) % count) for i in range(count)])]
  transfers between devices with their start and end apart: 12 -> 12, of which waited for: 5 -> 1; matrix products, arithmetic and copies ran while one was open for 7% -> 0% of each run, Pallas kernels for 56% -> 59%
where the time goes in v2:
time: 160 us; the launch traced here: 157 us
  Pallas kernels  127 us (79%)
  starting transfers between devices  21.2 us (13%)
  local copies, waits for them, and re-layouts  6.39 us (4%)
  waiting for transfers between devices  1.73 us (1%)
    pallas_call x1, Pallas kernels, call_near(): pl.pallas_call(near_kernel, out_shape=shape(targets, 128), in_specs=[SMEM...  45.6 us
    pallas_call x2, Pallas kernels, call_leaf(): pl.pallas_call(functools.partial(leaf_kernel, part), out_shape=shape(2, O...  32.3 us
    pallas_call x1, Pallas kernels, call_last(): pl.pallas_call(last_kernel, out_shape=(shape(PAIRS, 128), jax.ShapeDtypeS...  31 us
    pallas_call x1, Pallas kernels, call_turn(): pl.pallas_call(turn_kernel, out_shape=shape(CLASSES * OPROWS, 128), in_sp...  11.1 us
    ppermute x9, starting transfers between devices, sent_over(): lax.ppermute(block, axis, [(i, (i + s) % count) for i in range(count)])  8.82 us
    unnamed x18, local copies, waits for them, and re-layouts  6.39 us
    ppermute x1, starting transfers between devices, body(): behind = lax.ppermute(low, AXES, down)  5.29 us
    ppermute x1, starting transfers between devices, body(): before = lax.ppermute(high, AXES, up)  4.5 us
  transfers between devices with their start and end apart: 12, of which 1 were waited for; matrix products, arithmetic and copies ran while one was open for 0% of the time, Pallas kernels for 59%

profile of v2, /device:TPU:1, one launch (start us, length us, event | category | flops | bytes accessed | tf_op | source)
XLA Modules:
  0.0 157.2 jit_solution(6167174920200997169)
XLA Ops:
  0.0 0.0 copy-start.1
  0.0 0.9 copy-done.1
  1.0 0.0 copy-start.5
  1.0 0.7 copy-done.5
  1.6 3.8 %expand_own.1 = (f32[512,128]{1,0:T(8,128)S(1)}, f32[64,128]{1,0:T(8,128)S(1)}, f32[64,128]{1,0:T(8,128)S(1)}, f32[3,128,128]{2,1,0:T(8,128)S(1)}, f32[256,128]{...) custom-call(f32[512,128]{1,0:T(8,128)S(1)} %bitcast.20, ...), custom_call_target="tpu_custom_call" | custom-call | flops 1000000000 | bytes 10000000 | tf_op jit(solution)/shard_map/expand_own/pallas_call | solution.py:555
  5.4 4.5 %collective-permute-start.10 = (f32[64,128]{1,0:T(8,128)S(1)}, f32[64,128]{1,0:T(8,128)S(1)}, u32[]{:S(2)}, u32[]{:S(2)}) collective-permute-start(f32[64,128]{1,0:T(8,128)S(1)} %get-tuple-element.60), channel_id=1, source_target_pairs={{0,1},{1,2},{2,3},{3,4},{4,5},{5,6},{6,7},{7,8},{8,9},{9,10},{10,1... | collective-permute-start | bytes 98312 | tf_op jit(solution)/shard_map/ppermute | solution.py:712
  9.9 5.3 %collective-permute-start.11 = (f32[64,128]{1,0:T(8,128)S(1)}, f32[64,128]{1,0:T(8,128)S(1)}, u32[]{:S(2)}, u32[]{:S(2)}) collective-permute-start(f32[64,128]{1,0:T(8,128)S(1)} %get-tuple-element.61), channel_id=1, source_target_pairs={{1,0},{2,1},{3,2},{4,3},{5,4},{6,5},{7,6},{8,7},{9,8},{10,9},{11,1... | collective-permute-start | bytes 98312 | tf_op jit(solution)/shard_map/ppermute | solution.py:713
  15.2 0.0 collective-permute-start.7
  15.2 1.1 collective-permute-start.8
  16.3 1.6 %collective-permute-start.9 = (f32[56,128]{1,0:T(8,128)S(1)}, f32[56,128]{1,0:T(8,128)S(1)}, u32[]{:S(2)}, u32[]{:S(2)}) collective-permute-start(f32[56,128]{1,0:T(8,128)S(1)} %get-tuple-element.59.after_ref.refs_0_), channel_id=1, source_target_pairs={{0,24},{8,0},{16,8},{24,16},{1,25},{9,1},{17,9},{25,17},{2,26},{10... | collective-permute-start | bytes 86024 | tf_op jit(solution)/shard_map/ppermute | solution.py:693
  17.9 0.0 copy-start
  17.9 4.1 %copy-done = f32[316,81,81]{0,2,1:T(8,128)S(1)} copy-done((f32[316,81,81]{0,2,1:T(8,128)S(1)}, f32[316,81,81]{0,2,1:T(8,128)}, u32[]{:S(2)}) %copy-start) | copy-done | bytes 8293128
  22.0 11.1 %turn_operators.1.refs_4_.ops_ref = f32[27808,128]{1,0:T(8,128)} custom-call(f32[81,81,316]{2,1,0:T(8,128)S(1)} %bitcast.19, f32[56,128]{1,0:T(8,128)S(1)} %get-tuple-element.59.after_ref.refs_0_), custom_call_target="tpu_custom_call" | custom-call | flops 10000000 | bytes 30000000 | tf_op jit(solution)/shard_map/turn_operators/pallas_call | solution.py:575
  33.1 0.0 collective-permute-done.7.refs_1_
  33.1 0.0 collective-permute-done.8.refs_2_
  33.2 0.0 collective-permute-done.9.refs_3_
  33.2 0.0 collective-permute-done.10.refs_5_.before_ref
  33.2 0.0 collective-permute-done.11.refs_6_.behind_ref
  33.2 0.1 collective-permute-start.12
  33.3 1.0 collective-permute-start.13
  34.3 1.7 %collective-permute-start.14 = (f32[224,128]{1,0:T(8,128)S(1)}, f32[224,128]{1,0:T(8,128)S(1)}, u32[]{:S(2)}, u32[]{:S(2)}) collective-permute-start(f32[224,128]{1,0:T(8,128)S(1)} %join.3.after_ref.refs_0_), channel_id=1, source_target_pairs={{0,6},{2,0},{4,2},{6,4},{1,7},{3,1},{5,3},{7,5},{8,14},{10,8},{12,... | collective-permute-start | bytes 344072 | tf_op jit(solution)/shard_map/ppermute | solution.py:693
  36.0 0.0 copy-done.2
  36.0 45.6 %near.1.refs_4_.near_ref = f32[128,128]{1,0:T(8,128)S(1)} custom-call(s32[27,256]{1,0:T(8,128)S(1)} %bitcast.21, f32[512,128]{1,0:T(8,128)S(1)} %get-tuple-element.62.own_ref, f32[64,128]{1,0:T(8,128)S(1)} %collective-permute-done.10.refs_5_.before_ref, f32[64,128]{1,0:T(8,128)S(1)} %collective-permute-done.11.refs_6_.behind_ref, ...), custom_call_target="tpu_custom_call" | custom-call | flops 283115520 | bytes 30000000 | tf_op jit(solution)/shard_map/near/pallas_call | solution.py:601
  81.6 0.0 collective-permute-done.12.refs_1_
  81.6 0.0 collective-permute-done.13.refs_2_
  81.6 0.0 collective-permute-done.14.refs_3_
  81.7 2.2 %collective-permute-start.15 = (f32[896,128]{1,0:T(8,128)S(1)}, f32[896,128]{1,0:T(8,128)S(1)}, u32[]{:S(2)}, u32[]{:S(2)}) collective-permute-start(f32[896,128]{1,0:T(8,128)S(1)} %join.4.after_ref.refs_0_), channel_id=1, source_target_pairs={{0,1},{1,64},{64,65},{65,0},{2,3},{3,66},{66,67},{67,2},{4,5},{5,6... | collective-permute-start | bytes 1376264 | tf_op jit(solution)/shard_map/ppermute | solution.py:693
  83.9 0.7 collective-permute-start.16
  84.6 0.5 collective-permute-start.17
  85.1 0.0 copy-done.3
  85.1 0.0 copy-done.4
  85.1 1.5 expand_halo.1
  86.6 16.1 %leaf_translate.2.refs_4_.local_a_ref = f32[2,88,128]{2,1,0:T(8,128)S(1)} custom-call(s32[16,256]{1,0:T(8,128)S(1)} %get-tuple-element.64.code_ref, f32[27808,128]{1,0:T(8,128)} %turn_operators.1.refs_4_.ops_ref, f32[320,128]{1,0:T(8,128)S(1)} %get-tuple-element.65.rows_ref, f32[896,128]{1,0:T(8,128)S(1)} %join.4.after_ref.refs_0_), custom_call_target="tpu_custom_call" | custom-call | flops 214990848 | bytes 20000000 | tf_op jit(solution)/shard_map/leaf_translate/pallas_call | solution.py:638
  102.7 0.0 copy-start.7
  102.7 0.0 collective-permute-done.15.refs_1_
  102.7 0.0 collective-permute-done.16.refs_2_
  102.7 1.7 %collective-permute-done.17.refs_3_ = f32[896,128]{1,0:T(8,128)S(1)} collective-permute-done((f32[896,128]{1,0:T(8,128)S(1)}, f32[896,128]{1,0:T(8,128)S(1)}, u32[]{:S(2)}, u32[]{:S(2)}) %collective-permute-start.17) | collective-permute-done | bytes 458784 | tf_op jit(solution)/shard_map/ppermute | solution.py:693
  104.4 0.1 join.5.after_ref.mine_ref
  104.5 2.6 %collective-permute-start.18 = (f32[3584,128]{1,0:T(8,128)S(1)}, f32[3584,128]{1,0:T(8,128)S(1)}, u32[]{:S(2)}, u32[]{:S(2)}) collective-permute-start(f32[3584,128]{1,0:T(8,128)S(1)} %join.5.after_ref.mine_ref), channel_id=1, source_target_pairs={{0,32},{32,0},{1,33},{33,1},{2,34},{34,2},{3,35},{35,3},{4,36},{36... | collective-permute-start | bytes 5505032 | tf_op jit(solution)/shard_map/ppermute | solution.py:723
  107.1 0.0 copy-done.7
  107.1 1.5 fetch_lists.1.code_ref
  108.6 0.0 copy-start.6
  108.6 16.2 %leaf_translate.3.local_b_ref = f32[2,88,128]{2,1,0:T(8,128)S(1)} custom-call(s32[16,256]{1,0:T(8,128)S(1)} %get-tuple-element.64.code_ref, f32[27808,128]{1,0:T(8,128)} %turn_operators.1.refs_4_.ops_ref, f32[320,128]{1,0:T(8,128)S(1)} %get-tuple-element.65.rows_ref, f32[3584,128]{1,0:T(8,128)S(1)} %join.5.after_ref.mine_ref), custom_call_target="tpu_custom_call" | custom-call | flops 214990848 | bytes 20000000 | tf_op jit(solution)/shard_map/leaf_translate/pallas_call | solution.py:638
  124.8 0.0 collective-permute-done.18.other_ref
  124.8 0.0 copy-done.6
  124.9 31.0 %finish.1 = (f32[128,128]{1,0:T(8,128)S(1)}, s32[1]{0:T(128)}) custom-call(s32[256]{0:T(256)S(1)} %copy-done.7, s32[64,256]{1,0:T(8,128)S(1)} %fetch_lists.1.code_ref, f32[3584,128]{1,0:T(8,128)S(1)} %join.5.after_ref.mine_ref, f32[3584,128]{1,0:T(8,128)S(1)} %collective-permute-done.18.other_ref, f32[27808,128]{1,0:T(8,128)} %turn_operators.1.refs_4_.ops_ref, ...), custom_call_target="tpu_custom_call" | custom-call | tf_op jit(solution)/shard_map/finish/pallas_call | solution.py:668
  156.6 0.0 copy-start.8
  156.6 0.6 copy-done.8
  (6 shorter events, 0.1 us)
Async XLA Ops:
  0.0 0.9 copy-start.1
  1.0 0.7 copy-start.5
  5.4 27.7 %collective-permute-start.10 = (f32[64,128]{1,0:T(8,128)S(1)}, f32[64,128]{1,0:T(8,128)S(1)}, u32[]{:S(2)}, u32[]{:S(2)}) collective-permute-start(f32[64,128]{1,0:T(8,128)S(1)} %get-tuple-element.60), channel_id=1, source_target_pairs={{0,1},{1,2},{2,3},{3,4},{4,5},{5,6},{6,7},{7,8},{8,9},{9,10},{10,1... | collective-permute-start | bytes 98312 | tf_op jit(solution)/shard_map/ppermute | solution.py:712
  9.9 23.3 %collective-permute-start.11 = (f32[64,128]{1,0:T(8,128)S(1)}, f32[64,128]{1,0:T(8,128)S(1)}, u32[]{:S(2)}, u32[]{:S(2)}) collective-permute-start(f32[64,128]{1,0:T(8,128)S(1)} %get-tuple-element.61), channel_id=1, source_target_pairs={{1,0},{2,1},{3,2},{4,3},{5,4},{6,5},{7,6},{8,7},{9,8},{10,9},{11,1... | collective-permute-start | bytes 98312 | tf_op jit(solution)/shard_map/ppermute | solution.py:713
  15.2 17.9 %collective-permute-start.7 = (f32[56,128]{1,0:T(8,128)S(1)}, f32[56,128]{1,0:T(8,128)S(1)}, u32[]{:S(2)}, u32[]{:S(2)}) collective-permute-start(f32[56,128]{1,0:T(8,128)S(1)} %get-tuple-element.59.after_ref.refs_0_), channel_id=1, source_target_pairs={{0,8},{8,16},{16,24},{24,0},{1,9},{9,17},{17,25},{25,1},{2,10},{10... | collective-permute-start | bytes 86024 | tf_op jit(solution)/shard_map/ppermute | solution.py:693
  15.2 17.9 %collective-permute-start.8 = (f32[56,128]{1,0:T(8,128)S(1)}, f32[56,128]{1,0:T(8,128)S(1)}, u32[]{:S(2)}, u32[]{:S(2)}) collective-permute-start(f32[56,128]{1,0:T(8,128)S(1)} %get-tuple-element.59.after_ref.refs_0_), channel_id=1, source_target_pairs={{0,16},{8,24},{16,0},{24,8},{1,17},{9,25},{17,1},{25,9},{2,18},{10... | collective-permute-start | bytes 86024 | tf_op jit(solution)/shard_map/ppermute | solution.py:693
  16.3 16.9 %collective-permute-start.9 = (f32[56,128]{1,0:T(8,128)S(1)}, f32[56,128]{1,0:T(8,128)S(1)}, u32[]{:S(2)}, u32[]{:S(2)}) collective-permute-start(f32[56,128]{1,0:T(8,128)S(1)} %get-tuple-element.59.after_ref.refs_0_), channel_id=1, source_target_pairs={{0,24},{8,0},{16,8},{24,16},{1,25},{9,1},{17,9},{25,17},{2,26},{10... | collective-permute-start | bytes 86024 | tf_op jit(solution)/shard_map/ppermute | solution.py:693
  17.9 4.1 %copy-start = (f32[316,81,81]{0,2,1:T(8,128)S(1)}, f32[316,81,81]{0,2,1:T(8,128)}, u32[]{:S(2)}) copy-start(f32[316,81,81]{0,2,1:T(8,128)} %param.20) | copy-start | bytes 24879316
  33.1 2.8 %copy-start.2 = (s32[256,27]{0,1:T(8,128)S(1)}, s32[256,27]{0,1:T(8,128)}, u32[]{:S(2)}) copy-start(s32[256,27]{0,1:T(8,128)} %param.15) | copy-start | bytes 82948
  33.1 52.0 %copy-start.3 = (s32[256,16]{0,1:T(8,128)S(1)}, s32[256,16]{0,1:T(8,128)}, u32[]{:S(2)}) copy-start(s32[256,16]{0,1:T(8,128)} %param.16) | copy-start | bytes 49156
  33.1 52.0 %copy-start.4 = (s32[256,16]{0,1:T(8,128)S(1)}, s32[256,16]{0,1:T(8,128)}, u32[]{:S(2)}) copy-start(s32[256,16]{0,1:T(8,128)} %param.17) | copy-start | bytes 49156
  33.2 48.4 %collective-permute-start.12 = (f32[224,128]{1,0:T(8,128)S(1)}, f32[224,128]{1,0:T(8,128)S(1)}, u32[]{:S(2)}, u32[]{:S(2)}) collective-permute-start(f32[224,128]{1,0:T(8,128)S(1)} %join.3.after_ref.refs_0_), channel_id=1, source_target_pairs={{0,2},{2,4},{4,6},{6,0},{1,3},{3,5},{5,7},{7,1},{8,10},{10,12},{12... | collective-permute-start | bytes 344072 | tf_op jit(solution)/shard_map/ppermute | solution.py:693
  33.3 48.3 %collective-permute-start.13 = (f32[224,128]{1,0:T(8,128)S(1)}, f32[224,128]{1,0:T(8,128)S(1)}, u32[]{:S(2)}, u32[]{:S(2)}) collective-permute-start(f32[224,128]{1,0:T(8,128)S(1)} %join.3.after_ref.refs_0_), channel_id=1, source_target_pairs={{0,4},{2,6},{4,0},{6,2},{1,5},{3,7},{5,1},{7,3},{8,12},{10,14},{12... | collective-permute-start | bytes 344072 | tf_op jit(solution)/shard_map/ppermute | solution.py:693
  34.3 47.3 %collective-permute-start.14 = (f32[224,128]{1,0:T(8,128)S(1)}, f32[224,128]{1,0:T(8,128)S(1)}, u32[]{:S(2)}, u32[]{:S(2)}) collective-permute-start(f32[224,128]{1,0:T(8,128)S(1)} %join.3.after_ref.refs_0_), channel_id=1, source_target_pairs={{0,6},{2,0},{4,2},{6,4},{1,7},{3,1},{5,3},{7,5},{8,14},{10,8},{12,... | collective-permute-start | bytes 344072 | tf_op jit(solution)/shard_map/ppermute | solution.py:693
  81.7 21.0 %collective-permute-start.15 = (f32[896,128]{1,0:T(8,128)S(1)}, f32[896,128]{1,0:T(8,128)S(1)}, u32[]{:S(2)}, u32[]{:S(2)}) collective-permute-start(f32[896,128]{1,0:T(8,128)S(1)} %join.4.after_ref.refs_0_), channel_id=1, source_target_pairs={{0,1},{1,64},{64,65},{65,0},{2,3},{3,66},{66,67},{67,2},{4,5},{5,6... | collective-permute-start | bytes 1376264 | tf_op jit(solution)/shard_map/ppermute | solution.py:693
  83.9 18.8 %collective-permute-start.16 = (f32[896,128]{1,0:T(8,128)S(1)}, f32[896,128]{1,0:T(8,128)S(1)}, u32[]{:S(2)}, u32[]{:S(2)}) collective-permute-start(f32[896,128]{1,0:T(8,128)S(1)} %join.4.after_ref.refs_0_), channel_id=1, source_target_pairs={{0,64},{1,65},{64,0},{65,1},{2,66},{3,67},{66,2},{67,3},{4,68},{5,... | collective-permute-start | bytes 1376264 | tf_op jit(solution)/shard_map/ppermute | solution.py:693
  84.6 19.8 %collective-permute-start.17 = (f32[896,128]{1,0:T(8,128)S(1)}, f32[896,128]{1,0:T(8,128)S(1)}, u32[]{:S(2)}, u32[]{:S(2)}) collective-permute-start(f32[896,128]{1,0:T(8,128)S(1)} %join.4.after_ref.refs_0_), channel_id=1, source_target_pairs={{0,65},{1,0},{64,1},{65,64},{2,67},{3,2},{66,3},{67,66},{4,69},{5,... | collective-permute-start | bytes 1376264 | tf_op jit(solution)/shard_map/ppermute | solution.py:693
  102.7 4.4 %copy-start.7 = (s32[256]{0:T(256)S(1)}, s32[256]{0:T(256)}, u32[]{:S(2)}) copy-start(s32[256]{0:T(256)} %top_ref.5) | copy-start | bytes 3076
  104.5 20.3 %collective-permute-start.18 = (f32[3584,128]{1,0:T(8,128)S(1)}, f32[3584,128]{1,0:T(8,128)S(1)}, u32[]{:S(2)}, u32[]{:S(2)}) collective-permute-start(f32[3584,128]{1,0:T(8,128)S(1)} %join.5.after_ref.mine_ref), channel_id=1, source_target_pairs={{0,32},{32,0},{1,33},{33,1},{2,34},{34,2},{3,35},{35,3},{4,36},{36... | collective-permute-start | bytes 5505032 | tf_op jit(solution)/shard_map/ppermute | solution.py:723
  108.6 16.3 %copy-start.6 = (f32[8,81,81]{2,0,1:T(8,128)S(1)}, f32[8,81,81]{2,0,1:T(8,128)}, u32[]{:S(2)}) copy-start(f32[8,81,81]{2,0,1:T(8,128)} %param.21) | copy-start | bytes 629860
  156.6 0.6 copy-start.8

commit v3 on v2

--- a/solution.py
+++ b/solution.py
@@ -19,7 +19,7 @@
 LLIST = 16
 TLIST = 64
 TOPBOX = 4096
-ROW_BITS = 12
+ROW_BITS = 13
 CLASSES = 316
 OPROWS = 88
 SOFTENING = 0.01
@@ -414,7 +414,9 @@
         copy.start()
     for copy in copies:
         copy.wait()
-    code_ref[...] = pack_codes(class_vmem[...], list_vmem[...])
+    codes = pack_codes(class_vmem[...], list_vmem[...])
+    shift = top_ref[0] - window_start(top_ref)
+    code_ref[...] = pltpu.roll(codes, (TOP_WINDOW - shift) % TOP_WINDOW, 1)[:, :128]
 
 
 def window_start(top_ref):
@@ -422,7 +424,7 @@
 
 
 def finish(
-    cap, begin, top_ref, code_ref, table_ref, ops_ref, m2m_ref, tops_ref, local_refs, dist_ref,
+    cap, shift, top_ref, code_ref, table_ref, ops_ref, m2m_ref, tops_ref, local_refs, dist_ref,
     near_ref, mask_ref, out_ref, field_ref, pot_ref, total_ref, wide_ref, rows_ref,
 ):
     first = top_ref[0]
@@ -435,7 +437,7 @@
 
         def step(b, carry):
             put_sums(total_ref, wide_ref, b - 1)
-            column = first - begin + block * width + b
+            column = shift + block * width + b
             total_ref[...] = gather_products(
                 [code_ref[k, column] for k in range(TLIST)], ops_ref, table_ref
             )
@@ -476,44 +478,56 @@
 
 def last_kernel(
     top_ref, code_ref, mine_ref, other_ref, ops_ref, m2m_ref, tops_ref, local_a_ref, local_b_ref,
-    dist_ref, near_ref, mask_ref, out_ref, over_ref, table_ref, *scratch,
+    dist_ref, near_ref, mask_ref, out_ref, over_ref,
+    table_ref, rest_ref, meta_ref, ends_ref, packed_ref, scalar_ref, sems, *scratch,
 ):
+    half = mine_ref.shape[0]
+    blocks = half // SEND
+    table_ref[:half] = mine_ref[...]
+    table_ref[half:] = other_ref[...]
+    heads = pl.ds(0, 2 * blocks, stride=SEND)
+    turned = table_ref[heads, :].T[120:]
+    meta_ref[...] = turned.astype(jnp.int32)
+    copy = pltpu.make_async_copy(meta_ref, ends_ref, sems.at[0])
+    copy.start()
+    most = jnp.max(turned[6:7] - turned[7:8]).astype(jnp.int32) + 1
+    over_ref[0] = most
     core, my_y, my_x = lax.axis_index("core"), lax.axis_index("y"), lax.axis_index("x")
     my_z = lax.axis_index(("zlo", "zhi"))
-    table_ref[0:1, :] = jnp.zeros((1, 128), jnp.float32)
-    over_ref[0] = 0
-
-    def assemble(ref, zlo):
-        def step(i, carry):
-            y, x, zhi = i // 8, (i // 2) % 4, i % 2
-            block = ((my_z - (zlo * 2 + zhi)) & 3) * 16 + ((my_x - x) & 3) * 4 + ((my_y - y) & 3)
-            at = pl.multiple_of(block * SEND, 8)
-            ends = ref[pl.ds(at, 1), :]
-            begin = ends[0, 127].astype(jnp.int32)
-            end = ends[0, 126].astype(jnp.int32)
-            over_ref[0] = jnp.maximum(over_ref[0], end - begin + 1)
-            so_far = table_ref[pl.ds(begin, 1), :]
-            table_ref[pl.ds(begin, SEND), :] = ref[pl.ds(at, SEND), :]
-            table_ref[pl.ds(begin, 1), :] = ends + so_far
-            return carry
-
-        lax.fori_loop(0, 32, step, 0)
-
-    for zlo in range(2):
-        for side in range(2):
-
-            @pl.when(core == side)
-            def _():
-                assemble(mine_ref, zlo)
-
-            @pl.when(core != side)
-            def _():
-                assemble(other_ref, zlo)
-
-    @pl.when(over_ref[0] < SEND)
+    by_z = [((my_z - z) & 3) * 16 for z in range(4)]
+    by_x = [((my_x - x) & 3) * 4 for x in range(4)]
+    by_y = [(my_y - y) & 3 for y in range(4)]
+    by_core = [blocks * (core ^ side) for side in range(2)]
+    order = [
+        by_z[zlo * 2 + zhi] + by_x[x] + by_y[y] + by_core[side]
+        for zlo in range(2) for side in range(2) for y in range(4) for x in range(4)
+        for zhi in range(2)
+    ]
+    copy.wait()
+
+    @pl.when(most < SEND)
     def _():
+        code = code_ref[...]
+        box = code & ((1 << ROW_BITS) - 1)
+        row = code
+        last, last_begin = 0, 0
+        rest_ref[pl.ds(order[0], 1), :] = jnp.zeros((1, 128), jnp.float32)
+        for d, block in enumerate(order):
+            begin = ends_ref[7, block]
+            base = block * SEND
+            if d:
+                rest_ref[pl.ds(block, 1), :] = table_ref[pl.ds(last + begin - last_begin, 1), :]
+                row += jnp.where(box >= begin, base - begin - last + last_begin, 0)
+            else:
+                row += base - begin
+            last, last_begin = base, begin
+        packed_ref[...] = row
+        copy = pltpu.make_async_copy(packed_ref, scalar_ref, sems.at[1])
+        copy.start()
+        table_ref[heads, :] += rest_ref[...]
+        copy.wait()
         finish(
-            64, window_start(top_ref), top_ref, code_ref, table_ref, ops_ref, m2m_ref, tops_ref,
+            64, 0, top_ref, scalar_ref, table_ref, ops_ref, m2m_ref, tops_ref,
             (local_a_ref, local_b_ref), dist_ref, near_ref, mask_ref, out_ref, *scratch,
         )
 
@@ -523,7 +537,7 @@
     dist_ref, near_ref, mask_ref, out_ref, *scratch,
 ):
     finish(
-        LEAVES, jnp.minimum(top_ref[0], TOPBOX - LEAVES), top_ref, code_ref, table_ref, ops_ref, m2m_ref, tops_ref,
+        LEAVES, top_ref[0] - jnp.minimum(top_ref[0], TOPBOX - LEAVES), top_ref, code_ref, table_ref, ops_ref, m2m_ref, tops_ref,
         (local_a_ref, local_b_ref), dist_ref, near_ref, mask_ref, out_ref, *scratch,
     )
 
@@ -577,7 +591,7 @@
         out_shape=shape(CLASSES * OPROWS, 128),
         in_specs=[VMEM, ANY],
         out_specs=VMEM,
-        compiler_params=pltpu.CompilerParams(vmem_limit_bytes=30 * MIB),
+        compiler_params=pltpu.CompilerParams(vmem_limit_bytes=26 * MIB),
         cost_estimate=cost(10**7, 3 * 10**7),
         name="turn_operators",
     )(ops, after)
@@ -610,7 +624,7 @@
             pltpu.VMEM((width * 128, 128), jnp.bfloat16),
             pltpu.VMEM((width * 128, 128), F32),
         ],
-        compiler_params=pltpu.CompilerParams(vmem_limit_bytes=30 * MIB),
+        compiler_params=pltpu.CompilerParams(vmem_limit_bytes=24 * MIB),
         cost_estimate=cost(10 * targets * 2 * 64 * NEAR * 64, 3 * 10**7),
         name="near",
     )(near, own, before, behind, after)
@@ -641,7 +655,7 @@
         in_specs=[SMEM, VMEM, VMEM, ANY],
         out_specs=VMEM,
         scratch_shapes=[pltpu.VMEM((LEAF_STEP, OPROWS, 128), F32)],
-        compiler_params=pltpu.CompilerParams(vmem_limit_bytes=24 * MIB),
+        compiler_params=pltpu.CompilerParams(vmem_limit_bytes=17 * MIB),
         cost_estimate=cost(LEAVES * LLIST * COEF * COEF * 8, 2 * 10**7),
         name="leaf_translate",
     )(code, ops, rows, after)
@@ -651,7 +665,7 @@
     window = (TLIST, TOP_WINDOW)
     return pl.pallas_call(
         fetch_kernel,
-        out_shape=jax.ShapeDtypeStruct(window, jnp.int32),
+        out_shape=jax.ShapeDtypeStruct((TLIST, 128), jnp.int32),
         in_specs=[SMEM, ANY, ANY],
         out_specs=VMEM,
         scratch_shapes=[
@@ -668,10 +682,18 @@
     return pl.pallas_call(
         last_kernel,
         out_shape=(shape(PAIRS, 128), jax.ShapeDtypeStruct((1,), jnp.int32)),
-        in_specs=[SMEM, SMEM] + [VMEM] * 10,
+        in_specs=[SMEM] + [VMEM] * 11,
         out_specs=(VMEM, SMEM),
-        scratch_shapes=[pltpu.VMEM((TOPBOX + SEND, 128), F32)] + FINISH_SCRATCH,
-        compiler_params=pltpu.CompilerParams(vmem_limit_bytes=32 * MIB),
+        scratch_shapes=[
+            pltpu.VMEM((2 * mine.shape[0], 128), F32),
+            pltpu.VMEM((2 * mine.shape[0] // SEND, 128), F32),
+            pltpu.VMEM((8, 128), jnp.int32),
+            pltpu.SMEM((8, 128), jnp.int32),
+            pltpu.VMEM((TLIST, 128), jnp.int32),
+            pltpu.SMEM((TLIST, 128), jnp.int32),
+            pltpu.SemaphoreType.DMA((2,)),
+        ] + FINISH_SCRATCH,
+        compiler_params=pltpu.CompilerParams(vmem_limit_bytes=24 * MIB),
         name="finish",
     )(leaf_top, code, mine, other, *rest)
 
@@ -683,7 +705,7 @@
         in_specs=[SMEM, SMEM] + [VMEM] * 9,
         out_specs=VMEM,
         scratch_shapes=FINISH_SCRATCH,
-        compiler_params=pltpu.CompilerParams(vmem_limit_bytes=32 * MIB),
+        compiler_params=pltpu.CompilerParams(vmem_limit_bytes=24 * MIB),
         name="finish_spare",
     )(leaf_top, code, table, *rest)
 
@@ -714,12 +736,12 @@
     ops = call_turn(m2l_ops.transpose(1, 2, 0), send)
     by_y = call_join(over_y, ops, before, behind)
     over_x = sent_over(by_y, "x", 4)
-    near = call_near(near_list.T, own, before, behind, by_y)
-    by_x = call_join(over_x, near)
+    code, rows = call_halo(leaf_list.T, leaf_class.T, moments, before, behind)
+    local_a = call_leaf(0, code, ops, rows, by_y)
+    by_x = call_join(over_x, local_a)
     over_z = sent_over(by_x, ("zlo", "zhi"), 4)
-    code, rows = call_halo(leaf_list.T, leaf_class.T, moments, before, behind)
-    local_a = call_leaf(0, code, ops, rows, by_x)
-    mine = call_join(over_z, local_a)
+    near = call_near(near_list.T, own, before, behind, by_x)
+    mine = call_join(over_z, near)
     other = lax.ppermute(mine, "core", [(0, 1), (1, 0)])
     local_b = call_leaf(1, code, ops, rows, mine)
     top_code = call_fetch(leaf_top, top_list.T, top_class.T)
@@ -737,7 +759,8 @@
         lists, classes = (
             lax.dynamic_slice_in_dim(x, start, LEAVES, axis=0).T for x in (top_list, top_class)
         )
-        return call_spare(leaf_top, pack_codes(classes, lists), table, *rest)
+        again = call_turn(m2l_ops.transpose(1, 2, 0), table)
+        return call_spare(leaf_top, pack_codes(classes, lists), table, again, *rest[1:])
 
     result = lax.cond(over[0] >= SEND, spare, lambda: result)
     return result.reshape(-1)

time: 160 us -> 129 us (0.81); the launches traced: 157 us -> 130 us
  Pallas kernels: 127 us -> 104 us
  local copies, waits for them, and re-layouts: 6.39 us -> 2.28 us
  waiting for transfers between devices: 1.73 us -> 0.03 us
    pallas_call x1, Pallas kernels: 31 us -> 17.5 us  [call_last(): pl.pallas_call(last_kernel, out_shape=(shape(PAIRS, 128), jax.ShapeDtypeS...]
    pallas_call x2, Pallas kernels: 32.3 us -> 23.9 us  [call_leaf(): pl.pallas_call(functools.partial(leaf_kernel, part), out_shape=shape(2, O...]
    unnamed x18 -> x16, local copies, waits for them, and re-layouts: 6.39 us -> 2.28 us
    ppermute x9, waiting for transfers between devices: 1.72 us -> 0.02 us  [sent_over(): lax.ppermute(block, axis, [(i, (i + s) % count) for i in range(count)])]
  transfers between devices with their start and end apart: 12 -> 12, of which waited for: 1 -> 0; matrix products, arithmetic and copies ran while one was open for 0% -> 0% of each run, Pallas kernels for 59% -> 64%
where the time goes in v3:
time: 129 us; the launch traced here: 130 us
  Pallas kernels  104 us (81%)
  starting transfers between devices  22.4 us (17%)
  local copies, waits for them, and re-layouts  2.28 us (2%)
    pallas_call x1, Pallas kernels, call_near(): pl.pallas_call(near_kernel, out_shape=shape(targets, 128), in_specs=[SMEM...  45.6 us
    pallas_call x2, Pallas kernels, call_leaf(): pl.pallas_call(functools.partial(leaf_kernel, part), out_shape=shape(2, O...  23.9 us
    pallas_call x1, Pallas kernels, call_last(): pl.pallas_call(last_kernel, out_shape=(shape(PAIRS, 128), jax.ShapeDtypeS...  17.5 us
    pallas_call x1, Pallas kernels, call_turn(): pl.pallas_call(turn_kernel, out_shape=shape(CLASSES * OPROWS, 128), in_sp...  10.2 us
    ppermute x9, starting transfers between devices, sent_over(): lax.ppermute(block, axis, [(i, (i + s) % count) for i in range(count)])  8.6 us
    ppermute x1, starting transfers between devices, body(): behind = lax.ppermute(low, AXES, down)  5.29 us
    ppermute x1, starting transfers between devices, body(): before = lax.ppermute(high, AXES, up)  4.49 us
    ppermute x1, starting transfers between devices, body(): other = lax.ppermute(mine, 'core', [(0, 1), (1, 0)])  4.02 us
  transfers between devices with their start and end apart: 12, of which 0 were waited for; matrix products, arithmetic and copies ran while one was open for 0% of the time, Pallas kernels for 64%

profile of v3, /device:TPU:1, one launch (start us, length us, event | category | flops | bytes accessed | tf_op | source)
XLA Modules:
  0.0 129.8 jit_solution(18330453939911383480)
XLA Ops:
  0.0 0.0 copy-start
  0.0 0.9 copy-done
  1.0 0.7 copy-done.4
  1.6 3.8 %expand_own.1 = (f32[512,128]{1,0:T(8,128)S(1)}, f32[64,128]{1,0:T(8,128)S(1)}, f32[64,128]{1,0:T(8,128)S(1)}, f32[3,128,128]{2,1,0:T(8,128)S(1)}, f32[256,128]{...) custom-call(f32[512,128]{1,0:T(8,128)S(1)} %bitcast.20, ...), custom_call_target="tpu_custom_call" | custom-call | flops 1000000000 | bytes 10000000 | tf_op jit(solution)/shard_map/expand_own/pallas_call | solution.py:569
  5.4 4.5 %collective-permute-start.10 = (f32[64,128]{1,0:T(8,128)S(1)}, f32[64,128]{1,0:T(8,128)S(1)}, u32[]{:S(2)}, u32[]{:S(2)}) collective-permute-start(f32[64,128]{1,0:T(8,128)S(1)} %get-tuple-element.60), channel_id=1, source_target_pairs={{0,1},{1,2},{2,3},{3,4},{4,5},{5,6},{6,7},{7,8},{8,9},{9,10},{10,1... | collective-permute-start | bytes 98312 | tf_op jit(solution)/shard_map/ppermute | solution.py:734
  9.9 5.3 %collective-permute-start.11 = (f32[64,128]{1,0:T(8,128)S(1)}, f32[64,128]{1,0:T(8,128)S(1)}, u32[]{:S(2)}, u32[]{:S(2)}) collective-permute-start(f32[64,128]{1,0:T(8,128)S(1)} %get-tuple-element.61), channel_id=1, source_target_pairs={{1,0},{2,1},{3,2},{4,3},{5,4},{6,5},{7,6},{8,7},{9,8},{10,9},{11,1... | collective-permute-start | bytes 98312 | tf_op jit(solution)/shard_map/ppermute | solution.py:735
  15.2 0.0 collective-permute-start.7
  15.2 1.1 collective-permute-start.8
  16.3 1.6 %collective-permute-start.9 = (f32[56,128]{1,0:T(8,128)S(1)}, f32[56,128]{1,0:T(8,128)S(1)}, u32[]{:S(2)}, u32[]{:S(2)}) collective-permute-start(f32[56,128]{1,0:T(8,128)S(1)} %get-tuple-element.59.after_ref.refs_0_), channel_id=1, source_target_pairs={{0,24},{8,0},{16,8},{24,16},{1,25},{9,1},{17,9},{25,17},{2,26},{10... | collective-permute-start | bytes 86024 | tf_op jit(solution)/shard_map/ppermute | solution.py:715
  17.9 10.2 %turn_operators.3.refs_4_.ops_ref = f32[27808,128]{1,0:T(8,128)S(1)} custom-call(f32[81,81,316]{2,1,0:T(8,128)} %bitcast.24, f32[56,128]{1,0:T(8,128)S(1)} %get-tuple-element.59.after_ref.refs_0_), custom_call_target="tpu_custom_call" | custom-call | flops 10000000 | bytes 30000000 | tf_op jit(solution)/shard_map/turn_operators/pallas_call | solution.py:589
  28.1 0.0 copy-start.2
  28.1 0.0 copy-start.3
  28.1 0.0 collective-permute-done.7.refs_1_
  28.1 0.0 collective-permute-done.8.refs_2_
  28.1 0.0 collective-permute-done.9.refs_3_
  28.1 0.0 collective-permute-done.10.refs_5_.before_ref
  28.1 0.0 collective-permute-done.11.refs_6_.behind_ref
  28.2 0.1 collective-permute-start.12
  28.2 1.0 collective-permute-start.13
  29.3 1.7 %collective-permute-start.14 = (f32[224,128]{1,0:T(8,128)S(1)}, f32[224,128]{1,0:T(8,128)S(1)}, u32[]{:S(2)}, u32[]{:S(2)}) collective-permute-start(f32[224,128]{1,0:T(8,128)S(1)} %join.3.after_ref.refs_0_), channel_id=1, source_target_pairs={{0,6},{2,0},{4,2},{6,4},{1,7},{3,1},{5,3},{7,5},{8,14},{10,8},{12,... | collective-permute-start | bytes 344072 | tf_op jit(solution)/shard_map/ppermute | solution.py:715
  30.9 0.0 copy-done.2
  30.9 0.0 copy-done.3
  30.9 1.5 %expand_halo.1 = (s32[16,256]{1,0:T(8,128)S(1)}, f32[320,128]{1,0:T(8,128)S(1)}) custom-call(s32[16,256]{1,0:T(8,128)S(1)} %bitcast.22, s32[16,256]{1,0:T(8,128)S(1)} %bitcast.23, f32[256,128]{1,0:T(8,128)S(1)} %get-tuple-element.62.moment_ref, f32[64,128]{1,0:T(8,128)S(1)} %collective-permute-done.10.refs_5_.before_ref, ...), custom_call_target="tpu_custom_call" | custom-call | flops 100000000 | bytes 1000000 | tf_op jit(solution)/shard_map/expand_halo/pallas_call | solution.py:634
  32.4 0.0 copy-start.1
  32.4 11.8 %leaf_translate.2.refs_4_.local_a_ref = f32[2,88,128]{2,1,0:T(8,128)S(1)} custom-call(s32[16,256]{1,0:T(8,128)S(1)} %get-tuple-element.63.code_ref, f32[27808,128]{1,0:T(8,128)S(1)} %turn_operators.3.refs_4_.ops_ref, f32[320,128]{1,0:T(8,128)S(1)} %get-tuple-element.64.rows_ref, f32[224,128]{1,0:T(8,128)S(1)} %join.3.after_ref.refs_0_), custom_call_target="tpu_custom_call" | custom-call | flops 214990848 | bytes 20000000 | tf_op jit(solution)/shard_map/leaf_translate/pallas_call | solution.py:652
  44.2 0.0 collective-permute-done.12.refs_1_
  44.3 0.0 collective-permute-done.13.refs_2_
  44.3 0.0 collective-permute-done.14.refs_3_
  44.3 2.2 %collective-permute-start.15 = (f32[896,128]{1,0:T(8,128)S(1)}, f32[896,128]{1,0:T(8,128)S(1)}, u32[]{:S(2)}, u32[]{:S(2)}) collective-permute-start(f32[896,128]{1,0:T(8,128)S(1)} %join.4.after_ref.refs_0_), channel_id=1, source_target_pairs={{0,1},{1,64},{64,65},{65,0},{2,3},{3,66},{66,67},{67,2},{4,5},{5,6... | collective-permute-start | bytes 1376264 | tf_op jit(solution)/shard_map/ppermute | solution.py:715
  46.5 0.7 collective-permute-start.16
  47.2 0.3 collective-permute-start.17
  47.5 0.0 copy-done.1
  47.5 0.0 copy-start.6
  47.5 45.6 %near.1.refs_4_.near_ref = f32[128,128]{1,0:T(8,128)S(1)} custom-call(s32[27,256]{1,0:T(8,128)S(1)} %bitcast.21, f32[512,128]{1,0:T(8,128)S(1)} %get-tuple-element.65.own_ref, f32[64,128]{1,0:T(8,128)S(1)} %collective-permute-done.10.refs_5_.before_ref, f32[64,128]{1,0:T(8,128)S(1)} %collective-permute-done.11.refs_6_.behind_ref, ...), custom_call_target="tpu_custom_call" | custom-call | flops 283115520 | bytes 30000000 | tf_op jit(solution)/shard_map/near/pallas_call | solution.py:615
  93.2 0.0 collective-permute-done.15.refs_1_
  93.2 0.0 collective-permute-done.16.refs_2_
  93.2 0.0 collective-permute-done.17.refs_3_
  93.2 0.1 join.5.after_ref.mine_ref
  93.3 4.0 %collective-permute-start.18 = (f32[3584,128]{1,0:T(8,128)S(1)}, f32[3584,128]{1,0:T(8,128)S(1)}, u32[]{:S(2)}, u32[]{:S(2)}) collective-permute-start(f32[3584,128]{1,0:T(8,128)S(1)} %join.5.after_ref.mine_ref), channel_id=1, source_target_pairs={{0,32},{32,0},{1,33},{33,1},{2,34},{34,2},{3,35},{35,3},{4,36},{36... | collective-permute-start | bytes 5505032 | tf_op jit(solution)/shard_map/ppermute | solution.py:745
  97.3 0.0 copy-done.6
  97.3 1.5 %fetch_lists.1.code_ref = s32[64,128]{1,0:T(8,128)S(1)} custom-call(s32[256]{0:T(256)S(1)} %copy-done.6, s32[64,4096]{1,0:T(8,128)} %bitcast.5.list_ref, s32[64,4096]{1,0:T(8,128)} %bitcast.6.class_ref), custom_call_target="tpu_custom_call" | custom-call | flops 100000 | bytes 100000 | tf_op jit(solution)/shard_map/fetch_lists/pallas_call | solution.py:666
  98.9 0.0 copy-start.5
  98.9 12.0 %leaf_translate.3.local_b_ref = f32[2,88,128]{2,1,0:T(8,128)S(1)} custom-call(s32[16,256]{1,0:T(8,128)S(1)} %get-tuple-element.63.code_ref, f32[27808,128]{1,0:T(8,128)S(1)} %turn_operators.3.refs_4_.ops_ref, f32[320,128]{1,0:T(8,128)S(1)} %get-tuple-element.64.rows_ref, f32[3584,128]{1,0:T(8,128)S(1)} %join.5.after_ref.mine_ref), custom_call_target="tpu_custom_call" | custom-call | flops 214990848 | bytes 20000000 | tf_op jit(solution)/shard_map/leaf_translate/pallas_call | solution.py:652
  110.9 0.0 collective-permute-done.18.other_ref
  110.9 0.0 copy-done.5
  111.0 17.5 %finish.1 = (f32[128,128]{1,0:T(8,128)S(1)}, s32[1]{0:T(128)}) custom-call(s32[256]{0:T(256)S(1)} %copy-done.6, s32[64,128]{1,0:T(8,128)S(1)} %fetch_lists.1.code_ref, f32[3584,128]{1,0:T(8,128)S(1)} %join.5.after_ref.mine_ref, f32[3584,128]{1,0:T(8,128)S(1)} %collective-permute-done.18.other_ref, f32[27808,128]{1,0:T(8,128)S(1)} %turn_operators.3.refs_4_.ops_ref, ...), custom_call_target="tpu_custom_call" | custom-call | tf_op jit(solution)/shard_map/finish/pallas_call | solution.py:682
  129.2 0.0 copy-start.7
  129.2 0.6 copy-done.7
  (4 shorter events, 0.1 us)
Async XLA Ops:
  0.0 0.9 copy-start
  1.0 0.7 copy-start.4
  5.4 22.7 %collective-permute-start.10 = (f32[64,128]{1,0:T(8,128)S(1)}, f32[64,128]{1,0:T(8,128)S(1)}, u32[]{:S(2)}, u32[]{:S(2)}) collective-permute-start(f32[64,128]{1,0:T(8,128)S(1)} %get-tuple-element.60), channel_id=1, source_target_pairs={{0,1},{1,2},{2,3},{3,4},{4,5},{5,6},{6,7},{7,8},{8,9},{9,10},{10,1... | collective-permute-start | bytes 98312 | tf_op jit(solution)/shard_map/ppermute | solution.py:734
  9.9 18.2 %collective-permute-start.11 = (f32[64,128]{1,0:T(8,128)S(1)}, f32[64,128]{1,0:T(8,128)S(1)}, u32[]{:S(2)}, u32[]{:S(2)}) collective-permute-start(f32[64,128]{1,0:T(8,128)S(1)} %get-tuple-element.61), channel_id=1, source_target_pairs={{1,0},{2,1},{3,2},{4,3},{5,4},{6,5},{7,6},{8,7},{9,8},{10,9},{11,1... | collective-permute-start | bytes 98312 | tf_op jit(solution)/shard_map/ppermute | solution.py:735
  15.2 12.9 %collective-permute-start.7 = (f32[56,128]{1,0:T(8,128)S(1)}, f32[56,128]{1,0:T(8,128)S(1)}, u32[]{:S(2)}, u32[]{:S(2)}) collective-permute-start(f32[56,128]{1,0:T(8,128)S(1)} %get-tuple-element.59.after_ref.refs_0_), channel_id=1, source_target_pairs={{0,8},{8,16},{16,24},{24,0},{1,9},{9,17},{17,25},{25,1},{2,10},{10... | collective-permute-start | bytes 86024 | tf_op jit(solution)/shard_map/ppermute | solution.py:715
  15.2 12.9 %collective-permute-start.8 = (f32[56,128]{1,0:T(8,128)S(1)}, f32[56,128]{1,0:T(8,128)S(1)}, u32[]{:S(2)}, u32[]{:S(2)}) collective-permute-start(f32[56,128]{1,0:T(8,128)S(1)} %get-tuple-element.59.after_ref.refs_0_), channel_id=1, source_target_pairs={{0,16},{8,24},{16,0},{24,8},{1,17},{9,25},{17,1},{25,9},{2,18},{10... | collective-permute-start | bytes 86024 | tf_op jit(solution)/shard_map/ppermute | solution.py:715
  16.3 11.8 %collective-permute-start.9 = (f32[56,128]{1,0:T(8,128)S(1)}, f32[56,128]{1,0:T(8,128)S(1)}, u32[]{:S(2)}, u32[]{:S(2)}) collective-permute-start(f32[56,128]{1,0:T(8,128)S(1)} %get-tuple-element.59.after_ref.refs_0_), channel_id=1, source_target_pairs={{0,24},{8,0},{16,8},{24,16},{1,25},{9,1},{17,9},{25,17},{2,26},{10... | collective-permute-start | bytes 86024 | tf_op jit(solution)/shard_map/ppermute | solution.py:715
  28.1 2.8 %copy-start.2 = (s32[256,16]{0,1:T(8,128)S(1)}, s32[256,16]{0,1:T(8,128)}, u32[]{:S(2)}) copy-start(s32[256,16]{0,1:T(8,128)} %param.16) | copy-start | bytes 49156
  28.1 2.8 %copy-start.3 = (s32[256,16]{0,1:T(8,128)S(1)}, s32[256,16]{0,1:T(8,128)}, u32[]{:S(2)}) copy-start(s32[256,16]{0,1:T(8,128)} %param.17) | copy-start | bytes 49156
  28.2 16.1 %collective-permute-start.12 = (f32[224,128]{1,0:T(8,128)S(1)}, f32[224,128]{1,0:T(8,128)S(1)}, u32[]{:S(2)}, u32[]{:S(2)}) collective-permute-start(f32[224,128]{1,0:T(8,128)S(1)} %join.3.after_ref.refs_0_), channel_id=1, source_target_pairs={{0,2},{2,4},{4,6},{6,0},{1,3},{3,5},{5,7},{7,1},{8,10},{10,12},{12... | collective-permute-start | bytes 344072 | tf_op jit(solution)/shard_map/ppermute | solution.py:715
  28.2 16.0 %collective-permute-start.13 = (f32[224,128]{1,0:T(8,128)S(1)}, f32[224,128]{1,0:T(8,128)S(1)}, u32[]{:S(2)}, u32[]{:S(2)}) collective-permute-start(f32[224,128]{1,0:T(8,128)S(1)} %join.3.after_ref.refs_0_), channel_id=1, source_target_pairs={{0,4},{2,6},{4,0},{6,2},{1,5},{3,7},{5,1},{7,3},{8,12},{10,14},{12... | collective-permute-start | bytes 344072 | tf_op jit(solution)/shard_map/ppermute | solution.py:715
  29.3 15.0 %collective-permute-start.14 = (f32[224,128]{1,0:T(8,128)S(1)}, f32[224,128]{1,0:T(8,128)S(1)}, u32[]{:S(2)}, u32[]{:S(2)}) collective-permute-start(f32[224,128]{1,0:T(8,128)S(1)} %join.3.after_ref.refs_0_), channel_id=1, source_target_pairs={{0,6},{2,0},{4,2},{6,4},{1,7},{3,1},{5,3},{7,5},{8,14},{10,8},{12,... | collective-permute-start | bytes 344072 | tf_op jit(solution)/shard_map/ppermute | solution.py:715
  32.4 15.1 %copy-start.1 = (s32[256,27]{0,1:T(8,128)S(1)}, s32[256,27]{0,1:T(8,128)}, u32[]{:S(2)}) copy-start(s32[256,27]{0,1:T(8,128)} %param.15) | copy-start | bytes 82948
  44.3 48.9 %collective-permute-start.15 = (f32[896,128]{1,0:T(8,128)S(1)}, f32[896,128]{1,0:T(8,128)S(1)}, u32[]{:S(2)}, u32[]{:S(2)}) collective-permute-start(f32[896,128]{1,0:T(8,128)S(1)} %join.4.after_ref.refs_0_), channel_id=1, source_target_pairs={{0,1},{1,64},{64,65},{65,0},{2,3},{3,66},{66,67},{67,2},{4,5},{5,6... | collective-permute-start | bytes 1376264 | tf_op jit(solution)/shard_map/ppermute | solution.py:715
  46.5 46.7 %collective-permute-start.16 = (f32[896,128]{1,0:T(8,128)S(1)}, f32[896,128]{1,0:T(8,128)S(1)}, u32[]{:S(2)}, u32[]{:S(2)}) collective-permute-start(f32[896,128]{1,0:T(8,128)S(1)} %join.4.after_ref.refs_0_), channel_id=1, source_target_pairs={{0,64},{1,65},{64,0},{65,1},{2,66},{3,67},{66,2},{67,3},{4,68},{5,... | collective-permute-start | bytes 1376264 | tf_op jit(solution)/shard_map/ppermute | solution.py:715
  47.2 46.0 %collective-permute-start.17 = (f32[896,128]{1,0:T(8,128)S(1)}, f32[896,128]{1,0:T(8,128)S(1)}, u32[]{:S(2)}, u32[]{:S(2)}) collective-permute-start(f32[896,128]{1,0:T(8,128)S(1)} %join.4.after_ref.refs_0_), channel_id=1, source_target_pairs={{0,65},{1,0},{64,1},{65,64},{2,67},{3,2},{66,3},{67,66},{4,69},{5,... | collective-permute-start | bytes 1376264 | tf_op jit(solution)/shard_map/ppermute | solution.py:715
  47.5 49.8 %copy-start.6 = (s32[256]{0:T(256)S(1)}, s32[256]{0:T(256)}, u32[]{:S(2)}) copy-start(s32[256]{0:T(256)} %top_ref.5) | copy-start | bytes 3076
  93.3 17.6 %collective-permute-start.18 = (f32[3584,128]{1,0:T(8,128)S(1)}, f32[3584,128]{1,0:T(8,128)S(1)}, u32[]{:S(2)}, u32[]{:S(2)}) collective-permute-start(f32[3584,128]{1,0:T(8,128)S(1)} %join.5.after_ref.mine_ref), channel_id=1, source_target_pairs={{0,32},{32,0},{1,33},{33,1},{2,34},{34,2},{3,35},{35,3},{4,36},{36... | collective-permute-start | bytes 5505032 | tf_op jit(solution)/shard_map/ppermute | solution.py:745
  98.9 12.1 %copy-start.5 = (f32[8,81,81]{2,0,1:T(8,128)S(1)}, f32[8,81,81]{2,0,1:T(8,128)}, u32[]{:S(2)}) copy-start(f32[8,81,81]{2,0,1:T(8,128)} %param.21) | copy-start | bytes 629860
  129.2 0.6 copy-start.7

commit v4 on v3

--- a/solution.py
+++ b/solution.py
@@ -26,9 +26,12 @@
 SEND = 56
 REACH_SQ = 16.0
 FEAT = 32
+FEATS = 24
 LEAF_STEP = 4
 TURN_STEP = 3
 TOP_WINDOW = 256
+BUILD_STEP = 16
+NEAR_STEP = 32
 
 HIGH = lax.Precision.HIGHEST
 MIB = 1 << 20
@@ -187,7 +190,7 @@
 
 def near_kernel(
     near_ref, own_ref, before_ref, behind_ref, after_ref, out_ref,
-    win_ref, src_ref, tgt_ref, table_ref, charge_ref,
+    win_ref, src_ref, tgt_ref, source_ref, target_ref, charge_ref,
 ):
     del after_ref
     targets, width = PAIRS, WPAIRS
@@ -208,103 +211,91 @@
         moved.append(points[c] - 0.5 * (least + most))
     norm = moved[0] * moved[0] + moved[1] * moved[1] + moved[2] * moved[2]
     close = jnp.max(norm) <= REACH_SQ
+    out_ref[...] = jnp.zeros_like(out_ref)
 
     @pl.when(close)
     def _():
         own = slice(HPAIRS, HPAIRS + targets)
-        src_ref[...] = jnp.zeros_like(src_ref)
-        tgt_ref[...] = jnp.zeros_like(tgt_ref)
+
+        def keep(ref, f, feature):
+            rows = feature.shape[0]
+            ref[f * rows : (f + 1) * rows] = feature
+
         for c in range(3):
             h, m, l = split3(moved[c])
             for i, feature in enumerate((h, h, m, m, h, l)):
-                src_ref[pl.ds(6 * c + i, width, stride=FEAT), :] = feature
+                keep(src_ref, 6 * c + i, feature)
             th, tm, tl = [-2.0 * piece[own] for piece in (h, m, l)]
             for i, feature in enumerate((th, tm, th, tm, tl, th)):
-                tgt_ref[pl.ds(6 * c + i, targets, stride=FEAT), :] = feature
+                keep(tgt_ref, 6 * c + i, feature)
         ones = jnp.ones((width, 128), jnp.float32)
         for i, feature in enumerate(split3(norm + SOFTENING)):
-            src_ref[pl.ds(18 + i, width, stride=FEAT), :] = feature
-            tgt_ref[pl.ds(18 + i, targets, stride=FEAT), :] = ones[own]
+            keep(src_ref, 18 + i, feature)
+            keep(tgt_ref, 18 + i, ones[own])
         for i, feature in enumerate(split3(norm[own])):
-            src_ref[pl.ds(21 + i, width, stride=FEAT), :] = ones
-            tgt_ref[pl.ds(21 + i, targets, stride=FEAT), :] = feature
-        for i, feature in enumerate(split3(component(3))):
-            src_ref[pl.ds(24 + i, width, stride=FEAT), :] = feature
-
-        row = rows_of((128, 256))
-        lane = lanes((128, 256))
-        spread = []
-        for p in range(4):
-            local = row - FEAT * p
-            same = (lane < 128) & (local < 24) & (local == (lane & (FEAT - 1)))
-            charge = (lane >= 128) & (local >= 24) & (local < 27)
-            spread.append(jnp.where(same | charge, 1.0, 0.0).astype(jnp.bfloat16))
-
-        def build(i, carry):
-            for g in (2 * i, 2 * i + 1):
-                block = src_ref[pl.ds(pl.multiple_of(g * 128, 128), 128), :]
-                turned = block.T.astype(jnp.bfloat16)
-                for p in range(4):
-                    both = lax.dot_general(
-                        turned, spread[p], NN, preferred_element_type=jnp.float32
-                    )
-                    to = pl.ds(pl.multiple_of((g * 4 + p) * 128, 128), 128)
-                    table_ref[to, :] = both[:, :128].astype(jnp.bfloat16)
-                    charge_ref[to, :] = both[:, 128:]
+            keep(src_ref, 21 + i, ones)
+            keep(tgt_ref, 21 + i, feature)
+        charge = component(3)
+        charge_ref[pl.ds(0, width, stride=2), :] = charge
+        charge_ref[pl.ds(1, width, stride=2), :] = pltpu.roll(charge, PART, 1)
+        rest = jnp.zeros((FEAT - FEATS, 128), jnp.float32)
+
+        def build_source(i, carry):
+            for u in range(BUILD_STEP):
+                r = i * BUILD_STEP + u
+                some = src_ref[pl.ds(r, FEATS, stride=width), :]
+                some = jnp.concatenate([some, rest], axis=0)
+                source_ref[2 * r] = some.astype(jnp.bfloat16)
+                source_ref[2 * r + 1] = pltpu.roll(some, PART, 1).astype(jnp.bfloat16)
             return carry
 
-        lax.fori_loop(0, width // 8, build, 0)
-
-        lane_w = lanes((FEAT, 128))
-        lane_b = lanes((PART, 128))
-        low_half = lane_b < PART
-        def group(g, carry):
-            two = tgt_ref[pl.ds(pl.multiple_of(g * 2 * FEAT, 2 * FEAT), 2 * FEAT), :]
-            zero = jnp.zeros((FEAT, 128), jnp.float32)
-            left, right = [], []
-            for half in range(2):
-                one = two[half * FEAT : (half + 1) * FEAT]
-                low = jnp.where(lane_w < PART, one, 0.0)
-                high = jnp.where(lane_w < PART, 0.0, one)
-                left += [low, high] if half == 0 else [zero, zero]
-                right += [zero, zero] if half == 0 else [low, high]
-            weights = jnp.concatenate(
-                [jnp.concatenate(left, axis=0), jnp.concatenate(right, axis=0)], axis=1
-            ).astype(jnp.bfloat16)
-            mixed, spots = [], []
-            for k in range(NEAR):
-                four = []
-                for v in range(4):
-                    leaf = near_ref[k, g * 4 + v] - shift
-                    four.append(pl.ds(pl.multiple_of(leaf * PART, PART), PART))
-                rows = [table_ref[spot, :] for spot in four]
-                mixed.append(
-                    jnp.where(
-                        lane_b < 2 * FEAT,
-                        jnp.where(lane_b < FEAT, rows[0], rows[1]),
-                        jnp.where(lane_b < 3 * FEAT, rows[2], rows[3]),
-                    )
-                )
-                spots.append(four)
-            total = [jnp.zeros((8, 128), jnp.float32)] * 2
-            for some in range(0, NEAR, 14):
-                count = min(14, NEAR - some)
+        def build_target(i, carry):
+            for u in range(BUILD_STEP):
+                r = i * BUILD_STEP + u
+                some = tgt_ref[pl.ds(r, FEATS, stride=targets), :]
+                some = jnp.concatenate([some, rest], axis=0).T.astype(jnp.bfloat16)
+                for p in range(2):
+                    target_ref[2 * r + p] = some[p * PART : (p + 1) * PART]
+            return carry
+
+        lax.fori_loop(0, width // BUILD_STEP, build_source, 0)
+        lax.fori_loop(0, targets // BUILD_STEP, build_target, 0)
+
+        low_block = lanes((FEAT, 128)) < PART
+        low_row = lanes((1, 128)) < PART
+        lane = lanes((PART, 128))
+
+        def leaf_sums(l):
+            total = None
+            for k in range(0, NEAR + 1, 4):
+                blocks, charges = [], []
+                for j in range(k, k + 4, 2):
+                    one = near_ref[j, l] - shift
+                    two = (near_ref[min(j + 1, NEAR - 1), l] - shift) ^ 1
+                    blocks.append(jnp.where(low_block, source_ref[one], source_ref[two]))
+                    other = charge_ref[pl.ds(two, 1), :] if j + 1 < NEAR else 0.0
+                    charges.append(jnp.where(low_row, charge_ref[pl.ds(one, 1), :], other))
                 dist = lax.dot_general(
-                    jnp.concatenate(mixed[some : some + count], axis=0), weights, NN,
+                    target_ref[l], jnp.concatenate(blocks, axis=1), NN,
                     preferred_element_type=jnp.float32,
                 )
-                for k in range(count):
-                    inverse = lax.rsqrt(dist[k * PART : (k + 1) * PART])
-                    for half in range(2):
-                        low, high = spots[some + k][2 * half : 2 * half + 2]
-                        charge = jnp.where(low_half, charge_ref[low, :], charge_ref[high, :])
-                        term = charge * inverse[:, half * 128 : (half + 1) * 128]
-                        total[half] += jnp.sum(term.reshape(8, 8, 128), axis=0)
-            both = jnp.concatenate([jnp.sum(t, axis=0, keepdims=True) for t in total], axis=0)
-            out_ref[pl.ds(g * 2, 2), :] = both
+                for j in range(2):
+                    term = charges[j] * lax.rsqrt(dist[:, j * 128 : (j + 1) * 128])
+                    total = term if total is None else total + term
+            return total
+
+        def group(i, carry):
+            totals = [leaf_sums(i * NEAR_STEP + u) for u in range(NEAR_STEP)]
+            for p in range(2):
+                at = pl.ds(p * PART, PART)
+                wide = out_ref[at, :]
+                for u in range(p, NEAR_STEP, 2):
+                    sums = jnp.sum(totals[u], axis=1, keepdims=True)
+                    wide = jnp.where(lane == i * (NEAR_STEP // 2) + u // 2, sums, wide)
+                out_ref[at, :] = wide
             return carry
 
-        lax.fori_loop(0, targets // 2, group, 0)
+        lax.fori_loop(0, LEAVES // NEAR_STEP, group, 0)
 
     @pl.when(jnp.logical_not(close))
     def _():
@@ -317,7 +308,6 @@
                 ).T
                 for c in range(3)
             ]
-            results = []
             for p in range(2):
                 mine = [column[p * PART : (p + 1) * PART] for column in columns]
 
@@ -332,9 +322,9 @@
                     return total + half * (win_ref[pl.ds(at + 3, 1), :] * lax.rsqrt(gap))
 
                 total = lax.fori_loop(0, NEAR, entry, jnp.zeros((PART, 128), jnp.float32))
-                results.append(jnp.sum(total, axis=1, keepdims=True))
-            wide = jnp.broadcast_to(jnp.concatenate(results, axis=0), (128, 128)).T
-            out_ref[pl.ds(r, 1), :] = wide[:1]
+                at = pl.ds(p * PART, PART)
+                sums = jnp.sum(total, axis=1, keepdims=True)
+                out_ref[at, :] = jnp.where(lane == r, sums, out_ref[at, :])
             return carry
 
         lax.fori_loop(0, targets, pair, 0)
@@ -383,10 +373,15 @@
 def leaf_kernel(part, code_ref, ops_ref, rows_ref, after_ref, out_ref, total_ref):
     del after_ref
     begin = part * (PAIRS // 2)
+    lane = lanes((OPROWS, 128))
 
     def reduce(i):
-        for v in range(LEAF_STEP):
-            put_sums(total_ref.at[v], out_ref.at[v & 1], begin + 2 * i + (v >> 1))
+        for p in range(2):
+            wide = out_ref[p]
+            for v in range(p, LEAF_STEP, 2):
+                at = begin + i * (LEAF_STEP // 2) + v // 2
+                wide = jnp.where(lane == at, jnp.sum(total_ref[v], axis=1, keepdims=True), wide)
+            out_ref[p] = wide
 
     def step(i, carry):
         reduce(i - 1)
@@ -473,7 +468,7 @@
             return carry
 
         lax.fori_loop(0, PART // 16, step, 0)
-    out_ref[...] = (near_ref[...] + pot_ref[...].T) * mask_ref[...]
+    out_ref[...] = (near_ref[...] + pot_ref[...]).T * mask_ref[...]
 
 
 def last_kernel(
@@ -619,10 +614,11 @@
         out_specs=VMEM,
         scratch_shapes=[
             pltpu.VMEM((4 * WPAIRS, 128), F32),
-            pltpu.VMEM((width * FEAT, 128), F32),
-            pltpu.VMEM((targets * FEAT, 128), F32),
-            pltpu.VMEM((width * 128, 128), jnp.bfloat16),
-            pltpu.VMEM((width * 128, 128), F32),
+            pltpu.VMEM((width * FEATS, 128), F32),
+            pltpu.VMEM((targets * FEATS, 128), F32),
+            pltpu.VMEM((2 * width, FEAT, 128), jnp.bfloat16),
+            pltpu.VMEM((LEAVES, PART, FEAT), jnp.bfloat16),
+            pltpu.VMEM((2 * width, 128), F32),
         ],
         compiler_params=pltpu.CompilerParams(vmem_limit_bytes=24 * MIB),
         cost_estimate=cost(10 * targets * 2 * 64 * NEAR * 64, 3 * 10**7),

time: 129 us -> 107 us (0.83); the launches traced: 130 us -> 105 us
  Pallas kernels: 104 us -> 80 us
    pallas_call x1, Pallas kernels: 45.6 us -> 24 us  [call_near(): pl.pallas_call(near_kernel, out_shape=shape(targets, 128), in_specs=[SMEM...]
    pallas_call x1, Pallas kernels: 17.5 us -> 14.8 us  [call_last(): pl.pallas_call(last_kernel, out_shape=(shape(PAIRS, 128), jax.ShapeDtypeS...]
  transfers between devices with their start and end apart: 12 -> 12, of which waited for: 0 -> 0; matrix products, arithmetic and copies ran while one was open for 0% -> 0% of each run, Pallas kernels for 64% -> 58%
where the time goes in v4:
time: 107 us; the launch traced here: 105 us
  Pallas kernels  80 us (75%)
  starting transfers between devices  22.2 us (21%)
  local copies, waits for them, and re-layouts  2.28 us (2%)
    pallas_call x2, Pallas kernels, call_leaf(): pl.pallas_call(functools.partial(leaf_kernel, part), out_shape=shape(2, O...  24.1 us
    pallas_call x1, Pallas kernels, call_near(): pl.pallas_call(near_kernel, out_shape=shape(targets, 128), in_specs=[SMEM...  24 us
    pallas_call x1, Pallas kernels, call_last(): pl.pallas_call(last_kernel, out_shape=(shape(PAIRS, 128), jax.ShapeDtypeS...  14.8 us
    pallas_call x1, Pallas kernels, call_turn(): pl.pallas_call(turn_kernel, out_shape=shape(CLASSES * OPROWS, 128), in_sp...  10.2 us
    ppermute x9, starting transfers between devices, sent_over(): lax.ppermute(block, axis, [(i, (i + s) % count) for i in range(count)])  8.61 us
    ppermute x1, starting transfers between devices, body(): behind = lax.ppermute(low, AXES, down)  5.29 us
    ppermute x1, starting transfers between devices, body(): before = lax.ppermute(high, AXES, up)  4.49 us
    ppermute x1, starting transfers between devices, body(): other = lax.ppermute(mine, 'core', [(0, 1), (1, 0)])  3.82 us
  transfers between devices with their start and end apart: 12, of which 0 were waited for; matrix products, arithmetic and copies ran while one was open for 0% of the time, Pallas kernels for 58%

profile of v4, /device:TPU:1, one launch (start us, length us, event | category | flops | bytes accessed | tf_op | source)
XLA Modules:
  0.0 105.4 jit_solution(16297391012848863002)
XLA Ops:
  0.0 0.0 copy-start
  0.0 0.9 copy-done
  1.0 0.0 copy-start.4
  1.0 0.7 copy-done.4
  1.6 3.8 %expand_own.1 = (f32[512,128]{1,0:T(8,128)S(1)}, f32[64,128]{1,0:T(8,128)S(1)}, f32[64,128]{1,0:T(8,128)S(1)}, f32[3,128,128]{2,1,0:T(8,128)S(1)}, f32[256,128]{...) custom-call(f32[512,128]{1,0:T(8,128)S(1)} %bitcast.20, ...), custom_call_target="tpu_custom_call" | custom-call | flops 1000000000 | bytes 10000000 | tf_op jit(solution)/shard_map/expand_own/pallas_call | solution.py:564
  5.4 4.5 %collective-permute-start.10 = (f32[64,128]{1,0:T(8,128)S(1)}, f32[64,128]{1,0:T(8,128)S(1)}, u32[]{:S(2)}, u32[]{:S(2)}) collective-permute-start(f32[64,128]{1,0:T(8,128)S(1)} %get-tuple-element.60), channel_id=1, source_target_pairs={{0,1},{1,2},{2,3},{3,4},{4,5},{5,6},{6,7},{7,8},{8,9},{9,10},{10,1... | collective-permute-start | bytes 98312 | tf_op jit(solution)/shard_map/ppermute | solution.py:730
  9.9 5.3 %collective-permute-start.11 = (f32[64,128]{1,0:T(8,128)S(1)}, f32[64,128]{1,0:T(8,128)S(1)}, u32[]{:S(2)}, u32[]{:S(2)}) collective-permute-start(f32[64,128]{1,0:T(8,128)S(1)} %get-tuple-element.61), channel_id=1, source_target_pairs={{1,0},{2,1},{3,2},{4,3},{5,4},{6,5},{7,6},{8,7},{9,8},{10,9},{11,1... | collective-permute-start | bytes 98312 | tf_op jit(solution)/shard_map/ppermute | solution.py:731
  15.2 0.0 collective-permute-start.7
  15.2 1.1 %collective-permute-start.8 = (f32[56,128]{1,0:T(8,128)S(1)}, f32[56,128]{1,0:T(8,128)S(1)}, u32[]{:S(2)}, u32[]{:S(2)}) collective-permute-start(f32[56,128]{1,0:T(8,128)S(1)} %get-tuple-element.59.after_ref.refs_0_), channel_id=1, source_target_pairs={{0,16},{8,24},{16,0},{24,8},{1,17},{9,25},{17,1},{25,9},{2,18},{10... | collective-permute-start | bytes 86024 | tf_op jit(solution)/shard_map/ppermute | solution.py:711
  16.3 1.6 %collective-permute-start.9 = (f32[56,128]{1,0:T(8,128)S(1)}, f32[56,128]{1,0:T(8,128)S(1)}, u32[]{:S(2)}, u32[]{:S(2)}) collective-permute-start(f32[56,128]{1,0:T(8,128)S(1)} %get-tuple-element.59.after_ref.refs_0_), channel_id=1, source_target_pairs={{0,24},{8,0},{16,8},{24,16},{1,25},{9,1},{17,9},{25,17},{2,26},{10... | collective-permute-start | bytes 86024 | tf_op jit(solution)/shard_map/ppermute | solution.py:711
  17.9 10.2 %turn_operators.3.refs_4_.ops_ref = f32[27808,128]{1,0:T(8,128)S(1)} custom-call(f32[81,81,316]{2,1,0:T(8,128)} %bitcast.24, f32[56,128]{1,0:T(8,128)S(1)} %get-tuple-element.59.after_ref.refs_0_), custom_call_target="tpu_custom_call" | custom-call | flops 10000000 | bytes 30000000 | tf_op jit(solution)/shard_map/turn_operators/pallas_call | solution.py:584
  28.1 0.0 copy-start.2
  28.1 0.0 copy-start.3
  28.1 0.0 collective-permute-done.7.refs_1_
  28.1 0.0 collective-permute-done.8.refs_2_
  28.1 0.0 collective-permute-done.9.refs_3_
  28.1 0.0 collective-permute-done.10.refs_5_.before_ref
  28.1 0.0 collective-permute-done.11.refs_6_.behind_ref
  28.2 0.1 collective-permute-start.12
  28.2 1.0 collective-permute-start.13
  29.3 1.7 %collective-permute-start.14 = (f32[224,128]{1,0:T(8,128)S(1)}, f32[224,128]{1,0:T(8,128)S(1)}, u32[]{:S(2)}, u32[]{:S(2)}) collective-permute-start(f32[224,128]{1,0:T(8,128)S(1)} %join.3.after_ref.refs_0_), channel_id=1, source_target_pairs={{0,6},{2,0},{4,2},{6,4},{1,7},{3,1},{5,3},{7,5},{8,14},{10,8},{12,... | collective-permute-start | bytes 344072 | tf_op jit(solution)/shard_map/ppermute | solution.py:711
  30.9 0.0 copy-done.2
  30.9 0.0 copy-done.3
  30.9 1.5 %expand_halo.1 = (s32[16,256]{1,0:T(8,128)S(1)}, f32[320,128]{1,0:T(8,128)S(1)}) custom-call(s32[16,256]{1,0:T(8,128)S(1)} %bitcast.22, s32[16,256]{1,0:T(8,128)S(1)} %bitcast.23, f32[256,128]{1,0:T(8,128)S(1)} %get-tuple-element.62.moment_ref, f32[64,128]{1,0:T(8,128)S(1)} %collective-permute-done.10.refs_5_.before_ref, ...), custom_call_target="tpu_custom_call" | custom-call | flops 100000000 | bytes 1000000 | tf_op jit(solution)/shard_map/expand_halo/pallas_call | solution.py:630
  32.4 0.0 copy-start.1
  32.4 12.0 %leaf_translate.2.refs_4_.local_a_ref = f32[2,88,128]{2,1,0:T(8,128)S(1)} custom-call(s32[16,256]{1,0:T(8,128)S(1)} %get-tuple-element.63.code_ref, f32[27808,128]{1,0:T(8,128)S(1)} %turn_operators.3.refs_4_.ops_ref, f32[320,128]{1,0:T(8,128)S(1)} %get-tuple-element.64.rows_ref, f32[224,128]{1,0:T(8,128)S(1)} %join.3.after_ref.refs_0_), custom_call_target="tpu_custom_call" | custom-call | flops 214990848 | bytes 20000000 | tf_op jit(solution)/shard_map/leaf_translate/pallas_call | solution.py:648
  44.4 0.0 collective-permute-done.12.refs_1_
  44.4 0.0 collective-permute-done.13.refs_2_
  44.5 0.0 collective-permute-done.14.refs_3_
  44.5 2.2 %collective-permute-start.15 = (f32[896,128]{1,0:T(8,128)S(1)}, f32[896,128]{1,0:T(8,128)S(1)}, u32[]{:S(2)}, u32[]{:S(2)}) collective-permute-start(f32[896,128]{1,0:T(8,128)S(1)} %join.4.after_ref.refs_0_), channel_id=1, source_target_pairs={{0,1},{1,64},{64,65},{65,0},{2,3},{3,66},{66,67},{67,2},{4,5},{5,6... | collective-permute-start | bytes 1376264 | tf_op jit(solution)/shard_map/ppermute | solution.py:711
  46.7 0.7 collective-permute-start.16
  47.4 0.3 collective-permute-start.17
  47.7 0.0 copy-done.1
  47.7 24.0 %near.1.refs_4_.near_ref = f32[128,128]{1,0:T(8,128)S(1)} custom-call(s32[27,256]{1,0:T(8,128)S(1)} %bitcast.21, f32[512,128]{1,0:T(8,128)S(1)} %get-tuple-element.65.own_ref, f32[64,128]{1,0:T(8,128)S(1)} %collective-permute-done.10.refs_5_.before_ref, f32[64,128]{1,0:T(8,128)S(1)} %collective-permute-done.11.refs_6_.behind_ref, ...), custom_call_target="tpu_custom_call" | custom-call | flops 283115520 | bytes 30000000 | tf_op jit(solution)/shard_map/near/pallas_call | solution.py:610
  71.7 0.0 collective-permute-done.15.refs_1_
  71.7 0.0 collective-permute-done.16.refs_2_
  71.7 0.0 collective-permute-done.17.refs_3_
  71.7 0.1 join.5.after_ref.mine_ref
  71.9 3.8 %collective-permute-start.18 = (f32[3584,128]{1,0:T(8,128)S(1)}, f32[3584,128]{1,0:T(8,128)S(1)}, u32[]{:S(2)}, u32[]{:S(2)}) collective-permute-start(f32[3584,128]{1,0:T(8,128)S(1)} %join.5.after_ref.mine_ref), channel_id=1, source_target_pairs={{0,32},{32,0},{1,33},{33,1},{2,34},{34,2},{3,35},{35,3},{4,36},{36... | collective-permute-start | bytes 5505032 | tf_op jit(solution)/shard_map/ppermute | solution.py:741
  75.7 0.0 copy-done.6
  75.7 1.5 %fetch_lists.1.code_ref = s32[64,128]{1,0:T(8,128)S(1)} custom-call(s32[256]{0:T(256)S(1)} %copy-done.6, s32[64,4096]{1,0:T(8,128)} %bitcast.5.list_ref, s32[64,4096]{1,0:T(8,128)} %bitcast.6.class_ref), custom_call_target="tpu_custom_call" | custom-call | flops 100000 | bytes 100000 | tf_op jit(solution)/shard_map/fetch_lists/pallas_call | solution.py:662
  77.2 0.0 copy-start.5
  77.2 12.1 %leaf_translate.3.local_b_ref = f32[2,88,128]{2,1,0:T(8,128)S(1)} custom-call(s32[16,256]{1,0:T(8,128)S(1)} %get-tuple-element.63.code_ref, f32[27808,128]{1,0:T(8,128)S(1)} %turn_operators.3.refs_4_.ops_ref, f32[320,128]{1,0:T(8,128)S(1)} %get-tuple-element.64.rows_ref, f32[3584,128]{1,0:T(8,128)S(1)} %join.5.after_ref.mine_ref), custom_call_target="tpu_custom_call" | custom-call | flops 214990848 | bytes 20000000 | tf_op jit(solution)/shard_map/leaf_translate/pallas_call | solution.py:648
  89.3 0.0 collective-permute-done.18.other_ref
  89.3 0.0 copy-done.5
  89.3 14.8 %finish.1 = (f32[128,128]{1,0:T(8,128)S(1)}, s32[1]{0:T(128)}) custom-call(s32[256]{0:T(256)S(1)} %copy-done.6, s32[64,128]{1,0:T(8,128)S(1)} %fetch_lists.1.code_ref, f32[3584,128]{1,0:T(8,128)S(1)} %join.5.after_ref.mine_ref, f32[3584,128]{1,0:T(8,128)S(1)} %collective-permute-done.18.other_ref, f32[27808,128]{1,0:T(8,128)S(1)} %turn_operators.3.refs_4_.ops_ref, ...), custom_call_target="tpu_custom_call" | custom-call | tf_op jit(solution)/shard_map/finish/pallas_call | solution.py:678
  104.8 0.0 copy-start.7
  104.8 0.6 copy-done.7
  (4 shorter events, 0.1 us)
Async XLA Ops:
  0.0 0.9 copy-start
  1.0 0.7 copy-start.4
  5.4 22.7 %collective-permute-start.10 = (f32[64,128]{1,0:T(8,128)S(1)}, f32[64,128]{1,0:T(8,128)S(1)}, u32[]{:S(2)}, u32[]{:S(2)}) collective-permute-start(f32[64,128]{1,0:T(8,128)S(1)} %get-tuple-element.60), channel_id=1, source_target_pairs={{0,1},{1,2},{2,3},{3,4},{4,5},{5,6},{6,7},{7,8},{8,9},{9,10},{10,1... | collective-permute-start | bytes 98312 | tf_op jit(solution)/shard_map/ppermute | solution.py:730
  9.9 18.2 %collective-permute-start.11 = (f32[64,128]{1,0:T(8,128)S(1)}, f32[64,128]{1,0:T(8,128)S(1)}, u32[]{:S(2)}, u32[]{:S(2)}) collective-permute-start(f32[64,128]{1,0:T(8,128)S(1)} %get-tuple-element.61), channel_id=1, source_target_pairs={{1,0},{2,1},{3,2},{4,3},{5,4},{6,5},{7,6},{8,7},{9,8},{10,9},{11,1... | collective-permute-start | bytes 98312 | tf_op jit(solution)/shard_map/ppermute | solution.py:731
  15.2 12.9 %collective-permute-start.7 = (f32[56,128]{1,0:T(8,128)S(1)}, f32[56,128]{1,0:T(8,128)S(1)}, u32[]{:S(2)}, u32[]{:S(2)}) collective-permute-start(f32[56,128]{1,0:T(8,128)S(1)} %get-tuple-element.59.after_ref.refs_0_), channel_id=1, source_target_pairs={{0,8},{8,16},{16,24},{24,0},{1,9},{9,17},{17,25},{25,1},{2,10},{10... | collective-permute-start | bytes 86024 | tf_op jit(solution)/shard_map/ppermute | solution.py:711
  15.2 12.9 %collective-permute-start.8 = (f32[56,128]{1,0:T(8,128)S(1)}, f32[56,128]{1,0:T(8,128)S(1)}, u32[]{:S(2)}, u32[]{:S(2)}) collective-permute-start(f32[56,128]{1,0:T(8,128)S(1)} %get-tuple-element.59.after_ref.refs_0_), channel_id=1, source_target_pairs={{0,16},{8,24},{16,0},{24,8},{1,17},{9,25},{17,1},{25,9},{2,18},{10... | collective-permute-start | bytes 86024 | tf_op jit(solution)/shard_map/ppermute | solution.py:711
  16.3 11.8 %collective-permute-start.9 = (f32[56,128]{1,0:T(8,128)S(1)}, f32[56,128]{1,0:T(8,128)S(1)}, u32[]{:S(2)}, u32[]{:S(2)}) collective-permute-start(f32[56,128]{1,0:T(8,128)S(1)} %get-tuple-element.59.after_ref.refs_0_), channel_id=1, source_target_pairs={{0,24},{8,0},{16,8},{24,16},{1,25},{9,1},{17,9},{25,17},{2,26},{10... | collective-permute-start | bytes 86024 | tf_op jit(solution)/shard_map/ppermute | solution.py:711
  28.1 2.8 %copy-start.2 = (s32[256,16]{0,1:T(8,128)S(1)}, s32[256,16]{0,1:T(8,128)}, u32[]{:S(2)}) copy-start(s32[256,16]{0,1:T(8,128)} %param.16) | copy-start | bytes 49156
  28.1 2.8 %copy-start.3 = (s32[256,16]{0,1:T(8,128)S(1)}, s32[256,16]{0,1:T(8,128)}, u32[]{:S(2)}) copy-start(s32[256,16]{0,1:T(8,128)} %param.17) | copy-start | bytes 49156
  28.2 16.3 %collective-permute-start.12 = (f32[224,128]{1,0:T(8,128)S(1)}, f32[224,128]{1,0:T(8,128)S(1)}, u32[]{:S(2)}, u32[]{:S(2)}) collective-permute-start(f32[224,128]{1,0:T(8,128)S(1)} %join.3.after_ref.refs_0_), channel_id=1, source_target_pairs={{0,2},{2,4},{4,6},{6,0},{1,3},{3,5},{5,7},{7,1},{8,10},{10,12},{12... | collective-permute-start | bytes 344072 | tf_op jit(solution)/shard_map/ppermute | solution.py:711
  28.2 16.2 %collective-permute-start.13 = (f32[224,128]{1,0:T(8,128)S(1)}, f32[224,128]{1,0:T(8,128)S(1)}, u32[]{:S(2)}, u32[]{:S(2)}) collective-permute-start(f32[224,128]{1,0:T(8,128)S(1)} %join.3.after_ref.refs_0_), channel_id=1, source_target_pairs={{0,4},{2,6},{4,0},{6,2},{1,5},{3,7},{5,1},{7,3},{8,12},{10,14},{12... | collective-permute-start | bytes 344072 | tf_op jit(solution)/shard_map/ppermute | solution.py:711
  29.3 15.2 %collective-permute-start.14 = (f32[224,128]{1,0:T(8,128)S(1)}, f32[224,128]{1,0:T(8,128)S(1)}, u32[]{:S(2)}, u32[]{:S(2)}) collective-permute-start(f32[224,128]{1,0:T(8,128)S(1)} %join.3.after_ref.refs_0_), channel_id=1, source_target_pairs={{0,6},{2,0},{4,2},{6,4},{1,7},{3,1},{5,3},{7,5},{8,14},{10,8},{12,... | collective-permute-start | bytes 344072 | tf_op jit(solution)/shard_map/ppermute | solution.py:711
  32.4 15.3 %copy-start.1 = (s32[256,27]{0,1:T(8,128)S(1)}, s32[256,27]{0,1:T(8,128)}, u32[]{:S(2)}) copy-start(s32[256,27]{0,1:T(8,128)} %param.15) | copy-start | bytes 82948
  44.5 27.2 %collective-permute-start.15 = (f32[896,128]{1,0:T(8,128)S(1)}, f32[896,128]{1,0:T(8,128)S(1)}, u32[]{:S(2)}, u32[]{:S(2)}) collective-permute-start(f32[896,128]{1,0:T(8,128)S(1)} %join.4.after_ref.refs_0_), channel_id=1, source_target_pairs={{0,1},{1,64},{64,65},{65,0},{2,3},{3,66},{66,67},{67,2},{4,5},{5,6... | collective-permute-start | bytes 1376264 | tf_op jit(solution)/shard_map/ppermute | solution.py:711
  46.7 25.0 %collective-permute-start.16 = (f32[896,128]{1,0:T(8,128)S(1)}, f32[896,128]{1,0:T(8,128)S(1)}, u32[]{:S(2)}, u32[]{:S(2)}) collective-permute-start(f32[896,128]{1,0:T(8,128)S(1)} %join.4.after_ref.refs_0_), channel_id=1, source_target_pairs={{0,64},{1,65},{64,0},{65,1},{2,66},{3,67},{66,2},{67,3},{4,68},{5,... | collective-permute-start | bytes 1376264 | tf_op jit(solution)/shard_map/ppermute | solution.py:711
  47.4 24.3 %collective-permute-start.17 = (f32[896,128]{1,0:T(8,128)S(1)}, f32[896,128]{1,0:T(8,128)S(1)}, u32[]{:S(2)}, u32[]{:S(2)}) collective-permute-start(f32[896,128]{1,0:T(8,128)S(1)} %join.4.after_ref.refs_0_), channel_id=1, source_target_pairs={{0,65},{1,0},{64,1},{65,64},{2,67},{3,2},{66,3},{67,66},{4,69},{5,... | collective-permute-start | bytes 1376264 | tf_op jit(solution)/shard_map/ppermute | solution.py:711
  47.7 28.0 %copy-start.6 = (s32[256]{0:T(256)S(1)}, s32[256]{0:T(256)}, u32[]{:S(2)}) copy-start(s32[256]{0:T(256)} %top_ref.5) | copy-start | bytes 3076
  71.9 17.5 %collective-permute-start.18 = (f32[3584,128]{1,0:T(8,128)S(1)}, f32[3584,128]{1,0:T(8,128)S(1)}, u32[]{:S(2)}, u32[]{:S(2)}) collective-permute-start(f32[3584,128]{1,0:T(8,128)S(1)} %join.5.after_ref.mine_ref), channel_id=1, source_target_pairs={{0,32},{32,0},{1,33},{33,1},{2,34},{34,2},{3,35},{35,3},{4,36},{36... | collective-permute-start | bytes 5505032 | tf_op jit(solution)/shard_map/ppermute | solution.py:741
  77.2 12.1 %copy-start.5 = (f32[8,81,81]{2,0,1:T(8,128)S(1)}, f32[8,81,81]{2,0,1:T(8,128)}, u32[]{:S(2)}) copy-start(f32[8,81,81]{2,0,1:T(8,128)} %param.21) | copy-start | bytes 629860
  104.8 0.6 copy-start.7

commit v5 on v4

--- a/solution.py
+++ b/solution.py
@@ -28,7 +28,7 @@
 FEAT = 32
 FEATS = 24
 LEAF_STEP = 4
-TURN_STEP = 3
+TURN_STEP = 9
 TOP_WINDOW = 256
 BUILD_STEP = 16
 NEAR_STEP = 32
@@ -123,7 +123,7 @@
 
 def first_kernel(
     pts_ref, count_ref, top_ref, tops_ref, m2m_ref,
-    own_ref, low_ref, high_ref, dist_ref, moment_ref, send_ref, part_ref, mask_ref,
+    own_ref, near_edge_ref, far_edge_ref, dist_ref, moment_ref, send_ref, part_ref, mask_ref,
     q_ref, acc_ref, lift_ref,
 ):
     lane = lanes((1, 128))
@@ -139,8 +139,10 @@
     charge = pts_ref[pl.ds(3, PAIRS, stride=4), :] * mask_ref[...]
     own_ref[...] = pts_ref[...]
     own_ref[pl.ds(3, PAIRS, stride=4), :] = charge
-    low_ref[...] = own_ref[: 4 * HPAIRS]
-    high_ref[...] = own_ref[4 * (PAIRS - HPAIRS) :]
+    even = lax.axis_index("zhi") == 0
+    low, high = own_ref[: 4 * HPAIRS], own_ref[4 * (PAIRS - HPAIRS) :]
+    near_edge_ref[...] = jnp.where(even, high, low)
+    far_edge_ref[...] = jnp.where(even, low, high)
     for c in range(3):
         dist_ref[c] = centred(pts_ref[pl.ds(c, PAIRS, stride=4), :])
     q_ref[...] = charge.T
@@ -189,15 +191,16 @@
 
 
 def near_kernel(
-    near_ref, own_ref, before_ref, behind_ref, after_ref, out_ref,
+    near_ref, own_ref, partner_ref, far_ref, after_ref, out_ref,
     win_ref, src_ref, tgt_ref, source_ref, target_ref, charge_ref,
 ):
     del after_ref
     targets, width = PAIRS, WPAIRS
     edge = 4 * HPAIRS
-    win_ref[:edge] = before_ref[...]
+    even = lax.axis_index("zhi") == 0
+    win_ref[:edge] = jnp.where(even, far_ref[...], partner_ref[...])
     win_ref[edge : edge + 4 * PAIRS] = own_ref[...]
-    win_ref[edge + 4 * PAIRS :] = behind_ref[...]
+    win_ref[edge + 4 * PAIRS :] = jnp.where(even, partner_ref[...], far_ref[...])
     shift = lax.axis_index(AXES) * LEAVES - HALO
 
     def component(c):
@@ -334,10 +337,10 @@
     total = None
     for code in codes:
         at = pl.ds(pl.multiple_of(code >> ROW_BITS, 8), OPROWS)
-        row = rows_ref[pl.ds(code & ((1 << ROW_BITS) - 1), 1), :]
-        term = ops_ref[at, :] * row
+        row = rows_ref[pl.ds(code & ((1 << ROW_BITS) - 1), 8, stride=0), :]
+        term = ops_ref[at, :].reshape(OPROWS // 8, 8, 128) * row[None]
         total = term if total is None else total + term
-    return total
+    return total.reshape(OPROWS, 128)
 
 
 def pack_codes(kinds, rows):
@@ -350,16 +353,28 @@
 
 
 def halo_kernel(
-    list_ref, class_ref, moment_ref, before_ref, behind_ref, code_ref, rows_ref,
-    d_ref, q_ref, acc_ref, halo_ref,
+    top_ref, top_list_ref, top_class_ref,
+    list_ref, class_ref, moment_ref, partner_ref, far_ref, code_ref, rows_ref, top_code_ref,
+    d_ref, q_ref, acc_ref, halo_ref, list_vmem, class_vmem, sems,
 ):
+    window = pl.ds(pl.multiple_of(window_start(top_ref), 128), TOP_WINDOW)
+    copies = [
+        pltpu.make_async_copy(top_list_ref.at[:, window], list_vmem, sems.at[0]),
+        pltpu.make_async_copy(top_class_ref.at[:, window], class_vmem, sems.at[1]),
+    ]
+    for copy in copies:
+        copy.start()
+    even = lax.axis_index("zhi") == 0
     shift = lax.axis_index(AXES) * LEAVES - HALO
     code_ref[...] = pack_codes(class_ref[...], list_ref[...] - shift)
     fill = jnp.zeros((PAIRS - 2 * HPAIRS, 128), jnp.float32)
 
     def component(c):
         at = pl.ds(c, HPAIRS, stride=4)
-        return jnp.concatenate([before_ref[at, :], behind_ref[at, :], fill], axis=0)
+        one, two = partner_ref[at, :], far_ref[at, :]
+        return jnp.concatenate(
+            [jnp.where(even, two, one), jnp.where(even, one, two), fill], axis=0
+        )
 
     for c in range(3):
         d_ref[c] = centred(component(c))
@@ -368,6 +383,11 @@
     rows_ref[:HALO] = halo_ref[:HALO]
     rows_ref[HALO : HALO + LEAVES] = moment_ref[...]
     rows_ref[HALO + LEAVES :] = halo_ref[HALO : 2 * HALO]
+    for copy in copies:
+        copy.wait()
+    codes = pack_codes(class_vmem[...], list_vmem[...])
+    ahead = top_ref[0] - window_start(top_ref)
+    top_code_ref[...] = pltpu.roll(codes, (TOP_WINDOW - ahead) % TOP_WINDOW, 1)[:, :128]
 
 
 def leaf_kernel(part, code_ref, ops_ref, rows_ref, after_ref, out_ref, total_ref):
@@ -397,21 +417,6 @@
     steps = LEAVES // 2 // LEAF_STEP
     lax.fori_loop(0, steps, step, 0)
     reduce(steps - 1)
-
-
-def fetch_kernel(top_ref, list_ref, class_ref, code_ref, list_vmem, class_vmem, sems):
-    at = pl.ds(pl.multiple_of(window_start(top_ref), 128), TOP_WINDOW)
-    copies = [
-        pltpu.make_async_copy(list_ref.at[:, at], list_vmem, sems.at[0]),
-        pltpu.make_async_copy(class_ref.at[:, at], class_vmem, sems.at[1]),
-    ]
-    for copy in copies:
-        copy.start()
-    for copy in copies:
-        copy.wait()
-    codes = pack_codes(class_vmem[...], list_vmem[...])
-    shift = top_ref[0] - window_start(top_ref)
-    code_ref[...] = pltpu.roll(codes, (TOP_WINDOW - shift) % TOP_WINDOW, 1)[:, :128]
 
 
 def window_start(top_ref):
@@ -489,9 +494,9 @@
     over_ref[0] = most
     core, my_y, my_x = lax.axis_index("core"), lax.axis_index("y"), lax.axis_index("x")
     my_z = lax.axis_index(("zlo", "zhi"))
-    by_z = [((my_z - z) & 3) * 16 for z in range(4)]
-    by_x = [((my_x - x) & 3) * 4 for x in range(4)]
-    by_y = [(my_y - y) & 3 for y in range(4)]
+    by_z = [(my_z ^ z) * 16 for z in range(4)]
+    by_x = [(my_x ^ x) * 4 for x in range(4)]
+    by_y = [my_y ^ y for y in range(4)]
     by_core = [blocks * (core ^ side) for side in range(2)]
     order = [
         by_z[zlo * 2 + zhi] + by_x[x] + by_y[y] + by_core[side]
@@ -547,6 +552,7 @@
 
 
 ANY = pl.BlockSpec(memory_space=pl.ANY)
+HBM = pl.BlockSpec(memory_space=pltpu.HBM)
 FINISH_SCRATCH = [
     pltpu.VMEM((2, OPROWS, 128), F32),
     pltpu.VMEM((128, 128), F32),
@@ -626,22 +632,28 @@
     )(near, own, before, behind, after)
 
 
-def call_halo(lists, classes, moments, before, behind):
+def call_halo(leaf_top, top_lists, top_classes, lists, classes, moments, partner, far):
     return pl.pallas_call(
         halo_kernel,
-        out_shape=(jax.ShapeDtypeStruct((LLIST, LEAVES), jnp.int32), shape(2 * WPAIRS, 128)),
-        in_specs=[VMEM] * 5,
-        out_specs=(VMEM, VMEM),
+        out_shape=(
+            jax.ShapeDtypeStruct((LLIST, LEAVES), jnp.int32), shape(2 * WPAIRS, 128),
+            jax.ShapeDtypeStruct((TLIST, 128), jnp.int32),
+        ),
+        in_specs=[SMEM, HBM, HBM] + [VMEM] * 5,
+        out_specs=(VMEM,) * 3,
         scratch_shapes=[
             pltpu.VMEM((3, 128, 128), F32),
             pltpu.VMEM((128, 128), F32),
             pltpu.VMEM((COEF, 8, 128), F32),
             pltpu.VMEM((LEAVES, 128), F32),
+            pltpu.VMEM((TLIST, TOP_WINDOW), jnp.int32),
+            pltpu.VMEM((TLIST, TOP_WINDOW), jnp.int32),
+            pltpu.SemaphoreType.DMA((2,)),
         ],
         compiler_params=pltpu.CompilerParams(vmem_limit_bytes=16 * MIB),
         cost_estimate=cost(10**8, 10**6),
         name="expand_halo",
-    )(lists, classes, moments, before, behind)
+    )(leaf_top, top_lists, top_classes, lists, classes, moments, partner, far)
 
 
 def call_leaf(part, code, ops, rows, after):
@@ -655,23 +667,6 @@
         cost_estimate=cost(LEAVES * LLIST * COEF * COEF * 8, 2 * 10**7),
         name="leaf_translate",
     )(code, ops, rows, after)
-
-
-def call_fetch(leaf_top, lists, classes):
-    window = (TLIST, TOP_WINDOW)
-    return pl.pallas_call(
-        fetch_kernel,
-        out_shape=jax.ShapeDtypeStruct((TLIST, 128), jnp.int32),
-        in_specs=[SMEM, ANY, ANY],
-        out_specs=VMEM,
-        scratch_shapes=[
-            pltpu.VMEM(window, jnp.int32), pltpu.VMEM(window, jnp.int32),
-            pltpu.SemaphoreType.DMA((2,)),
-        ],
-        compiler_params=pltpu.CompilerParams(vmem_limit_bytes=8 * MIB),
-        cost_estimate=cost(10**5, 10**5),
-        name="fetch_lists",
-    )(leaf_top, lists, classes)
 
 
 def call_last(leaf_top, code, mine, other, *rest):
@@ -706,10 +701,9 @@
     )(leaf_top, code, table, *rest)
 
 
-def sent_over(block, axis, count):
+def sent_over(block, axis):
     return [block] + [
-        lax.ppermute(block, axis, [(i, (i + s) % count) for i in range(count)])
-        for s in range(1, count)
+        lax.ppermute(block, axis, [(i, i ^ s) for i in range(4)]) for s in range(1, 4)
     ]
 
 
@@ -720,27 +714,29 @@
     pts = particles.reshape(4, PAIRS, 128).transpose(1, 0, 2).reshape(4 * PAIRS, 128)
     tops = leaf_top.reshape(1, LEAVES)
     m2m = m2m_ops.transpose(1, 0, 2)
-    own, low, high, dist, moments, send, partial, mask = call_first(
+    own, near_edge, far_edge, dist, moments, send, partial, mask = call_first(
         pts, counts, leaf_top, tops, m2m
     )
     devices = lax.axis_size(AXES)
-    up = [(i, (i + 1) % devices) for i in range(devices)]
-    down = [(j, i) for i, j in up]
-    over_y = sent_over(send, "y", 4)
-    before = lax.ppermute(high, AXES, up)
-    behind = lax.ppermute(low, AXES, down)
+    partner = [(i, i ^ 1) for i in range(devices)]
+    far = [(i, (i + 2 * (i & 1) - 1) % devices) for i in range(devices)]
+    over_y = sent_over(send, "y")
+    from_partner = lax.ppermute(near_edge, AXES, partner)
+    from_far = lax.ppermute(far_edge, AXES, far)
     ops = call_turn(m2l_ops.transpose(1, 2, 0), send)
-    by_y = call_join(over_y, ops, before, behind)
-    over_x = sent_over(by_y, "x", 4)
-    code, rows = call_halo(leaf_list.T, leaf_class.T, moments, before, behind)
+    by_y = call_join(over_y, ops, from_partner, from_far)
+    over_x = sent_over(by_y, "x")
+    code, rows, top_code = call_halo(
+        leaf_top, top_list.T, top_class.T, leaf_list.T, leaf_class.T, moments,
+        from_partner, from_far,
+    )
     local_a = call_leaf(0, code, ops, rows, by_y)
     by_x = call_join(over_x, local_a)
-    over_z = sent_over(by_x, ("zlo", "zhi"), 4)
-    near = call_near(near_list.T, own, before, behind, by_x)
+    over_z = sent_over(by_x, ("zlo", "zhi"))
+    near = call_near(near_list.T, own, from_partner, from_far, by_x)
     mine = call_join(over_z, near)
     other = lax.ppermute(mine, "core", [(0, 1), (1, 0)])
     local_b = call_leaf(1, code, ops, rows, mine)
-    top_code = call_fetch(leaf_top, top_list.T, top_class.T)
     rest = (ops, m2m, tops, local_a, local_b, dist, near, mask)
     result, over = call_last(leaf_top, top_code, mine, other, *rest)
 

time: 107 us -> 105 us (0.981); the launches traced: 105 us -> 105 us
    pallas_call x1, Pallas kernels: 14.8 us -> 17 us  [call_last(): pl.pallas_call(last_kernel, out_shape=(shape(PAIRS, 128), jax.ShapeDtypeS...]
    ppermute x11, starting transfers between devices: 18.4 us -> 20.3 us  [the longest x9 10.5 us: sent_over(): lax.ppermute(block, axis, [(i, i ^ s) for i in range(4)])]
    pallas_call x1 -> x0, Pallas kernels: 1.54 us -> none  [call_fetch(): pl.pallas_call(fetch_kernel, out_shape=jax.ShapeDtypeStruct((TLIST, 128),...]
    pallas_call x1, Pallas kernels: 10.2 us -> 8.73 us  [call_turn(): pl.pallas_call(turn_kernel, out_shape=shape(CLASSES * OPROWS, 128), in_sp...]
    ppermute x1, starting transfers between devices: 3.82 us -> 2.68 us  [body(): other = lax.ppermute(mine, 'core', [(0, 1), (1, 0)])]
    unnamed x16 -> x20, local copies, waits for them, and re-layouts: 2.28 us -> 2.3 us
  transfers between devices with their start and end apart: 12 -> 12, of which waited for: 0 -> 0; matrix products, arithmetic and copies ran while one was open for 0% -> 0% of each run, Pallas kernels for 58% -> 55%
where the time goes in v5:
time: 105 us
  Pallas kernels  79.1 us (75%)
  starting transfers between devices  23 us (22%)
  local copies, waits for them, and re-layouts  2.3 us (2%)
    pallas_call x1, Pallas kernels, call_near(): pl.pallas_call(near_kernel, out_shape=shape(targets, 128), in_specs=[SMEM...  24 us
    pallas_call x2, Pallas kernels, call_leaf(): pl.pallas_call(functools.partial(leaf_kernel, part), out_shape=shape(2, O...  23.2 us
    pallas_call x1, Pallas kernels, call_last(): pl.pallas_call(last_kernel, out_shape=(shape(PAIRS, 128), jax.ShapeDtypeS...  17 us
    ppermute x9, starting transfers between devices, sent_over(): lax.ppermute(block, axis, [(i, i ^ s) for i in range(4)])  10.5 us
    pallas_call x1, Pallas kernels, call_turn(): pl.pallas_call(turn_kernel, out_shape=shape(CLASSES * OPROWS, 128), in_sp...  8.73 us
    ppermute x1, starting transfers between devices, body(): from_far = lax.ppermute(far_edge, AXES, far)  5.3 us
    ppermute x1, starting transfers between devices, body(): from_partner = lax.ppermute(near_edge, AXES, partner)  4.5 us
    pallas_call x1, Pallas kernels, call_first(): pl.pallas_call(first_kernel, out_shape=(shape(4 * PAIRS, 128), shape(4 *...  3.8 us
  transfers between devices with their start and end apart: 12, of which 0 were waited for; matrix products, arithmetic and copies ran while one was open for 0% of the time, Pallas kernels for 55%

profile of v5, /device:TPU:1, one launch (start us, length us, event | category | flops | bytes accessed | tf_op | source)
XLA Modules:
  0.0 105.4 jit_solution(81562578812134991)
XLA Ops:
  0.0 0.9 copy-done.2
  1.0 0.7 copy-done.4
  1.6 3.8 %expand_own.1 = (f32[512,128]{1,0:T(8,128)S(1)}, f32[64,128]{1,0:T(8,128)S(1)}, f32[64,128]{1,0:T(8,128)S(1)}, f32[3,128,128]{2,1,0:T(8,128)S(1)}, f32[256,128]{...) custom-call(f32[512,128]{1,0:T(8,128)S(1)} %bitcast.22, ...), custom_call_target="tpu_custom_call" | custom-call | flops 1000000000 | bytes 10000000 | tf_op jit(solution)/shard_map/expand_own/pallas_call | solution.py:570
  5.4 4.5 %collective-permute-start.7 = (f32[64,128]{1,0:T(8,128)S(1)}, f32[64,128]{1,0:T(8,128)S(1)}, u32[]{:S(2)}, u32[]{:S(2)}) collective-permute-start(f32[64,128]{1,0:T(8,128)S(1)} %get-tuple-element.61), channel_id=1, source_target_pairs={{0,1},{1,0},{2,3},{3,2},{4,5},{5,4},{6,7},{7,6},{8,9},{9,8},{10,11... | collective-permute-start | bytes 98312 | tf_op jit(solution)/shard_map/ppermute | solution.py:724
  9.9 5.3 %collective-permute-start.8 = (f32[64,128]{1,0:T(8,128)S(1)}, f32[64,128]{1,0:T(8,128)S(1)}, u32[]{:S(2)}, u32[]{:S(2)}) collective-permute-start(f32[64,128]{1,0:T(8,128)S(1)} %get-tuple-element.62), channel_id=1, source_target_pairs={{0,127},{1,2},{2,1},{3,4},{4,3},{5,6},{6,5},{7,8},{8,7},{9,10},{10... | collective-permute-start | bytes 98312 | tf_op jit(solution)/shard_map/ppermute | solution.py:725
  15.2 0.0 collective-permute-start.11
  15.2 0.0 collective-permute-start.10
  15.2 3.2 %collective-permute-start.9 = (f32[56,128]{1,0:T(8,128)S(1)}, f32[56,128]{1,0:T(8,128)S(1)}, u32[]{:S(2)}, u32[]{:S(2)}) collective-permute-start(f32[56,128]{1,0:T(8,128)S(1)} %get-tuple-element.64.after_ref.refs_0_), channel_id=1, source_target_pairs={{0,8},{8,0},{16,24},{24,16},{1,9},{9,1},{17,25},{25,17},{2,10},{10... | collective-permute-start | bytes 86024 | tf_op jit(solution)/shard_map/ppermute | solution.py:706
  18.5 8.7 %turn_operators.3.refs_4_.ops_ref = f32[27808,128]{1,0:T(8,128)S(1)} custom-call(f32[81,81,316]{2,1,0:T(8,128)} %bitcast.24, f32[56,128]{1,0:T(8,128)S(1)} %get-tuple-element.64.after_ref.refs_0_), custom_call_target="tpu_custom_call" | custom-call | flops 10000000 | bytes 30000000 | tf_op jit(solution)/shard_map/turn_operators/pallas_call | solution.py:590
  27.2 0.0 copy-start
  27.2 0.0 copy-start.1
  27.3 0.0 copy-start.6
  27.3 0.0 copy-start.7
  27.3 0.0 copy-start.8
  27.3 0.0 collective-permute-done.11.refs_3_
  27.3 0.0 collective-permute-done.10.refs_2_
  27.3 0.0 collective-permute-done.9.refs_1_
  27.3 0.0 collective-permute-done.7.partner_ref.refs_5_
  27.3 0.0 collective-permute-done.8.far_ref.refs_6_
  27.4 0.1 collective-permute-start.14
  27.5 0.1 collective-permute-start.13
  27.5 3.1 %collective-permute-start.12 = (f32[224,128]{1,0:T(8,128)S(1)}, f32[224,128]{1,0:T(8,128)S(1)}, u32[]{:S(2)}, u32[]{:S(2)}) collective-permute-start(f32[224,128]{1,0:T(8,128)S(1)} %join.3.after_ref.refs_0_), channel_id=1, source_target_pairs={{0,2},{2,0},{4,6},{6,4},{1,3},{3,1},{5,7},{7,5},{8,10},{10,8},{12,... | collective-permute-start | bytes 344072 | tf_op jit(solution)/shard_map/ppermute | solution.py:706
  30.7 0.0 copy-done
  30.7 0.0 copy-done.1
  30.7 0.0 copy-done.6
  30.7 0.0 copy-done.7
  30.7 0.0 copy-done.8
  30.7 2.2 %expand_halo.1 = (s32[16,256]{1,0:T(8,128)S(1)}, f32[320,128]{1,0:T(8,128)S(1)}, s32[64,128]{1,0:T(8,128)S(1)}) custom-call(s32[256]{0:T(256)S(1)} %copy-done.8, s32[64,4096]{1,0:T(8,128)S(1)} %bitcast.29, s32[64,4096]{1,0:T(8,128)S(1)} %bitcast.30, s32[16,256]{1,0:T(8,128)S(1)} %bitcast.20, s32[16,256]{1,0:T(8,128)S(1)} %bitcast.21, ...), custom_call_target="tpu_custom_call" | custom-call | flops 100000000 | bytes 1000000 | tf_op jit(solution)/shard_map/expand_halo/pallas_call | solution.py:636
  32.9 0.0 copy-start.3
  33.0 11.6 %leaf_translate.2.refs_4_.local_a_ref = f32[2,88,128]{2,1,0:T(8,128)S(1)} custom-call(s32[16,256]{1,0:T(8,128)S(1)} %get-tuple-element.65.code_ref, f32[27808,128]{1,0:T(8,128)S(1)} %turn_operators.3.refs_4_.ops_ref, f32[320,128]{1,0:T(8,128)S(1)} %get-tuple-element.66.rows_ref, f32[224,128]{1,0:T(8,128)S(1)} %join.3.after_ref.refs_0_), custom_call_target="tpu_custom_call" | custom-call | flops 214990848 | bytes 20000000 | tf_op jit(solution)/shard_map/leaf_translate/pallas_call | solution.py:660
  44.5 0.0 collective-permute-done.14.refs_3_
  44.6 0.0 collective-permute-done.13.refs_2_
  44.6 0.0 collective-permute-done.12.refs_1_
  44.6 0.1 collective-permute-start.17
  44.7 1.2 %collective-permute-start.16 = (f32[896,128]{1,0:T(8,128)S(1)}, f32[896,128]{1,0:T(8,128)S(1)}, u32[]{:S(2)}, u32[]{:S(2)}) collective-permute-start(f32[896,128]{1,0:T(8,128)S(1)} %join.4.after_ref.refs_0_), channel_id=1, source_target_pairs={{0,64},{1,65},{64,0},{65,1},{2,66},{3,67},{66,2},{67,3},{4,68},{5,... | collective-permute-start | bytes 1376264 | tf_op jit(solution)/shard_map/ppermute | solution.py:706
  45.9 2.6 %collective-permute-start.15 = (f32[896,128]{1,0:T(8,128)S(1)}, f32[896,128]{1,0:T(8,128)S(1)}, u32[]{:S(2)}, u32[]{:S(2)}) collective-permute-start(f32[896,128]{1,0:T(8,128)S(1)} %join.4.after_ref.refs_0_), channel_id=1, source_target_pairs={{0,1},{1,0},{64,65},{65,64},{2,3},{3,2},{66,67},{67,66},{4,5},{5,4... | collective-permute-start | bytes 1376264 | tf_op jit(solution)/shard_map/ppermute | solution.py:706
  48.6 24.0 %near.1.refs_4_.near_ref = f32[128,128]{1,0:T(8,128)S(1)} custom-call(s32[27,256]{1,0:T(8,128)S(1)} %bitcast.23, f32[512,128]{1,0:T(8,128)S(1)} %get-tuple-element.67.own_ref, f32[64,128]{1,0:T(8,128)S(1)} %collective-permute-done.7.partner_ref.refs_5_, f32[64,128]{1,0:T(8,128)S(1)} %collective-permute-done.8.far_ref.refs_6_, ...), custom_call_target="tpu_custom_call" | custom-call | flops 283115520 | bytes 30000000 | tf_op jit(solution)/shard_map/near/pallas_call | solution.py:616
  72.5 0.0 collective-permute-done.17.refs_3_
  72.6 0.0 collective-permute-done.16.refs_2_
  72.6 0.0 collective-permute-done.15.refs_1_
  72.6 0.1 join.5.after_ref.mine_ref
  72.7 0.0 copy-start.5
  72.7 2.7 %collective-permute-start.18 = (f32[3584,128]{1,0:T(8,128)S(1)}, f32[3584,128]{1,0:T(8,128)S(1)}, u32[]{:S(2)}, u32[]{:S(2)}) collective-permute-start(f32[3584,128]{1,0:T(8,128)S(1)} %join.5.after_ref.mine_ref), channel_id=1, source_target_pairs={{0,32},{32,0},{1,33},{33,1},{2,34},{34,2},{3,35},{35,3},{4,36},{36... | collective-permute-start | bytes 5505032 | tf_op jit(solution)/shard_map/ppermute | solution.py:738
  75.4 11.6 %leaf_translate.3.local_b_ref = f32[2,88,128]{2,1,0:T(8,128)S(1)} custom-call(s32[16,256]{1,0:T(8,128)S(1)} %get-tuple-element.65.code_ref, f32[27808,128]{1,0:T(8,128)S(1)} %turn_operators.3.refs_4_.ops_ref, f32[320,128]{1,0:T(8,128)S(1)} %get-tuple-element.66.rows_ref, f32[3584,128]{1,0:T(8,128)S(1)} %join.5.after_ref.mine_ref), custom_call_target="tpu_custom_call" | custom-call | flops 214990848 | bytes 20000000 | tf_op jit(solution)/shard_map/leaf_translate/pallas_call | solution.py:660
  87.0 0.0 collective-permute-done.18.other_ref
  87.1 17.0 %finish.1 = (f32[128,128]{1,0:T(8,128)S(1)}, s32[1]{0:T(128)}) custom-call(s32[256]{0:T(256)S(1)} %copy-done.8, s32[64,128]{1,0:T(8,128)S(1)} %get-tuple-element.63.code_ref, f32[3584,128]{1,0:T(8,128)S(1)} %join.5.after_ref.mine_ref, f32[3584,128]{1,0:T(8,128)S(1)} %collective-permute-done.18.other_ref, f32[27808,128]{1,0:T(8,128)S(1)} %turn_operators.3.refs_4_.ops_ref, ...), custom_call_target="tpu_custom_call" | custom-call | tf_op jit(solution)/shard_map/finish/pallas_call | solution.py:673
  104.7 0.0 copy-start.9
  104.7 0.6 copy-done.9
  (7 shorter events, 0.1 us)
Async XLA Ops:
  0.0 0.9 copy-start.2
  1.0 0.7 copy-start.4
  5.4 21.9 %collective-permute-start.7 = (f32[64,128]{1,0:T(8,128)S(1)}, f32[64,128]{1,0:T(8,128)S(1)}, u32[]{:S(2)}, u32[]{:S(2)}) collective-permute-start(f32[64,128]{1,0:T(8,128)S(1)} %get-tuple-element.61), channel_id=1, source_target_pairs={{0,1},{1,0},{2,3},{3,2},{4,5},{5,4},{6,7},{7,6},{8,9},{9,8},{10,11... | collective-permute-start | bytes 98312 | tf_op jit(solution)/shard_map/ppermute | solution.py:724
  9.9 17.4 %collective-permute-start.8 = (f32[64,128]{1,0:T(8,128)S(1)}, f32[64,128]{1,0:T(8,128)S(1)}, u32[]{:S(2)}, u32[]{:S(2)}) collective-permute-start(f32[64,128]{1,0:T(8,128)S(1)} %get-tuple-element.62), channel_id=1, source_target_pairs={{0,127},{1,2},{2,1},{3,4},{4,3},{5,6},{6,5},{7,8},{8,7},{9,10},{10... | collective-permute-start | bytes 98312 | tf_op jit(solution)/shard_map/ppermute | solution.py:725
  15.2 12.1 %collective-permute-start.11 = (f32[56,128]{1,0:T(8,128)S(1)}, f32[56,128]{1,0:T(8,128)S(1)}, u32[]{:S(2)}, u32[]{:S(2)}) collective-permute-start(f32[56,128]{1,0:T(8,128)S(1)} %get-tuple-element.64.after_ref.refs_0_), channel_id=1, source_target_pairs={{0,24},{8,16},{16,8},{24,0},{1,25},{9,17},{17,9},{25,1},{2,26},{10... | collective-permute-start | bytes 86024 | tf_op jit(solution)/shard_map/ppermute | solution.py:706
  15.2 12.1 %collective-permute-start.10 = (f32[56,128]{1,0:T(8,128)S(1)}, f32[56,128]{1,0:T(8,128)S(1)}, u32[]{:S(2)}, u32[]{:S(2)}) collective-permute-start(f32[56,128]{1,0:T(8,128)S(1)} %get-tuple-element.64.after_ref.refs_0_), channel_id=1, source_target_pairs={{0,16},{8,24},{16,0},{24,8},{1,17},{9,25},{17,1},{25,9},{2,18},{10... | collective-permute-start | bytes 86024 | tf_op jit(solution)/shard_map/ppermute | solution.py:706
  15.2 12.1 %collective-permute-start.9 = (f32[56,128]{1,0:T(8,128)S(1)}, f32[56,128]{1,0:T(8,128)S(1)}, u32[]{:S(2)}, u32[]{:S(2)}) collective-permute-start(f32[56,128]{1,0:T(8,128)S(1)} %get-tuple-element.64.after_ref.refs_0_), channel_id=1, source_target_pairs={{0,8},{8,0},{16,24},{24,16},{1,9},{9,1},{17,25},{25,17},{2,10},{10... | collective-permute-start | bytes 86024 | tf_op jit(solution)/shard_map/ppermute | solution.py:706
  27.2 3.5 %copy-start = (s32[256,16]{0,1:T(8,128)S(1)}, s32[256,16]{0,1:T(8,128)}, u32[]{:S(2)}) copy-start(s32[256,16]{0,1:T(8,128)} %param.16) | copy-start | bytes 49156
  27.2 3.5 %copy-start.1 = (s32[256,16]{0,1:T(8,128)S(1)}, s32[256,16]{0,1:T(8,128)}, u32[]{:S(2)}) copy-start(s32[256,16]{0,1:T(8,128)} %param.17) | copy-start | bytes 49156
  27.3 3.5 %copy-start.6 = (s32[4096,64]{0,1:T(8,128)S(1)}, s32[4096,64]{0,1:T(8,128)}, u32[]{:S(2)}) copy-start(s32[4096,64]{0,1:T(8,128)} %param.18) | copy-start | bytes 3145732
  27.3 3.4 %copy-start.7 = (s32[4096,64]{0,1:T(8,128)S(1)}, s32[4096,64]{0,1:T(8,128)}, u32[]{:S(2)}) copy-start(s32[4096,64]{0,1:T(8,128)} %param.19) | copy-start | bytes 3145732
  27.3 3.4 %copy-start.8 = (s32[256]{0:T(256)S(1)}, s32[256]{0:T(256)}, u32[]{:S(2)}) copy-start(s32[256]{0:T(256)} %top_ref.5) | copy-start | bytes 3076
  27.4 17.2 %collective-permute-start.14 = (f32[224,128]{1,0:T(8,128)S(1)}, f32[224,128]{1,0:T(8,128)S(1)}, u32[]{:S(2)}, u32[]{:S(2)}) collective-permute-start(f32[224,128]{1,0:T(8,128)S(1)} %join.3.after_ref.refs_0_), channel_id=1, source_target_pairs={{0,6},{2,4},{4,2},{6,0},{1,7},{3,5},{5,3},{7,1},{8,14},{10,12},{12... | collective-permute-start | bytes 344072 | tf_op jit(solution)/shard_map/ppermute | solution.py:706
  27.5 17.1 %collective-permute-start.13 = (f32[224,128]{1,0:T(8,128)S(1)}, f32[224,128]{1,0:T(8,128)S(1)}, u32[]{:S(2)}, u32[]{:S(2)}) collective-permute-start(f32[224,128]{1,0:T(8,128)S(1)} %join.3.after_ref.refs_0_), channel_id=1, source_target_pairs={{0,4},{2,6},{4,0},{6,2},{1,5},{3,7},{5,1},{7,3},{8,12},{10,14},{12... | collective-permute-start | bytes 344072 | tf_op jit(solution)/shard_map/ppermute | solution.py:706
  27.5 17.0 %collective-permute-start.12 = (f32[224,128]{1,0:T(8,128)S(1)}, f32[224,128]{1,0:T(8,128)S(1)}, u32[]{:S(2)}, u32[]{:S(2)}) collective-permute-start(f32[224,128]{1,0:T(8,128)S(1)} %join.3.after_ref.refs_0_), channel_id=1, source_target_pairs={{0,2},{2,0},{4,6},{6,4},{1,3},{3,1},{5,7},{7,5},{8,10},{10,8},{12,... | collective-permute-start | bytes 344072 | tf_op jit(solution)/shard_map/ppermute | solution.py:706
  32.9 15.6 %copy-start.3 = (s32[256,27]{0,1:T(8,128)S(1)}, s32[256,27]{0,1:T(8,128)}, u32[]{:S(2)}) copy-start(s32[256,27]{0,1:T(8,128)} %param.15) | copy-start | bytes 82948
  44.6 27.9 %collective-permute-start.17 = (f32[896,128]{1,0:T(8,128)S(1)}, f32[896,128]{1,0:T(8,128)S(1)}, u32[]{:S(2)}, u32[]{:S(2)}) collective-permute-start(f32[896,128]{1,0:T(8,128)S(1)} %join.4.after_ref.refs_0_), channel_id=1, source_target_pairs={{0,65},{1,64},{64,1},{65,0},{2,67},{3,66},{66,3},{67,2},{4,69},{5,... | collective-permute-start | bytes 1376264 | tf_op jit(solution)/shard_map/ppermute | solution.py:706
  44.7 27.9 %collective-permute-start.16 = (f32[896,128]{1,0:T(8,128)S(1)}, f32[896,128]{1,0:T(8,128)S(1)}, u32[]{:S(2)}, u32[]{:S(2)}) collective-permute-start(f32[896,128]{1,0:T(8,128)S(1)} %join.4.after_ref.refs_0_), channel_id=1, source_target_pairs={{0,64},{1,65},{64,0},{65,1},{2,66},{3,67},{66,2},{67,3},{4,68},{5,... | collective-permute-start | bytes 1376264 | tf_op jit(solution)/shard_map/ppermute | solution.py:706
  45.9 26.7 %collective-permute-start.15 = (f32[896,128]{1,0:T(8,128)S(1)}, f32[896,128]{1,0:T(8,128)S(1)}, u32[]{:S(2)}, u32[]{:S(2)}) collective-permute-start(f32[896,128]{1,0:T(8,128)S(1)} %join.4.after_ref.refs_0_), channel_id=1, source_target_pairs={{0,1},{1,0},{64,65},{65,64},{2,3},{3,2},{66,67},{67,66},{4,5},{5,4... | collective-permute-start | bytes 1376264 | tf_op jit(solution)/shard_map/ppermute | solution.py:706
  72.7 14.3 %copy-start.5 = (f32[8,81,81]{2,0,1:T(8,128)S(1)}, f32[8,81,81]{2,0,1:T(8,128)}, u32[]{:S(2)}) copy-start(f32[8,81,81]{2,0,1:T(8,128)} %param.21) | copy-start | bytes 629860
  72.7 14.3 %collective-permute-start.18 = (f32[3584,128]{1,0:T(8,128)S(1)}, f32[3584,128]{1,0:T(8,128)S(1)}, u32[]{:S(2)}, u32[]{:S(2)}) collective-permute-start(f32[3584,128]{1,0:T(8,128)S(1)} %join.5.after_ref.mine_ref), channel_id=1, source_target_pairs={{0,32},{32,0},{1,33},{33,1},{2,34},{34,2},{3,35},{35,3},{4,36},{36... | collective-permute-start | bytes 5505032 | tf_op jit(solution)/shard_map/ppermute | solution.py:738
  104.7 0.6 copy-start.9

commit v6 on v5

--- a/solution.py
+++ b/solution.py
@@ -28,7 +28,7 @@
 FEAT = 32
 FEATS = 24
 LEAF_STEP = 4
-TURN_STEP = 9
+TURN_STEP = 27
 TOP_WINDOW = 256
 BUILD_STEP = 16
 NEAR_STEP = 32
@@ -123,15 +123,15 @@
 
 def first_kernel(
     pts_ref, count_ref, top_ref, tops_ref, m2m_ref,
-    own_ref, near_edge_ref, far_edge_ref, dist_ref, moment_ref, send_ref, part_ref, mask_ref,
-    q_ref, acc_ref, lift_ref,
+    own_ref, near_edge_ref, far_edge_ref, dist_ref, moment_ref, send_ref, lift_ref, mask_ref,
+    q_ref, acc_ref,
 ):
     lane = lanes((1, 128))
 
     def hold(i, carry):
         for u in range(8):
             r = i * 8 + u
-            held = jnp.where(lane < PART, count_ref[2 * r], count_ref[2 * r + 1])
+            held = jnp.where(lane < PART, count_ref[0, 2 * r], count_ref[0, 2 * r + 1])
             mask_ref[pl.ds(r, 1), :] = jnp.where((lane & (PART - 1)) < held, 1.0, 0.0)
         return carry
 
@@ -151,13 +151,12 @@
     for a in range(8):
         at = pl.ds(a, LEAVES // 8, stride=8)
         lift_ref[at, :] = widen(dot_f32(moment_ref[at, :][:, :COEF], m2m_ref[:, a, :], NT))
-    held = jnp.where(rows_of((LEAVES, LEAVES)) == tops_ref[...] - first, 1.0, 0.0)
+    held = jnp.where(rows_of((SEND, LEAVES)) == tops_ref[...] - first, 1.0, 0.0)
     wide = dot_f32(held, lift_ref[...])
-    lane = lanes((LEAVES, 128))
+    lane = lanes((SEND, 128))
     wide = jnp.where(lane == 127, first.astype(jnp.float32), wide)
     wide = jnp.where(lane == 126, last.astype(jnp.float32), wide)
-    part_ref[...] = wide
-    send_ref[...] = wide[:SEND]
+    send_ref[...] = wide
 
 
 def turn_kernel(in_ref, after_ref, out_ref):
@@ -191,12 +190,14 @@
 
 
 def near_kernel(
-    near_ref, own_ref, partner_ref, far_ref, after_ref, out_ref,
-    win_ref, src_ref, tgt_ref, source_ref, target_ref, charge_ref,
+    list_ref, own_ref, partner_ref, far_ref, after_ref, out_ref,
+    win_ref, src_ref, tgt_ref, source_ref, target_ref, charge_ref, near_ref, sem,
 ):
     del after_ref
     targets, width = PAIRS, WPAIRS
     edge = 4 * HPAIRS
+    lists = pltpu.make_async_copy(list_ref, near_ref, sem)
+    lists.start()
     even = lax.axis_index("zhi") == 0
     win_ref[:edge] = jnp.where(even, far_ref[...], partner_ref[...])
     win_ref[edge : edge + 4 * PAIRS] = own_ref[...]
@@ -263,6 +264,7 @@
 
         lax.fori_loop(0, width // BUILD_STEP, build_source, 0)
         lax.fori_loop(0, targets // BUILD_STEP, build_target, 0)
+        lists.wait()
 
         low_block = lanes((FEAT, 128)) < PART
         low_row = lanes((1, 128)) < PART
@@ -303,6 +305,7 @@
     @pl.when(jnp.logical_not(close))
     def _():
         lane = lanes((PART, 128))
+        lists.wait()
 
         def pair(r, carry):
             columns = [
@@ -354,7 +357,7 @@
 
 def halo_kernel(
     top_ref, top_list_ref, top_class_ref,
-    list_ref, class_ref, moment_ref, partner_ref, far_ref, code_ref, rows_ref, top_code_ref,
+    list_ref, class_ref, moment_ref, partner_ref, far_ref, code_a_ref, code_b_ref, rows_ref, top_code_ref,
     d_ref, q_ref, acc_ref, halo_ref, list_vmem, class_vmem, sems,
 ):
     window = pl.ds(pl.multiple_of(window_start(top_ref), 128), TOP_WINDOW)
@@ -366,7 +369,9 @@
         copy.start()
     even = lax.axis_index("zhi") == 0
     shift = lax.axis_index(AXES) * LEAVES - HALO
-    code_ref[...] = pack_codes(class_ref[...], list_ref[...] - shift)
+    packed = pack_codes(class_ref[...], list_ref[...] - shift)
+    code_a_ref[...] = packed[:, : LEAVES // 2]
+    code_b_ref[...] = packed[:, LEAVES // 2 :]
     fill = jnp.zeros((PAIRS - 2 * HPAIRS, 128), jnp.float32)
 
     def component(c):
@@ -406,7 +411,7 @@
     def step(i, carry):
         reduce(i - 1)
         for v in range(LEAF_STEP):
-            leaf = 2 * begin + i * LEAF_STEP + v
+            leaf = i * LEAF_STEP + v
             total_ref[v] = gather_products(
                 [code_ref[k, leaf] for k in range(LLIST)], ops_ref, rows_ref
             )
@@ -424,11 +429,11 @@
 
 
 def finish(
-    cap, shift, top_ref, code_ref, table_ref, ops_ref, m2m_ref, tops_ref, local_refs, dist_ref,
+    cap, shift, ends, code_ref, table_ref, ops_ref, m2m_ref, tops_ref, local_refs, dist_ref,
     near_ref, mask_ref, out_ref, field_ref, pot_ref, total_ref, wide_ref, rows_ref,
 ):
-    first = top_ref[0]
-    boxes = top_ref[LEAVES - 1] - first + 1
+    first, last = ends
+    boxes = last - first + 1
     spread = jnp.zeros((OPROWS, LEAVES), jnp.float32)
     width = min(cap, 128)
     for block in range(cap // width):
@@ -477,21 +482,24 @@
 
 
 def last_kernel(
-    top_ref, code_ref, mine_ref, other_ref, ops_ref, m2m_ref, tops_ref, local_a_ref, local_b_ref,
+    code_ref, mine_ref, other_ref, ops_ref, m2m_ref, tops_ref, local_a_ref, local_b_ref,
     dist_ref, near_ref, mask_ref, out_ref, over_ref,
-    table_ref, rest_ref, meta_ref, ends_ref, packed_ref, scalar_ref, sems, *scratch,
+    most_ref, table_ref, rest_ref, meta_ref, ends_ref, packed_ref, scalar_ref, sems, *scratch,
 ):
     half = mine_ref.shape[0]
     blocks = half // SEND
-    table_ref[:half] = mine_ref[...]
-    table_ref[half:] = other_ref[...]
     heads = pl.ds(0, 2 * blocks, stride=SEND)
-    turned = table_ref[heads, :].T[120:]
+    some = pl.ds(0, blocks, stride=SEND)
+    turned = jnp.concatenate([mine_ref[some, :], other_ref[some, :]], axis=0).T[120:]
     meta_ref[...] = turned.astype(jnp.int32)
     copy = pltpu.make_async_copy(meta_ref, ends_ref, sems.at[0])
     copy.start()
+    table_ref[:half] = mine_ref[...]
+    table_ref[half:] = other_ref[...]
     most = jnp.max(turned[6:7] - turned[7:8]).astype(jnp.int32) + 1
-    over_ref[0] = most
+    most_ref[0] = most
+    tell = pltpu.make_async_copy(most_ref, over_ref, sems.at[2])
+    tell.start()
     core, my_y, my_x = lax.axis_index("core"), lax.axis_index("y"), lax.axis_index("x")
     my_z = lax.axis_index(("zlo", "zhi"))
     by_z = [(my_z ^ z) * 16 for z in range(4)]
@@ -527,9 +535,11 @@
         table_ref[heads, :] += rest_ref[...]
         copy.wait()
         finish(
-            64, 0, top_ref, scalar_ref, table_ref, ops_ref, m2m_ref, tops_ref,
+            64, 0, (ends_ref[7, 0], ends_ref[6, 0]), scalar_ref, table_ref, ops_ref, m2m_ref, tops_ref,
             (local_a_ref, local_b_ref), dist_ref, near_ref, mask_ref, out_ref, *scratch,
         )
+
+    tell.wait()
 
 
 def spare_kernel(
@@ -537,7 +547,8 @@
     dist_ref, near_ref, mask_ref, out_ref, *scratch,
 ):
     finish(
-        LEAVES, top_ref[0] - jnp.minimum(top_ref[0], TOPBOX - LEAVES), top_ref, code_ref, table_ref, ops_ref, m2m_ref, tops_ref,
+        LEAVES, top_ref[0] - jnp.minimum(top_ref[0], TOPBOX - LEAVES),
+        (top_ref[0], top_ref[LEAVES - 1]), code_ref, table_ref, ops_ref, m2m_ref, tops_ref,
         (local_a_ref, local_b_ref), dist_ref, near_ref, mask_ref, out_ref, *scratch,
     )
 
@@ -578,7 +589,6 @@
         out_specs=(VMEM,) * 8,
         scratch_shapes=[
             pltpu.VMEM((128, 128), F32), pltpu.VMEM((COEF, 8, 128), F32),
-            pltpu.VMEM((LEAVES, 128), F32),
         ],
         compiler_params=pltpu.CompilerParams(vmem_limit_bytes=16 * MIB),
         cost_estimate=cost(10**9, 10**7),
@@ -616,7 +626,7 @@
     return pl.pallas_call(
         near_kernel,
         out_shape=shape(targets, 128),
-        in_specs=[SMEM, VMEM, VMEM, VMEM, ANY],
+        in_specs=[VMEM, VMEM, VMEM, VMEM, ANY],
         out_specs=VMEM,
         scratch_shapes=[
             pltpu.VMEM((4 * WPAIRS, 128), F32),
@@ -625,6 +635,8 @@
             pltpu.VMEM((2 * width, FEAT, 128), jnp.bfloat16),
             pltpu.VMEM((LEAVES, PART, FEAT), jnp.bfloat16),
             pltpu.VMEM((2 * width, 128), F32),
+            pltpu.SMEM((NEAR, LEAVES), jnp.int32),
+            pltpu.SemaphoreType.DMA,
         ],
         compiler_params=pltpu.CompilerParams(vmem_limit_bytes=24 * MIB),
         cost_estimate=cost(10 * targets * 2 * 64 * NEAR * 64, 3 * 10**7),
@@ -636,11 +648,12 @@
     return pl.pallas_call(
         halo_kernel,
         out_shape=(
-            jax.ShapeDtypeStruct((LLIST, LEAVES), jnp.int32), shape(2 * WPAIRS, 128),
+            jax.ShapeDtypeStruct((LLIST, LEAVES // 2), jnp.int32),
+            jax.ShapeDtypeStruct((LLIST, LEAVES // 2), jnp.int32), shape(2 * WPAIRS, 128),
             jax.ShapeDtypeStruct((TLIST, 128), jnp.int32),
         ),
         in_specs=[SMEM, HBM, HBM] + [VMEM] * 5,
-        out_specs=(VMEM,) * 3,
+        out_specs=(VMEM,) * 4,
         scratch_shapes=[
             pltpu.VMEM((3, 128, 128), F32),
             pltpu.VMEM((128, 128), F32),
@@ -669,24 +682,25 @@
     )(code, ops, rows, after)
 
 
-def call_last(leaf_top, code, mine, other, *rest):
+def call_last(code, mine, other, *rest):
     return pl.pallas_call(
         last_kernel,
         out_shape=(shape(PAIRS, 128), jax.ShapeDtypeStruct((1,), jnp.int32)),
-        in_specs=[SMEM] + [VMEM] * 11,
-        out_specs=(VMEM, SMEM),
+        in_specs=[VMEM] * 11,
+        out_specs=(VMEM, ANY),
         scratch_shapes=[
+            pltpu.SMEM((1,), jnp.int32),
             pltpu.VMEM((2 * mine.shape[0], 128), F32),
             pltpu.VMEM((2 * mine.shape[0] // SEND, 128), F32),
             pltpu.VMEM((8, 128), jnp.int32),
             pltpu.SMEM((8, 128), jnp.int32),
             pltpu.VMEM((TLIST, 128), jnp.int32),
             pltpu.SMEM((TLIST, 128), jnp.int32),
-            pltpu.SemaphoreType.DMA((2,)),
+            pltpu.SemaphoreType.DMA((3,)),
         ] + FINISH_SCRATCH,
         compiler_params=pltpu.CompilerParams(vmem_limit_bytes=24 * MIB),
         name="finish",
-    )(leaf_top, code, mine, other, *rest)
+    )(code, mine, other, *rest)
 
 
 def call_spare(leaf_top, code, table, *rest):
@@ -714,8 +728,8 @@
     pts = particles.reshape(4, PAIRS, 128).transpose(1, 0, 2).reshape(4 * PAIRS, 128)
     tops = leaf_top.reshape(1, LEAVES)
     m2m = m2m_ops.transpose(1, 0, 2)
-    own, near_edge, far_edge, dist, moments, send, partial, mask = call_first(
-        pts, counts, leaf_top, tops, m2m
+    own, near_edge, far_edge, dist, moments, send, lifted, mask = call_first(
+        pts, counts.reshape(1, LEAVES), leaf_top, tops, m2m
     )
     devices = lax.axis_size(AXES)
     partner = [(i, i ^ 1) for i in range(devices)]
@@ -726,21 +740,23 @@
     ops = call_turn(m2l_ops.transpose(1, 2, 0), send)
     by_y = call_join(over_y, ops, from_partner, from_far)
     over_x = sent_over(by_y, "x")
-    code, rows, top_code = call_halo(
+    code_a, code_b, rows, top_code = call_halo(
         leaf_top, top_list.T, top_class.T, leaf_list.T, leaf_class.T, moments,
         from_partner, from_far,
     )
-    local_a = call_leaf(0, code, ops, rows, by_y)
+    local_a = call_leaf(0, code_a, ops, rows, by_y)
     by_x = call_join(over_x, local_a)
     over_z = sent_over(by_x, ("zlo", "zhi"))
     near = call_near(near_list.T, own, from_partner, from_far, by_x)
     mine = call_join(over_z, near)
     other = lax.ppermute(mine, "core", [(0, 1), (1, 0)])
-    local_b = call_leaf(1, code, ops, rows, mine)
+    local_b = call_leaf(1, code_b, ops, rows, mine)
     rest = (ops, m2m, tops, local_a, local_b, dist, near, mask)
-    result, over = call_last(leaf_top, top_code, mine, other, *rest)
+    result, over = call_last(top_code, mine, other, *rest)
 
     def spare():
+        held = jnp.arange(LEAVES, dtype=jnp.int32)[:, None] == (leaf_top - leaf_top[0])[None]
+        partial = jnp.matmul(held.astype(F32), lifted, precision=HIGH)
         table = lax.dynamic_update_slice(
             jnp.zeros((TOPBOX + LEAVES, 128), F32), partial, (leaf_top[0], 0)
         )

time: 105 us -> 101 us (0.962)
  Pallas kernels: 79.1 us -> 74.3 us
    pallas_call x1, Pallas kernels: 17 us -> 13.8 us  [call_last(): pl.pallas_call(last_kernel, out_shape=(shape(PAIRS, 128), jax.ShapeDtypeS...]
  transfers between devices with their start and end apart: 12 -> 12, of which waited for: 0 -> 0; matrix products, arithmetic and copies ran while one was open for 0% -> 0% of each run, Pallas kernels for 55% -> 56%
where the time goes in v6:
time: 101 us
  Pallas kernels  74.3 us (74%)
  starting transfers between devices  23 us (23%)
  local copies, waits for them, and re-layouts  2.29 us (2%)
    pallas_call x2, Pallas kernels, call_leaf(): pl.pallas_call(functools.partial(leaf_kernel, part), out_shape=shape(2, O...  23.2 us
    pallas_call x1, Pallas kernels, call_near(): pl.pallas_call(near_kernel, out_shape=shape(targets, 128), in_specs=[VMEM...  23 us
    pallas_call x1, Pallas kernels, call_last(): pl.pallas_call(last_kernel, out_shape=(shape(PAIRS, 128), jax.ShapeDtypeS...  13.8 us
    ppermute x9, starting transfers between devices, sent_over(): lax.ppermute(block, axis, [(i, i ^ s) for i in range(4)])  10.5 us
    pallas_call x1, Pallas kernels, call_turn(): pl.pallas_call(turn_kernel, out_shape=shape(CLASSES * OPROWS, 128), in_sp...  8.29 us
    ppermute x1, starting transfers between devices, body(): from_far = lax.ppermute(far_edge, AXES, far)  5.3 us
    ppermute x1, starting transfers between devices, body(): from_partner = lax.ppermute(near_edge, AXES, partner)  4.51 us
    pallas_call x1, Pallas kernels, call_first(): pl.pallas_call(first_kernel, out_shape=(shape(4 * PAIRS, 128), shape(4 *...  3.63 us
  transfers between devices with their start and end apart: 12, of which 0 were waited for; matrix products, arithmetic and copies ran while one was open for 0% of the time, Pallas kernels for 56%

profile of v6, /device:TPU:1, one launch (start us, length us, event | category | flops | bytes accessed | tf_op | source)
XLA Modules:
  0.0 100.5 jit_solution(5893764072961972856)
XLA Ops:
  0.0 0.9 copy-done.2
  1.0 0.7 copy-done.4
  1.6 3.6 %expand_own.1 = (f32[512,128]{1,0:T(8,128)S(1)}, f32[64,128]{1,0:T(8,128)S(1)}, f32[64,128]{1,0:T(8,128)S(1)}, f32[3,128,128]{2,1,0:T(8,128)S(1)}, f32[256,128]{...) custom-call(f32[512,128]{1,0:T(8,128)S(1)} %bitcast.24, ...), custom_call_target="tpu_custom_call" | custom-call | flops 1000000000 | bytes 10000000 | tf_op jit(solution)/shard_map/expand_own/pallas_call | solution.py:581
  5.3 4.5 %collective-permute-start.7 = (f32[64,128]{1,0:T(8,128)S(1)}, f32[64,128]{1,0:T(8,128)S(1)}, u32[]{:S(2)}, u32[]{:S(2)}) collective-permute-start(f32[64,128]{1,0:T(8,128)S(1)} %get-tuple-element.62), channel_id=1, source_target_pairs={{0,1},{1,0},{2,3},{3,2},{4,5},{5,4},{6,7},{7,6},{8,9},{9,8},{10,11... | collective-permute-start | bytes 98312 | tf_op jit(solution)/shard_map/ppermute | solution.py:738
  9.8 5.3 %collective-permute-start.8 = (f32[64,128]{1,0:T(8,128)S(1)}, f32[64,128]{1,0:T(8,128)S(1)}, u32[]{:S(2)}, u32[]{:S(2)}) collective-permute-start(f32[64,128]{1,0:T(8,128)S(1)} %get-tuple-element.63), channel_id=1, source_target_pairs={{0,127},{1,2},{2,1},{3,4},{4,3},{5,6},{6,5},{7,8},{8,7},{9,10},{10... | collective-permute-start | bytes 98312 | tf_op jit(solution)/shard_map/ppermute | solution.py:739
  15.1 0.0 collective-permute-start.11
  15.1 0.0 collective-permute-start.10
  15.1 3.2 %collective-permute-start.9 = (f32[56,128]{1,0:T(8,128)S(1)}, f32[56,128]{1,0:T(8,128)S(1)}, u32[]{:S(2)}, u32[]{:S(2)}) collective-permute-start(f32[56,128]{1,0:T(8,128)S(1)} %get-tuple-element.65.after_ref.refs_0_), channel_id=1, source_target_pairs={{0,8},{8,0},{16,24},{24,16},{1,9},{9,1},{17,25},{25,17},{2,10},{10... | collective-permute-start | bytes 86024 | tf_op jit(solution)/shard_map/ppermute | solution.py:720
  18.3 8.3 %turn_operators.3.refs_4_.ops_ref = f32[27808,128]{1,0:T(8,128)S(1)} custom-call(f32[81,81,316]{2,1,0:T(8,128)} %bitcast.27, f32[56,128]{1,0:T(8,128)S(1)} %get-tuple-element.65.after_ref.refs_0_), custom_call_target="tpu_custom_call" | custom-call | flops 10000000 | bytes 30000000 | tf_op jit(solution)/shard_map/turn_operators/pallas_call | solution.py:600
  26.6 0.0 copy-start
  26.6 0.0 copy-start.1
  26.6 0.0 copy-start.6
  26.7 0.0 copy-start.7
  26.7 0.0 copy-start.8
  26.7 0.0 collective-permute-done.11.refs_3_
  26.7 0.0 collective-permute-done.10.refs_2_
  26.7 0.0 collective-permute-done.9.refs_1_
  26.7 0.0 collective-permute-done.7.partner_ref.refs_5_
  26.7 0.0 collective-permute-done.8.far_ref.refs_6_
  26.8 0.1 collective-permute-start.14
  26.8 0.1 collective-permute-start.13
  26.9 3.1 %collective-permute-start.12 = (f32[224,128]{1,0:T(8,128)S(1)}, f32[224,128]{1,0:T(8,128)S(1)}, u32[]{:S(2)}, u32[]{:S(2)}) collective-permute-start(f32[224,128]{1,0:T(8,128)S(1)} %join.3.after_ref.refs_0_), channel_id=1, source_target_pairs={{0,2},{2,0},{4,6},{6,4},{1,3},{3,1},{5,7},{7,5},{8,10},{10,8},{12,... | collective-permute-start | bytes 344072 | tf_op jit(solution)/shard_map/ppermute | solution.py:720
  30.1 0.0 copy-done
  30.1 0.0 copy-done.1
  30.1 0.0 copy-done.6
  30.1 0.0 copy-done.7
  30.1 0.0 copy-done.8
  30.1 2.2 %expand_halo.1 = (s32[16,128]{1,0:T(8,128)S(1)}, s32[16,128]{1,0:T(8,128)S(1)}, f32[320,128]{1,0:T(8,128)S(1)}, s32[64,128]{1,0:T(8,128)S(1)}) custom-call(s32[256]{0:T(256)S(1)} %copy-done.8, s32[64,4096]{1,0:T(8,128)S(1)} %bitcast.32, s32[64,4096]{1,0:T(8,128)S(1)} %bitcast.33, s32[16,256]{1,0:T(8,128)S(1)} %bitcast.22, s32[16,256]{1,0:T(8,128)S(1)} %bitcast.23, ...), custom_call_target="tpu_custom_call" | custom-call | flops 100000000 | bytes 1000000 | tf_op jit(solution)/shard_map/expand_halo/pallas_call | solution.py:648
  32.3 0.0 copy-start.3
  32.3 11.6 %leaf_translate.2.refs_4_.local_a_ref = f32[2,88,128]{2,1,0:T(8,128)S(1)} custom-call(s32[16,128]{1,0:T(8,128)S(1)} %get-tuple-element.66.code_ref, f32[27808,128]{1,0:T(8,128)S(1)} %turn_operators.3.refs_4_.ops_ref, f32[320,128]{1,0:T(8,128)S(1)} %get-tuple-element.67.rows_ref, f32[224,128]{1,0:T(8,128)S(1)} %join.3.after_ref.refs_0_), custom_call_target="tpu_custom_call" | custom-call | flops 214990848 | bytes 20000000 | tf_op jit(solution)/shard_map/leaf_translate/pallas_call | solution.py:673
  43.9 0.0 collective-permute-done.14.refs_3_
  43.9 0.0 collective-permute-done.13.refs_2_
  44.0 0.0 collective-permute-done.12.refs_1_
  44.0 0.1 collective-permute-start.17
  44.1 1.3 %collective-permute-start.16 = (f32[896,128]{1,0:T(8,128)S(1)}, f32[896,128]{1,0:T(8,128)S(1)}, u32[]{:S(2)}, u32[]{:S(2)}) collective-permute-start(f32[896,128]{1,0:T(8,128)S(1)} %join.4.after_ref.refs_0_), channel_id=1, source_target_pairs={{0,64},{1,65},{64,0},{65,1},{2,66},{3,67},{66,2},{67,3},{4,68},{5,... | collective-permute-start | bytes 1376264 | tf_op jit(solution)/shard_map/ppermute | solution.py:720
  45.4 2.6 %collective-permute-start.15 = (f32[896,128]{1,0:T(8,128)S(1)}, f32[896,128]{1,0:T(8,128)S(1)}, u32[]{:S(2)}, u32[]{:S(2)}) collective-permute-start(f32[896,128]{1,0:T(8,128)S(1)} %join.4.after_ref.refs_0_), channel_id=1, source_target_pairs={{0,1},{1,0},{64,65},{65,64},{2,3},{3,2},{66,67},{67,66},{4,5},{5,4... | collective-permute-start | bytes 1376264 | tf_op jit(solution)/shard_map/ppermute | solution.py:720
  47.9 0.0 copy-done.3
  47.9 23.0 %near.1.refs_4_.near_ref = f32[128,128]{1,0:T(8,128)S(1)} custom-call(s32[27,256]{1,0:T(8,128)S(1)} %bitcast.25, f32[512,128]{1,0:T(8,128)S(1)} %get-tuple-element.68.own_ref, f32[64,128]{1,0:T(8,128)S(1)} %collective-permute-done.7.partner_ref.refs_5_, f32[64,128]{1,0:T(8,128)S(1)} %collective-permute-done.8.far_ref.refs_6_, ...), custom_call_target="tpu_custom_call" | custom-call | flops 283115520 | bytes 30000000 | tf_op jit(solution)/shard_map/near/pallas_call | solution.py:626
  70.9 0.0 collective-permute-done.17.refs_3_
  70.9 0.0 collective-permute-done.16.refs_2_
  70.9 0.0 collective-permute-done.15.refs_1_
  70.9 0.1 join.5.after_ref.mine_ref
  71.1 2.7 %collective-permute-start.18 = (f32[3584,128]{1,0:T(8,128)S(1)}, f32[3584,128]{1,0:T(8,128)S(1)}, u32[]{:S(2)}, u32[]{:S(2)}) collective-permute-start(f32[3584,128]{1,0:T(8,128)S(1)} %join.5.after_ref.mine_ref), channel_id=1, source_target_pairs={{0,32},{32,0},{1,33},{33,1},{2,34},{34,2},{3,35},{35,3},{4,36},{36... | collective-permute-start | bytes 5505032 | tf_op jit(solution)/shard_map/ppermute | solution.py:752
  73.8 11.6 %leaf_translate.3.local_b_ref = f32[2,88,128]{2,1,0:T(8,128)S(1)} custom-call(s32[16,128]{1,0:T(8,128)S(1)} %get-tuple-element.69.code_ref, f32[27808,128]{1,0:T(8,128)S(1)} %turn_operators.3.refs_4_.ops_ref, f32[320,128]{1,0:T(8,128)S(1)} %get-tuple-element.67.rows_ref, f32[3584,128]{1,0:T(8,128)S(1)} %join.5.after_ref.mine_ref), custom_call_target="tpu_custom_call" | custom-call | flops 214990848 | bytes 20000000 | tf_op jit(solution)/shard_map/leaf_translate/pallas_call | solution.py:673
  85.4 0.0 collective-permute-done.18.other_ref
  85.4 13.8 %finish.1 = (f32[128,128]{1,0:T(8,128)S(1)}, s32[1]{0:T(128)}) custom-call(s32[64,128]{1,0:T(8,128)S(1)} %get-tuple-element.64.code_ref, f32[3584,128]{1,0:T(8,128)S(1)} %join.5.after_ref.mine_ref, f32[3584,128]{1,0:T(8,128)S(1)} %collective-permute-done.18.other_ref, f32[27808,128]{1,0:T(8,128)S(1)} %turn_operators.3.refs_4_.ops_ref, ...), custom_call_target="tpu_custom_call" | custom-call | tf_op jit(solution)/shard_map/finish/pallas_call | solution.py:686
  99.9 0.0 copy-start.9
  99.9 0.6 copy-done.9
  (7 shorter events, 0.1 us)
Async XLA Ops:
  0.0 0.9 copy-start.2
  1.0 0.7 copy-start.4
  5.3 21.4 %collective-permute-start.7 = (f32[64,128]{1,0:T(8,128)S(1)}, f32[64,128]{1,0:T(8,128)S(1)}, u32[]{:S(2)}, u32[]{:S(2)}) collective-permute-start(f32[64,128]{1,0:T(8,128)S(1)} %get-tuple-element.62), channel_id=1, source_target_pairs={{0,1},{1,0},{2,3},{3,2},{4,5},{5,4},{6,7},{7,6},{8,9},{9,8},{10,11... | collective-permute-start | bytes 98312 | tf_op jit(solution)/shard_map/ppermute | solution.py:738
  9.8 17.0 %collective-permute-start.8 = (f32[64,128]{1,0:T(8,128)S(1)}, f32[64,128]{1,0:T(8,128)S(1)}, u32[]{:S(2)}, u32[]{:S(2)}) collective-permute-start(f32[64,128]{1,0:T(8,128)S(1)} %get-tuple-element.63), channel_id=1, source_target_pairs={{0,127},{1,2},{2,1},{3,4},{4,3},{5,6},{6,5},{7,8},{8,7},{9,10},{10... | collective-permute-start | bytes 98312 | tf_op jit(solution)/shard_map/ppermute | solution.py:739
  15.1 11.6 %collective-permute-start.11 = (f32[56,128]{1,0:T(8,128)S(1)}, f32[56,128]{1,0:T(8,128)S(1)}, u32[]{:S(2)}, u32[]{:S(2)}) collective-permute-start(f32[56,128]{1,0:T(8,128)S(1)} %get-tuple-element.65.after_ref.refs_0_), channel_id=1, source_target_pairs={{0,24},{8,16},{16,8},{24,0},{1,25},{9,17},{17,9},{25,1},{2,26},{10... | collective-permute-start | bytes 86024 | tf_op jit(solution)/shard_map/ppermute | solution.py:720
  15.1 11.6 %collective-permute-start.10 = (f32[56,128]{1,0:T(8,128)S(1)}, f32[56,128]{1,0:T(8,128)S(1)}, u32[]{:S(2)}, u32[]{:S(2)}) collective-permute-start(f32[56,128]{1,0:T(8,128)S(1)} %get-tuple-element.65.after_ref.refs_0_), channel_id=1, source_target_pairs={{0,16},{8,24},{16,0},{24,8},{1,17},{9,25},{17,1},{25,9},{2,18},{10... | collective-permute-start | bytes 86024 | tf_op jit(solution)/shard_map/ppermute | solution.py:720
  15.1 11.6 %collective-permute-start.9 = (f32[56,128]{1,0:T(8,128)S(1)}, f32[56,128]{1,0:T(8,128)S(1)}, u32[]{:S(2)}, u32[]{:S(2)}) collective-permute-start(f32[56,128]{1,0:T(8,128)S(1)} %get-tuple-element.65.after_ref.refs_0_), channel_id=1, source_target_pairs={{0,8},{8,0},{16,24},{24,16},{1,9},{9,1},{17,25},{25,17},{2,10},{10... | collective-permute-start | bytes 86024 | tf_op jit(solution)/shard_map/ppermute | solution.py:720
  26.6 3.5 %copy-start = (s32[256,16]{0,1:T(8,128)S(1)}, s32[256,16]{0,1:T(8,128)}, u32[]{:S(2)}) copy-start(s32[256,16]{0,1:T(8,128)} %param.16) | copy-start | bytes 49156
  26.6 3.5 %copy-start.1 = (s32[256,16]{0,1:T(8,128)S(1)}, s32[256,16]{0,1:T(8,128)}, u32[]{:S(2)}) copy-start(s32[256,16]{0,1:T(8,128)} %param.17) | copy-start | bytes 49156
  26.6 3.5 %copy-start.6 = (s32[4096,64]{0,1:T(8,128)S(1)}, s32[4096,64]{0,1:T(8,128)}, u32[]{:S(2)}) copy-start(s32[4096,64]{0,1:T(8,128)} %param.18) | copy-start | bytes 3145732
  26.7 3.4 %copy-start.7 = (s32[4096,64]{0,1:T(8,128)S(1)}, s32[4096,64]{0,1:T(8,128)}, u32[]{:S(2)}) copy-start(s32[4096,64]{0,1:T(8,128)} %param.19) | copy-start | bytes 3145732
  26.7 3.4 %copy-start.8 = (s32[256]{0:T(256)S(1)}, s32[256]{0:T(256)}, u32[]{:S(2)}) copy-start(s32[256]{0:T(256)} %top_ref.3) | copy-start | bytes 3076
  26.8 17.2 %collective-permute-start.14 = (f32[224,128]{1,0:T(8,128)S(1)}, f32[224,128]{1,0:T(8,128)S(1)}, u32[]{:S(2)}, u32[]{:S(2)}) collective-permute-start(f32[224,128]{1,0:T(8,128)S(1)} %join.3.after_ref.refs_0_), channel_id=1, source_target_pairs={{0,6},{2,4},{4,2},{6,0},{1,7},{3,5},{5,3},{7,1},{8,14},{10,12},{12... | collective-permute-start | bytes 344072 | tf_op jit(solution)/shard_map/ppermute | solution.py:720
  26.8 17.1 %collective-permute-start.13 = (f32[224,128]{1,0:T(8,128)S(1)}, f32[224,128]{1,0:T(8,128)S(1)}, u32[]{:S(2)}, u32[]{:S(2)}) collective-permute-start(f32[224,128]{1,0:T(8,128)S(1)} %join.3.after_ref.refs_0_), channel_id=1, source_target_pairs={{0,4},{2,6},{4,0},{6,2},{1,5},{3,7},{5,1},{7,3},{8,12},{10,14},{12... | collective-permute-start | bytes 344072 | tf_op jit(solution)/shard_map/ppermute | solution.py:720
  26.9 17.0 %collective-permute-start.12 = (f32[224,128]{1,0:T(8,128)S(1)}, f32[224,128]{1,0:T(8,128)S(1)}, u32[]{:S(2)}, u32[]{:S(2)}) collective-permute-start(f32[224,128]{1,0:T(8,128)S(1)} %join.3.after_ref.refs_0_), channel_id=1, source_target_pairs={{0,2},{2,0},{4,6},{6,4},{1,3},{3,1},{5,7},{7,5},{8,10},{10,8},{12,... | collective-permute-start | bytes 344072 | tf_op jit(solution)/shard_map/ppermute | solution.py:720
  32.3 15.6 %copy-start.3 = (s32[256,27]{0,1:T(8,128)S(1)}, s32[256,27]{0,1:T(8,128)}, u32[]{:S(2)}) copy-start(s32[256,27]{0,1:T(8,128)} %param.15) | copy-start | bytes 82948
  44.0 26.9 %collective-permute-start.17 = (f32[896,128]{1,0:T(8,128)S(1)}, f32[896,128]{1,0:T(8,128)S(1)}, u32[]{:S(2)}, u32[]{:S(2)}) collective-permute-start(f32[896,128]{1,0:T(8,128)S(1)} %join.4.after_ref.refs_0_), channel_id=1, source_target_pairs={{0,65},{1,64},{64,1},{65,0},{2,67},{3,66},{66,3},{67,2},{4,69},{5,... | collective-permute-start | bytes 1376264 | tf_op jit(solution)/shard_map/ppermute | solution.py:720
  44.1 26.8 %collective-permute-start.16 = (f32[896,128]{1,0:T(8,128)S(1)}, f32[896,128]{1,0:T(8,128)S(1)}, u32[]{:S(2)}, u32[]{:S(2)}) collective-permute-start(f32[896,128]{1,0:T(8,128)S(1)} %join.4.after_ref.refs_0_), channel_id=1, source_target_pairs={{0,64},{1,65},{64,0},{65,1},{2,66},{3,67},{66,2},{67,3},{4,68},{5,... | collective-permute-start | bytes 1376264 | tf_op jit(solution)/shard_map/ppermute | solution.py:720
  45.4 25.6 %collective-permute-start.15 = (f32[896,128]{1,0:T(8,128)S(1)}, f32[896,128]{1,0:T(8,128)S(1)}, u32[]{:S(2)}, u32[]{:S(2)}) collective-permute-start(f32[896,128]{1,0:T(8,128)S(1)} %join.4.after_ref.refs_0_), channel_id=1, source_target_pairs={{0,1},{1,0},{64,65},{65,64},{2,3},{3,2},{66,67},{67,66},{4,5},{5,4... | collective-permute-start | bytes 1376264 | tf_op jit(solution)/shard_map/ppermute | solution.py:720
  71.1 14.3 %collective-permute-start.18 = (f32[3584,128]{1,0:T(8,128)S(1)}, f32[3584,128]{1,0:T(8,128)S(1)}, u32[]{:S(2)}, u32[]{:S(2)}) collective-permute-start(f32[3584,128]{1,0:T(8,128)S(1)} %join.5.after_ref.mine_ref), channel_id=1, source_target_pairs={{0,32},{32,0},{1,33},{33,1},{2,34},{34,2},{3,35},{35,3},{4,36},{36... | collective-permute-start | bytes 5505032 | tf_op jit(solution)/shard_map/ppermute | solution.py:752
  73.8 11.6 %copy-start.5 = (f32[8,81,81]{2,0,1:T(8,128)S(1)}, f32[8,81,81]{2,0,1:T(8,128)}, u32[]{:S(2)}) copy-start(f32[8,81,81]{2,0,1:T(8,128)} %param.21) | copy-start | bytes 629860
  99.9 0.6 copy-start.9

commit v7 on v6

--- a/solution.py
+++ b/solution.py
@@ -27,11 +27,12 @@
 REACH_SQ = 16.0
 FEAT = 32
 FEATS = 24
-LEAF_STEP = 4
+LEAF_STEP = 8
+CHAIN = 8
 TURN_STEP = 27
 TOP_WINDOW = 256
-BUILD_STEP = 16
-NEAR_STEP = 32
+BUILD_STEP = 32
+NEAR_STEP = 64
 
 HIGH = lax.Precision.HIGHEST
 MIB = 1 << 20
@@ -338,11 +339,14 @@
 
 def gather_products(codes, ops_ref, rows_ref):
     total = None
-    for code in codes:
-        at = pl.ds(pl.multiple_of(code >> ROW_BITS, 8), OPROWS)
-        row = rows_ref[pl.ds(code & ((1 << ROW_BITS) - 1), 8, stride=0), :]
-        term = ops_ref[at, :].reshape(OPROWS // 8, 8, 128) * row[None]
-        total = term if total is None else total + term
+    for begin in range(0, len(codes), CHAIN):
+        part = None
+        for code in codes[begin : begin + CHAIN]:
+            at = pl.ds(pl.multiple_of(code >> ROW_BITS, 8), OPROWS)
+            row = rows_ref[pl.ds(code & ((1 << ROW_BITS) - 1), 8, stride=0), :]
+            term = ops_ref[at, :].reshape(OPROWS // 8, 8, 128) * row[None]
+            part = term if part is None else part + term
+        total = part if total is None else total + part
     return total.reshape(OPROWS, 128)
 
 

time: 101 us -> 100 us (0.990)
  Pallas kernels: 74.3 us -> 72.8 us
where the time goes in v7:
time: 100 us; the launch traced here: 99.1 us
  Pallas kernels  72.8 us (73%)
  starting transfers between devices  23 us (23%)
  local copies, waits for them, and re-layouts  2.29 us (2%)
    pallas_call x2, Pallas kernels, call_leaf(): pl.pallas_call(functools.partial(leaf_kernel, part), out_shape=shape(2, O...  23.2 us
    pallas_call x1, Pallas kernels, call_near(): pl.pallas_call(near_kernel, out_shape=shape(targets, 128), in_specs=[VMEM...  22.1 us
    pallas_call x1, Pallas kernels, call_last(): pl.pallas_call(last_kernel, out_shape=(shape(PAIRS, 128), jax.ShapeDtypeS...  13.3 us
    ppermute x9, starting transfers between devices, sent_over(): lax.ppermute(block, axis, [(i, i ^ s) for i in range(4)])  10.5 us
    pallas_call x1, Pallas kernels, call_turn(): pl.pallas_call(turn_kernel, out_shape=shape(CLASSES * OPROWS, 128), in_sp...  8.29 us
    ppermute x1, starting transfers between devices, body(): from_far = lax.ppermute(far_edge, AXES, far)  5.3 us
    ppermute x1, starting transfers between devices, body(): from_partner = lax.ppermute(near_edge, AXES, partner)  4.51 us
    pallas_call x1, Pallas kernels, call_first(): pl.pallas_call(first_kernel, out_shape=(shape(4 * PAIRS, 128), shape(4 *...  3.63 us
  transfers between devices with their start and end apart: 12, of which 0 were waited for; matrix products, arithmetic and copies ran while one was open for 0% of the time, Pallas kernels for 56%

profile of v7, /device:TPU:1, one launch (start us, length us, event | category | flops | bytes accessed | tf_op | source)
XLA Modules:
  0.0 99.1 jit_solution(13168575118776607708)
XLA Ops:
  0.0 0.9 copy-done.2
  1.0 0.7 copy-done.4
  1.6 3.6 %expand_own.1 = (f32[512,128]{1,0:T(8,128)S(1)}, f32[64,128]{1,0:T(8,128)S(1)}, f32[64,128]{1,0:T(8,128)S(1)}, f32[3,128,128]{2,1,0:T(8,128)S(1)}, f32[256,128]{...) custom-call(f32[512,128]{1,0:T(8,128)S(1)} %bitcast.24, ...), custom_call_target="tpu_custom_call" | custom-call | flops 1000000000 | bytes 10000000 | tf_op jit(solution)/shard_map/expand_own/pallas_call | solution.py:585
  5.3 4.5 %collective-permute-start.7 = (f32[64,128]{1,0:T(8,128)S(1)}, f32[64,128]{1,0:T(8,128)S(1)}, u32[]{:S(2)}, u32[]{:S(2)}) collective-permute-start(f32[64,128]{1,0:T(8,128)S(1)} %get-tuple-element.62), channel_id=1, source_target_pairs={{0,1},{1,0},{2,3},{3,2},{4,5},{5,4},{6,7},{7,6},{8,9},{9,8},{10,11... | collective-permute-start | bytes 98312 | tf_op jit(solution)/shard_map/ppermute | solution.py:742
  9.8 5.3 %collective-permute-start.8 = (f32[64,128]{1,0:T(8,128)S(1)}, f32[64,128]{1,0:T(8,128)S(1)}, u32[]{:S(2)}, u32[]{:S(2)}) collective-permute-start(f32[64,128]{1,0:T(8,128)S(1)} %get-tuple-element.63), channel_id=1, source_target_pairs={{0,127},{1,2},{2,1},{3,4},{4,3},{5,6},{6,5},{7,8},{8,7},{9,10},{10... | collective-permute-start | bytes 98312 | tf_op jit(solution)/shard_map/ppermute | solution.py:743
  15.1 0.0 collective-permute-start.11
  15.1 0.0 collective-permute-start.10
  15.1 3.2 %collective-permute-start.9 = (f32[56,128]{1,0:T(8,128)S(1)}, f32[56,128]{1,0:T(8,128)S(1)}, u32[]{:S(2)}, u32[]{:S(2)}) collective-permute-start(f32[56,128]{1,0:T(8,128)S(1)} %get-tuple-element.65.after_ref.refs_0_), channel_id=1, source_target_pairs={{0,8},{8,0},{16,24},{24,16},{1,9},{9,1},{17,25},{25,17},{2,10},{10... | collective-permute-start | bytes 86024 | tf_op jit(solution)/shard_map/ppermute | solution.py:724
  18.3 8.3 %turn_operators.3.refs_4_.ops_ref = f32[27808,128]{1,0:T(8,128)S(1)} custom-call(f32[81,81,316]{2,1,0:T(8,128)} %bitcast.27, f32[56,128]{1,0:T(8,128)S(1)} %get-tuple-element.65.after_ref.refs_0_), custom_call_target="tpu_custom_call" | custom-call | flops 10000000 | bytes 30000000 | tf_op jit(solution)/shard_map/turn_operators/pallas_call | solution.py:604
  26.6 0.0 copy-start
  26.6 0.0 copy-start.1
  26.6 0.0 copy-start.6
  26.7 0.0 copy-start.7
  26.7 0.0 copy-start.8
  26.7 0.0 collective-permute-done.11.refs_3_
  26.7 0.0 collective-permute-done.10.refs_2_
  26.7 0.0 collective-permute-done.9.refs_1_
  26.7 0.0 collective-permute-done.7.partner_ref.refs_5_
  26.7 0.0 collective-permute-done.8.far_ref.refs_6_
  26.8 0.1 collective-permute-start.14
  26.8 0.1 collective-permute-start.13
  26.9 3.1 %collective-permute-start.12 = (f32[224,128]{1,0:T(8,128)S(1)}, f32[224,128]{1,0:T(8,128)S(1)}, u32[]{:S(2)}, u32[]{:S(2)}) collective-permute-start(f32[224,128]{1,0:T(8,128)S(1)} %join.3.after_ref.refs_0_), channel_id=1, source_target_pairs={{0,2},{2,0},{4,6},{6,4},{1,3},{3,1},{5,7},{7,5},{8,10},{10,8},{12,... | collective-permute-start | bytes 344072 | tf_op jit(solution)/shard_map/ppermute | solution.py:724
  30.1 0.0 copy-done
  30.1 0.0 copy-done.1
  30.1 0.0 copy-done.6
  30.1 0.0 copy-done.7
  30.1 0.0 copy-done.8
  30.1 2.2 %expand_halo.1 = (s32[16,128]{1,0:T(8,128)S(1)}, s32[16,128]{1,0:T(8,128)S(1)}, f32[320,128]{1,0:T(8,128)S(1)}, s32[64,128]{1,0:T(8,128)S(1)}) custom-call(s32[256]{0:T(256)S(1)} %copy-done.8, s32[64,4096]{1,0:T(8,128)S(1)} %bitcast.32, s32[64,4096]{1,0:T(8,128)S(1)} %bitcast.33, s32[16,256]{1,0:T(8,128)S(1)} %bitcast.22, s32[16,256]{1,0:T(8,128)S(1)} %bitcast.23, ...), custom_call_target="tpu_custom_call" | custom-call | flops 100000000 | bytes 1000000 | tf_op jit(solution)/shard_map/expand_halo/pallas_call | solution.py:652
  32.3 0.0 copy-start.3
  32.3 11.6 %leaf_translate.2.refs_4_.local_a_ref = f32[2,88,128]{2,1,0:T(8,128)S(1)} custom-call(s32[16,128]{1,0:T(8,128)S(1)} %get-tuple-element.66.code_ref, f32[27808,128]{1,0:T(8,128)S(1)} %turn_operators.3.refs_4_.ops_ref, f32[320,128]{1,0:T(8,128)S(1)} %get-tuple-element.67.rows_ref, f32[224,128]{1,0:T(8,128)S(1)} %join.3.after_ref.refs_0_), custom_call_target="tpu_custom_call" | custom-call | flops 214990848 | bytes 20000000 | tf_op jit(solution)/shard_map/leaf_translate/pallas_call | solution.py:677
  43.9 0.0 collective-permute-done.14.refs_3_
  44.0 0.0 collective-permute-done.13.refs_2_
  44.0 0.0 collective-permute-done.12.refs_1_
  44.0 0.1 collective-permute-start.17
  44.1 1.2 %collective-permute-start.16 = (f32[896,128]{1,0:T(8,128)S(1)}, f32[896,128]{1,0:T(8,128)S(1)}, u32[]{:S(2)}, u32[]{:S(2)}) collective-permute-start(f32[896,128]{1,0:T(8,128)S(1)} %join.4.after_ref.refs_0_), channel_id=1, source_target_pairs={{0,64},{1,65},{64,0},{65,1},{2,66},{3,67},{66,2},{67,3},{4,68},{5,... | collective-permute-start | bytes 1376264 | tf_op jit(solution)/shard_map/ppermute | solution.py:724
  45.3 2.7 %collective-permute-start.15 = (f32[896,128]{1,0:T(8,128)S(1)}, f32[896,128]{1,0:T(8,128)S(1)}, u32[]{:S(2)}, u32[]{:S(2)}) collective-permute-start(f32[896,128]{1,0:T(8,128)S(1)} %join.4.after_ref.refs_0_), channel_id=1, source_target_pairs={{0,1},{1,0},{64,65},{65,64},{2,3},{3,2},{66,67},{67,66},{4,5},{5,4... | collective-permute-start | bytes 1376264 | tf_op jit(solution)/shard_map/ppermute | solution.py:724
  48.0 0.0 copy-done.3
  48.0 22.1 %near.1.refs_4_.near_ref = f32[128,128]{1,0:T(8,128)S(1)} custom-call(s32[27,256]{1,0:T(8,128)S(1)} %bitcast.25, f32[512,128]{1,0:T(8,128)S(1)} %get-tuple-element.68.own_ref, f32[64,128]{1,0:T(8,128)S(1)} %collective-permute-done.7.partner_ref.refs_5_, f32[64,128]{1,0:T(8,128)S(1)} %collective-permute-done.8.far_ref.refs_6_, ...), custom_call_target="tpu_custom_call" | custom-call | flops 283115520 | bytes 30000000 | tf_op jit(solution)/shard_map/near/pallas_call | solution.py:630
  70.1 0.0 collective-permute-done.17.refs_3_
  70.1 0.0 collective-permute-done.16.refs_2_
  70.1 0.0 collective-permute-done.15.refs_1_
  70.1 0.1 join.5.after_ref.mine_ref
  70.3 2.7 %collective-permute-start.18 = (f32[3584,128]{1,0:T(8,128)S(1)}, f32[3584,128]{1,0:T(8,128)S(1)}, u32[]{:S(2)}, u32[]{:S(2)}) collective-permute-start(f32[3584,128]{1,0:T(8,128)S(1)} %join.5.after_ref.mine_ref), channel_id=1, source_target_pairs={{0,32},{32,0},{1,33},{33,1},{2,34},{34,2},{3,35},{35,3},{4,36},{36... | collective-permute-start | bytes 5505032 | tf_op jit(solution)/shard_map/ppermute | solution.py:756
  72.9 11.6 %leaf_translate.3.local_b_ref = f32[2,88,128]{2,1,0:T(8,128)S(1)} custom-call(s32[16,128]{1,0:T(8,128)S(1)} %get-tuple-element.69.code_ref, f32[27808,128]{1,0:T(8,128)S(1)} %turn_operators.3.refs_4_.ops_ref, f32[320,128]{1,0:T(8,128)S(1)} %get-tuple-element.67.rows_ref, f32[3584,128]{1,0:T(8,128)S(1)} %join.5.after_ref.mine_ref), custom_call_target="tpu_custom_call" | custom-call | flops 214990848 | bytes 20000000 | tf_op jit(solution)/shard_map/leaf_translate/pallas_call | solution.py:677
  84.5 0.0 collective-permute-done.18.other_ref
  84.5 13.3 %finish.1 = (f32[128,128]{1,0:T(8,128)S(1)}, s32[1]{0:T(128)}) custom-call(s32[64,128]{1,0:T(8,128)S(1)} %get-tuple-element.64.code_ref, f32[3584,128]{1,0:T(8,128)S(1)} %join.5.after_ref.mine_ref, f32[3584,128]{1,0:T(8,128)S(1)} %collective-permute-done.18.other_ref, f32[27808,128]{1,0:T(8,128)S(1)} %turn_operators.3.refs_4_.ops_ref, ...), custom_call_target="tpu_custom_call" | custom-call | tf_op jit(solution)/shard_map/finish/pallas_call | solution.py:690
  98.5 0.0 copy-start.9
  98.5 0.6 copy-done.9
  (7 shorter events, 0.1 us)
Async XLA Ops:
  0.0 0.9 copy-start.2
  1.0 0.7 copy-start.4
  5.3 21.4 %collective-permute-start.7 = (f32[64,128]{1,0:T(8,128)S(1)}, f32[64,128]{1,0:T(8,128)S(1)}, u32[]{:S(2)}, u32[]{:S(2)}) collective-permute-start(f32[64,128]{1,0:T(8,128)S(1)} %get-tuple-element.62), channel_id=1, source_target_pairs={{0,1},{1,0},{2,3},{3,2},{4,5},{5,4},{6,7},{7,6},{8,9},{9,8},{10,11... | collective-permute-start | bytes 98312 | tf_op jit(solution)/shard_map/ppermute | solution.py:742
  9.8 17.0 %collective-permute-start.8 = (f32[64,128]{1,0:T(8,128)S(1)}, f32[64,128]{1,0:T(8,128)S(1)}, u32[]{:S(2)}, u32[]{:S(2)}) collective-permute-start(f32[64,128]{1,0:T(8,128)S(1)} %get-tuple-element.63), channel_id=1, source_target_pairs={{0,127},{1,2},{2,1},{3,4},{4,3},{5,6},{6,5},{7,8},{8,7},{9,10},{10... | collective-permute-start | bytes 98312 | tf_op jit(solution)/shard_map/ppermute | solution.py:743
  15.1 11.6 %collective-permute-start.11 = (f32[56,128]{1,0:T(8,128)S(1)}, f32[56,128]{1,0:T(8,128)S(1)}, u32[]{:S(2)}, u32[]{:S(2)}) collective-permute-start(f32[56,128]{1,0:T(8,128)S(1)} %get-tuple-element.65.after_ref.refs_0_), channel_id=1, source_target_pairs={{0,24},{8,16},{16,8},{24,0},{1,25},{9,17},{17,9},{25,1},{2,26},{10... | collective-permute-start | bytes 86024 | tf_op jit(solution)/shard_map/ppermute | solution.py:724
  15.1 11.6 %collective-permute-start.10 = (f32[56,128]{1,0:T(8,128)S(1)}, f32[56,128]{1,0:T(8,128)S(1)}, u32[]{:S(2)}, u32[]{:S(2)}) collective-permute-start(f32[56,128]{1,0:T(8,128)S(1)} %get-tuple-element.65.after_ref.refs_0_), channel_id=1, source_target_pairs={{0,16},{8,24},{16,0},{24,8},{1,17},{9,25},{17,1},{25,9},{2,18},{10... | collective-permute-start | bytes 86024 | tf_op jit(solution)/shard_map/ppermute | solution.py:724
  15.1 11.6 %collective-permute-start.9 = (f32[56,128]{1,0:T(8,128)S(1)}, f32[56,128]{1,0:T(8,128)S(1)}, u32[]{:S(2)}, u32[]{:S(2)}) collective-permute-start(f32[56,128]{1,0:T(8,128)S(1)} %get-tuple-element.65.after_ref.refs_0_), channel_id=1, source_target_pairs={{0,8},{8,0},{16,24},{24,16},{1,9},{9,1},{17,25},{25,17},{2,10},{10... | collective-permute-start | bytes 86024 | tf_op jit(solution)/shard_map/ppermute | solution.py:724
  26.6 3.5 %copy-start = (s32[256,16]{0,1:T(8,128)S(1)}, s32[256,16]{0,1:T(8,128)}, u32[]{:S(2)}) copy-start(s32[256,16]{0,1:T(8,128)} %param.16) | copy-start | bytes 49156
  26.6 3.5 %copy-start.1 = (s32[256,16]{0,1:T(8,128)S(1)}, s32[256,16]{0,1:T(8,128)}, u32[]{:S(2)}) copy-start(s32[256,16]{0,1:T(8,128)} %param.17) | copy-start | bytes 49156
  26.6 3.5 %copy-start.6 = (s32[4096,64]{0,1:T(8,128)S(1)}, s32[4096,64]{0,1:T(8,128)}, u32[]{:S(2)}) copy-start(s32[4096,64]{0,1:T(8,128)} %param.18) | copy-start | bytes 3145732
  26.7 3.4 %copy-start.7 = (s32[4096,64]{0,1:T(8,128)S(1)}, s32[4096,64]{0,1:T(8,128)}, u32[]{:S(2)}) copy-start(s32[4096,64]{0,1:T(8,128)} %param.19) | copy-start | bytes 3145732
  26.7 3.4 %copy-start.8 = (s32[256]{0:T(256)S(1)}, s32[256]{0:T(256)}, u32[]{:S(2)}) copy-start(s32[256]{0:T(256)} %top_ref.3) | copy-start | bytes 3076
  26.8 17.2 %collective-permute-start.14 = (f32[224,128]{1,0:T(8,128)S(1)}, f32[224,128]{1,0:T(8,128)S(1)}, u32[]{:S(2)}, u32[]{:S(2)}) collective-permute-start(f32[224,128]{1,0:T(8,128)S(1)} %join.3.after_ref.refs_0_), channel_id=1, source_target_pairs={{0,6},{2,4},{4,2},{6,0},{1,7},{3,5},{5,3},{7,1},{8,14},{10,12},{12... | collective-permute-start | bytes 344072 | tf_op jit(solution)/shard_map/ppermute | solution.py:724
  26.8 17.1 %collective-permute-start.13 = (f32[224,128]{1,0:T(8,128)S(1)}, f32[224,128]{1,0:T(8,128)S(1)}, u32[]{:S(2)}, u32[]{:S(2)}) collective-permute-start(f32[224,128]{1,0:T(8,128)S(1)} %join.3.after_ref.refs_0_), channel_id=1, source_target_pairs={{0,4},{2,6},{4,0},{6,2},{1,5},{3,7},{5,1},{7,3},{8,12},{10,14},{12... | collective-permute-start | bytes 344072 | tf_op jit(solution)/shard_map/ppermute | solution.py:724
  26.9 17.0 %collective-permute-start.12 = (f32[224,128]{1,0:T(8,128)S(1)}, f32[224,128]{1,0:T(8,128)S(1)}, u32[]{:S(2)}, u32[]{:S(2)}) collective-permute-start(f32[224,128]{1,0:T(8,128)S(1)} %join.3.after_ref.refs_0_), channel_id=1, source_target_pairs={{0,2},{2,0},{4,6},{6,4},{1,3},{3,1},{5,7},{7,5},{8,10},{10,8},{12,... | collective-permute-start | bytes 344072 | tf_op jit(solution)/shard_map/ppermute | solution.py:724
  32.3 15.6 %copy-start.3 = (s32[256,27]{0,1:T(8,128)S(1)}, s32[256,27]{0,1:T(8,128)}, u32[]{:S(2)}) copy-start(s32[256,27]{0,1:T(8,128)} %param.15) | copy-start | bytes 82948
  44.0 26.1 %collective-permute-start.17 = (f32[896,128]{1,0:T(8,128)S(1)}, f32[896,128]{1,0:T(8,128)S(1)}, u32[]{:S(2)}, u32[]{:S(2)}) collective-permute-start(f32[896,128]{1,0:T(8,128)S(1)} %join.4.after_ref.refs_0_), channel_id=1, source_target_pairs={{0,65},{1,64},{64,1},{65,0},{2,67},{3,66},{66,3},{67,2},{4,69},{5,... | collective-permute-start | bytes 1376264 | tf_op jit(solution)/shard_map/ppermute | solution.py:724
  44.1 26.0 %collective-permute-start.16 = (f32[896,128]{1,0:T(8,128)S(1)}, f32[896,128]{1,0:T(8,128)S(1)}, u32[]{:S(2)}, u32[]{:S(2)}) collective-permute-start(f32[896,128]{1,0:T(8,128)S(1)} %join.4.after_ref.refs_0_), channel_id=1, source_target_pairs={{0,64},{1,65},{64,0},{65,1},{2,66},{3,67},{66,2},{67,3},{4,68},{5,... | collective-permute-start | bytes 1376264 | tf_op jit(solution)/shard_map/ppermute | solution.py:724
  45.3 24.8 %collective-permute-start.15 = (f32[896,128]{1,0:T(8,128)S(1)}, f32[896,128]{1,0:T(8,128)S(1)}, u32[]{:S(2)}, u32[]{:S(2)}) collective-permute-start(f32[896,128]{1,0:T(8,128)S(1)} %join.4.after_ref.refs_0_), channel_id=1, source_target_pairs={{0,1},{1,0},{64,65},{65,64},{2,3},{3,2},{66,67},{67,66},{4,5},{5,4... | collective-permute-start | bytes 1376264 | tf_op jit(solution)/shard_map/ppermute | solution.py:724
  70.3 14.2 %collective-permute-start.18 = (f32[3584,128]{1,0:T(8,128)S(1)}, f32[3584,128]{1,0:T(8,128)S(1)}, u32[]{:S(2)}, u32[]{:S(2)}) collective-permute-start(f32[3584,128]{1,0:T(8,128)S(1)} %join.5.after_ref.mine_ref), channel_id=1, source_target_pairs={{0,32},{32,0},{1,33},{33,1},{2,34},{34,2},{3,35},{35,3},{4,36},{36... | collective-permute-start | bytes 5505032 | tf_op jit(solution)/shard_map/ppermute | solution.py:756
  72.9 11.6 %copy-start.5 = (f32[8,81,81]{2,0,1:T(8,128)S(1)}, f32[8,81,81]{2,0,1:T(8,128)}, u32[]{:S(2)}) copy-start(f32[8,81,81]{2,0,1:T(8,128)} %param.21) | copy-start | bytes 629860
  98.5 0.6 copy-start.9
